TPU v7x, 32 devices: a whole 2x2x4 slice. The times are simulated.
32 devices in a mesh: dp: 8 (over z, x), mp: 4 (over y, core).
Axes of the slice: x: 2, y: 2, z: 4, core: 2. Of those that a mesh axis runs over, the one named last changes fastest.
Arguments:
- tokens: bfloat16 [49152, 1280], P(('dp', 'mp')), may hold values from -40 to 40, as said below
- lengths: int32 [768, 32], P('dp'), may hold values from 0 to 64, as said below
- cotangent: bfloat16 [49152, 1280], P(('dp', 'mp')), may hold values from -6 to 6
- query_weight: bfloat16 [1280, 1280], P(None, 'mp'), may hold values from -0.15625 to 0.15625
- key_weight: bfloat16 [1280, 1280], P(None, 'mp'), may hold values from -0.15625 to 0.15625
- value_weight: bfloat16 [1280, 1280], P(None, 'mp'), may hold values from -0.15625 to 0.15625
- out_weight: bfloat16 [1280, 1280], P('mp'), may hold values from -0.3125 to 0.3125
- up_weight: bfloat16 [1280, 5120], P(None, 'mp'), may hold values from -0.15625 to 0.15625
- hidden_bias: bfloat16 [5120], P('mp'), may hold values from -3 to 3
- down_weight: bfloat16 [5120, 1280], P('mp'), may hold values from -0.078125 to 0.078125
- output_bias: bfloat16 [1280], replicated, may hold values from -2 to 2
- first_gain: bfloat16 [1280], replicated, may hold values from 0.099609375 to 1.8984375
- second_gain: bfloat16 [1280], replicated, may hold values from 0.099609375 to 1.8984375
Outputs:
- layer_output: bfloat16 [49152, 1280], P(('dp', 'mp'))
- input_gradient: float32 [49152, 1280], P(('dp', 'mp'))
- query_gradient: float32 [1280, 1280], P(None, 'mp')
- key_gradient: float32 [1280, 1280], P(None, 'mp')
- value_gradient: float32 [1280, 1280], P(None, 'mp')
- out_gradient: float32 [1280, 1280], P('mp')
- up_gradient: float32 [1280, 5120], P(None, 'mp')
- hidden_bias_gradient: float32 [5120], P('mp')
- down_gradient: float32 [5120, 1280], P('mp')
- output_bias_gradient: float32 [1280], replicated
- first_gain_gradient: float32 [1280], replicated
- second_gain_gradient: float32 [1280], replicated
- rms_stats: float32 [3], replicated
Inputs may be any that keep to these rules, and one draw needn't show every extreme that they name: Each row lists the lengths of the series packed into it in order, zeros only after the last; every row holds one series or more and at most 64 patches; some row holds a single series of 64. `tokens`: activations of order one.
All inputs are finite; a program needn't handle non-finite values.
Results may differ from a plain program's by a relative error of at most 0.018.
Values may be sent and summed in bfloat16 or wider, within the bound.
A program may use at most 384 MiB of HBM per device.

v0:
```python
import math

import jax
import jax.numpy as jnp
from jax import lax
from jax.sharding import PartitionSpec as P

D = 1280
HD = 80
L = 64
SLOTS = 32


EPSILON = 1e-06
MASKED_SCORE = -1e30


def segments(lengths):
    ends = jnp.cumsum(lengths, axis=1)
    places = lax.broadcasted_iota(jnp.int32, (lengths.shape[0], L, lengths.shape[1]), 1)
    return jnp.sum((ends[:, None, :] <= places).astype(jnp.int32), axis=2)


def normalize(values, gain):
    scale_rows = lax.rsqrt(jnp.mean(values * values, axis=1, keepdims=True) + EPSILON)
    normed = (values * scale_rows * gain.astype(jnp.float32)).astype(jnp.bfloat16)
    return (scale_rows, normed)


def norm_back(values, scale_rows, gain, grad):
    weighted = gain.astype(jnp.float32) * grad
    inner = jnp.sum(weighted * values, axis=1, keepdims=True)
    gain_part = jnp.sum(grad * values * scale_rows, axis=0)
    back = (
        weighted * scale_rows
        - values * scale_rows * scale_rows * scale_rows * inner / values.shape[1]
    )
    return (gain_part, back)


def per_device(
    tokens,
    lengths,
    cotangent,
    query_weight,
    key_weight,
    value_weight,
    out_weight,
    up_weight,
    hidden_bias,
    down_weight,
    output_bias,
    first_gain,
    second_gain,
):
    local_rows = tokens.shape[0]
    width = query_weight.shape[1]
    heads_here = width // HD
    rows_here = lengths.shape[0]
    scale = 1.0 / math.sqrt(HD)
    segment_ids = segments(lengths)
    valid_all = (segment_ids < SLOTS).reshape(-1).astype(jnp.float32)
    valid = lax.dynamic_slice_in_dim(valid_all, lax.axis_index("mp") * local_rows, local_rows)
    causal = lax.broadcasted_iota(jnp.int32, (L, L), 1) <= lax.broadcasted_iota(
        jnp.int32, (L, L), 0
    )
    allowed = ((segment_ids[:, :, None] == segment_ids[:, None, :]) & causal[None])[:, None]
    inputs = tokens.astype(jnp.float32)
    first_scale, first_normed = normalize(inputs, first_gain)
    first_rows = lax.all_gather(first_normed, "mp", axis=0, tiled=True)
    joined_weight = jnp.concatenate([query_weight, key_weight, value_weight], axis=1)
    joined = jnp.dot(first_rows, joined_weight, preferred_element_type=jnp.float32).astype(
        jnp.bfloat16
    )
    queries = joined[:, :width].reshape(rows_here, L, heads_here, HD)
    keys = joined[:, width : 2 * width].reshape(rows_here, L, heads_here, HD)
    values = joined[:, 2 * width :].reshape(rows_here, L, heads_here, HD)

    def masked_scores():
        scores = (
            jnp.einsum("rqhe,rkhe->rhqk", queries, keys, preferred_element_type=jnp.float32) * scale
        )
        return jnp.where(allowed, scores, MASKED_SCORE)

    scores = masked_scores()
    peak = jnp.max(scores, axis=-1, keepdims=True)
    logsum = peak + jnp.log(jnp.sum(jnp.exp(scores - peak), axis=-1, keepdims=True))
    probs_low = jnp.exp(scores - logsum).astype(jnp.bfloat16)
    mixed = jnp.einsum("rhqk,rkhe->rqhe", probs_low, values, preferred_element_type=jnp.float32)
    mixed = mixed.astype(jnp.bfloat16).reshape(rows_here * L, width)
    attention_local = lax.psum_scatter(
        jnp.dot(mixed, out_weight, preferred_element_type=jnp.float32).astype(jnp.bfloat16),
        "mp",
        scatter_dimension=0,
        tiled=True,
    ).astype(jnp.float32)
    hidden = inputs + attention_local
    second_scale, second_normed = normalize(hidden, second_gain)
    second_rows = lax.all_gather(second_normed, "mp", axis=0, tiled=True)
    preact = jnp.dot(
        second_rows, up_weight, preferred_element_type=jnp.float32
    ) + hidden_bias.astype(jnp.float32)
    sigma = jax.nn.sigmoid(preact)
    active = (preact * sigma).astype(jnp.bfloat16)
    feed_local = lax.psum_scatter(
        jnp.dot(active, down_weight, preferred_element_type=jnp.float32).astype(jnp.bfloat16),
        "mp",
        scatter_dimension=0,
        tiled=True,
    ).astype(jnp.float32) + output_bias.astype(jnp.float32)
    result = hidden + feed_local
    mask_col = valid[:, None]
    squares = jnp.stack(
        [
            jnp.sum(mask_col * attention_local * attention_local),
            jnp.sum(mask_col * feed_local * feed_local),
            jnp.sum(mask_col * result * result),
        ]
    )
    count = jnp.sum(valid)
    grad_out = cotangent.astype(jnp.float32)
    output_bias_part = jnp.sum(grad_out, axis=0)
    grad_rows = lax.all_gather(cotangent, "mp", axis=0, tiled=True)
    down_part = jnp.einsum("tf,td->fd", active, grad_rows, preferred_element_type=jnp.float32)
    active_grad = jnp.einsum(
        "td,fd->tf", grad_rows, down_weight, preferred_element_type=jnp.float32
    )
    active_grad = active_grad.astype(jnp.bfloat16).astype(jnp.float32)
    preact_grad = (active_grad * (sigma + preact * sigma * (1.0 - sigma))).astype(jnp.bfloat16)
    bias_part = jnp.sum(preact_grad.astype(jnp.float32), axis=0)
    up_part = jnp.einsum("td,tf->df", second_rows, preact_grad, preferred_element_type=jnp.float32)
    second_grad = lax.psum_scatter(
        jnp.einsum("tf,df->td", preact_grad, up_weight, preferred_element_type=jnp.float32).astype(
            jnp.bfloat16
        ),
        "mp",
        scatter_dimension=0,
        tiled=True,
    ).astype(jnp.float32)
    second_gain_part, second_back = norm_back(hidden, second_scale, second_gain, second_grad)
    hidden_grad = grad_out + second_back
    branch_low = hidden_grad.astype(jnp.bfloat16)
    branch_grad = lax.all_gather(branch_low, "mp", axis=0, tiled=True)
    out_part = jnp.einsum("tk,td->kd", mixed, branch_grad, preferred_element_type=jnp.float32)
    mixed_grad = jnp.einsum(
        "td,kd->tk", branch_grad, out_weight, preferred_element_type=jnp.float32
    )
    mixed_grad = mixed_grad.astype(jnp.bfloat16).reshape(rows_here, L, heads_here, HD)
    probs = jnp.exp(masked_scores() - logsum)
    probs_grad = jnp.einsum(
        "rqhe,rkhe->rhqk", mixed_grad, values, preferred_element_type=jnp.float32
    )
    value_grad = jnp.einsum(
        "rhqk,rqhe->rkhe",
        probs.astype(jnp.bfloat16),
        mixed_grad,
        preferred_element_type=jnp.float32,
    ).astype(jnp.bfloat16)
    inner = jnp.sum(probs * probs_grad, axis=-1, keepdims=True)
    scores_grad = (probs * (probs_grad - inner)).astype(jnp.bfloat16)
    query_grad = (
        jnp.einsum("rhqk,rkhe->rqhe", scores_grad, keys, preferred_element_type=jnp.float32) * scale
    ).astype(jnp.bfloat16)
    key_grad = (
        jnp.einsum("rhqk,rqhe->rkhe", scores_grad, queries, preferred_element_type=jnp.float32)
        * scale
    ).astype(jnp.bfloat16)
    joined_grad = jnp.concatenate(
        [
            query_grad.reshape(rows_here * L, width),
            key_grad.reshape(rows_here * L, width),
            value_grad.reshape(rows_here * L, width),
        ],
        axis=1,
    )
    joined_part = jnp.einsum(
        "td,tk->dk", first_rows, joined_grad, preferred_element_type=jnp.float32
    )
    query_part = joined_part[:, :width]
    key_part = joined_part[:, width : 2 * width]
    value_part = joined_part[:, 2 * width :]
    first_grad = lax.psum_scatter(
        jnp.einsum(
            "tk,dk->td", joined_grad, joined_weight, preferred_element_type=jnp.float32
        ).astype(jnp.bfloat16),
        "mp",
        scatter_dimension=0,
        tiled=True,
    ).astype(jnp.float32)
    first_gain_part, first_back = norm_back(inputs, first_scale, first_gain, first_grad)
    input_gradient = hidden_grad + first_back
    query_total, key_total, value_total, out_total, up_total, bias_total, down_total = (
        lax.psum(query_part.astype(jnp.bfloat16), "dp").astype(jnp.float32),
        lax.psum(key_part.astype(jnp.bfloat16), "dp").astype(jnp.float32),
        lax.psum(value_part.astype(jnp.bfloat16), "dp").astype(jnp.float32),
        lax.psum(out_part.astype(jnp.bfloat16), "dp").astype(jnp.float32),
        lax.psum(up_part.astype(jnp.bfloat16), "dp").astype(jnp.float32),
        lax.psum(bias_part.astype(jnp.bfloat16), "dp").astype(jnp.float32),
        lax.psum(down_part.astype(jnp.bfloat16), "dp").astype(jnp.float32),
    )
    first_total, second_total, output_bias_total, squares_total, count_total = lax.psum(
        (first_gain_part, second_gain_part, output_bias_part, squares, count), ("dp", "mp")
    )
    rms_stats = jnp.sqrt(squares_total / (count_total * D))
    return (
        result.astype(jnp.bfloat16),
        input_gradient,
        query_total,
        key_total,
        value_total,
        out_total,
        up_total,
        bias_total,
        down_total,
        output_bias_total,
        first_total,
        second_total,
        rms_stats,
    )


def solution(mesh):
    return jax.shard_map(
        per_device,
        mesh=mesh,
        in_specs=(
            P(("dp", "mp"), None),
            P("dp", None),
            P(("dp", "mp"), None),
            P(None, "mp"),
            P(None, "mp"),
            P(None, "mp"),
            P("mp", None),
            P(None, "mp"),
            P("mp"),
            P("mp", None),
            P(),
            P(),
            P(),
        ),
        out_specs=(
            P(("dp", "mp"), None),
            P(("dp", "mp"), None),
            P(None, "mp"),
            P(None, "mp"),
            P(None, "mp"),
            P("mp", None),
            P(None, "mp"),
            P("mp"),
            P("mp", None),
            P(),
            P(),
            P(),
            P(),
        ),
        check_vma=False,
    )
```

profile of v0, /device:TPU:0, one launch (start us, length us, event | category | flops | bytes accessed | tf_op | source)
XLA Modules:
  0.0 1699.4 jit_solution(6496326896694240132)
XLA Ops:
  26.2 93.4 %all-gather.5.cloned.1.call-done = bf16[6144,1280]{1,0:T(8,128)(2,1)} async-done(((bf16[1536,1280]{1,0:T(8,128)(2,1)}), bf16[6144,1280]{1,0:T(8,128)(2,1)}) %all-gather.5.cloned.1.call-update) | async-done | bytes 15728656 | tf_op jit(solution)/shard_map/all_gather | solution.py:70
  119.6 19.1 %convolution_convert_fusion.5 = bf16[6144,960]{0,1:T(8,128)(2,1)S(1)} fusion(bf16[6144,1280]{1,0:T(8,128)(2,1)} %all-gather.5.cloned.1.call-done, bf16[1280,960]{0,1:T(8,128)(2,1)} %constant_dynamic-update-slice_fusion), kind=kOutput, calls=%fused_computation.25 | convolution fusion | flops 15105392640 | bytes 29982720 | tf_op jit(solution)/shard_map/dot_general | solution.py:72
  143.3 11.6 reshape.114
  154.9 11.6 copy.64
  166.6 11.6 reshape.113
  178.2 11.6 copy.63
  189.8 11.6 reshape.112
  201.5 11.6 copy.65
  213.1 12.7 fusion.1
  225.8 8.1 exponential_reduce_fusion
  235.0 8.6 convert_bitcast_fusion.1
  243.6 18.5 %copy.67 = bf16[96,64,4,80]{3,2,1,0:T(4,128)(2,1)} copy(bf16[96,64,4,80]{3,1,2,0:T(8,128)(2,1)} %convert_bitcast_fusion.1) | data formatting | bytes 7864320 | tf_op jit(solution)/shard_map/convert_element_type | solution.py:90
  262.1 10.8 reshape.106
  272.9 13.5 convolution_convert_fusion.3
  287.1 119.3 %reduce-scatter.5.cloned.1.call-done = bf16[1536,1280]{1,0:T(8,128)(2,1)} async-done(((bf16[6144,1280]{1,0:T(8,128)(2,1)}), bf16[1536,1280]{1,0:T(8,128)(2,1)}) %reduce-scatter.5.cloned.1.call-update) | async-done | bytes 3932176 | tf_op jit(solution)/shard_map/reduce_scatter | solution.py:91
  415.8 99.5 %all-gather.7.cloned.1.call-done = bf16[6144,1280]{1,0:T(8,128)(2,1)} async-done(((bf16[1536,1280]{1,0:T(8,128)(2,1)}), bf16[6144,1280]{1,0:T(8,128)(2,1)}) %all-gather.7.cloned.1.call-update) | async-done | bytes 15728656 | tf_op jit(solution)/shard_map/all_gather | solution.py:99
  515.3 32.7 %fusion = (bf16[6144,1280]{1,0:T(8,128)(2,1)}, f32[6144,1280]{1,0:T(8,128)}) fusion(f32[1280]{0:T(1024)S(1)} %convert_element_type.161, bf16[6144,1280]{1,0:T(8,128)(2,1)} %all-gather.7.cloned.1.call-done, bf16[1280,1280]{1,0:T(8,128)(2,1)S(1)} %copy-done), kind=kOutput, calls=%fused_computation.3 | convolution fusion | flops 20179845120 | bytes 66196480 | tf_op jit(solution)/shard_map/dot_general | solution.py:100
  548.0 25.9 %convolution_convert_fusion.2 = bf16[6144,1280]{1,0:T(8,128)(2,1)} fusion(bf16[6144,1280]{1,0:T(8,128)(2,1)} %get-tuple-element.44, bf16[1280,1280]{1,0:T(8,128)(2,1)S(1)} %copy-done.38), kind=kOutput, calls=%fused_computation.6 | convolution fusion | flops 20140523520 | bytes 34734080 | tf_op jit(solution)/shard_map/dot_general | solution.py:106
  574.0 42.7 %all-gather.9.cloned.1.call-done = bf16[6144,1280]{1,0:T(8,128)(2,1)} async-done(((bf16[1536,1280]{1,0:T(8,128)(2,1)}), bf16[6144,1280]{1,0:T(8,128)(2,1)}) %all-gather.9.cloned.1.call-update) | async-done | bytes 15728656 | tf_op jit(solution)/shard_map/all_gather | solution.py:123
  616.7 38.4 %fusion.39 = (bf16[1280]{0:T(1024)(128)(2,1)}, bf16[6144,1280]{1,0:T(8,128)(2,1)}) fusion(f32[6144,1280]{1,0:T(8,128)} %get-tuple-element.45, f32[1280]{0:T(1024)S(1)} %convert_element_type.161, bf16[6144,1280]{1,0:T(8,128)(2,1)} %all-gather.9.cloned.1.call-done, bf16[1280,1280]{1,0:T(8,128)(2,1)} %param.22), kind=kOutput, calls=%fused_computation.89 | convolution fusion | flops 20234893312 | bytes 66199040 | tf_op jit(solution)/shard_map/td,fd->tf/dot_general | solution.py:125
  655.1 25.9 %convolution_convert_fusion = bf16[6144,1280]{1,0:T(8,128)(2,1)} fusion(bf16[6144,1280]{1,0:T(8,128)(2,1)} %get-tuple-element.49, bf16[1280,1280]{1,0:T(8,128)(2,1)S(1)} %copy-done), kind=kOutput, calls=%fused_computation.4 | convolution fusion | flops 20140523520 | bytes 34734080 | tf_op jit(solution)/shard_map/tf,df->td/dot_general | solution.py:133
  682.7 56.3 %reduce-scatter.7.cloned.1.call-done = bf16[1536,1280]{1,0:T(8,128)(2,1)} async-done(((bf16[6144,1280]{1,0:T(8,128)(2,1)}), bf16[1536,1280]{1,0:T(8,128)(2,1)}) %reduce-scatter.7.cloned.1.call-update) | async-done | bytes 3932176 | tf_op jit(solution)/shard_map/reduce_scatter | solution.py:105
  739.0 122.3 %reduce-scatter.9.cloned.1.call-done = bf16[1536,1280]{1,0:T(8,128)(2,1)} async-done(((bf16[6144,1280]{1,0:T(8,128)(2,1)}), bf16[1536,1280]{1,0:T(8,128)(2,1)}) %reduce-scatter.9.cloned.1.call-update) | async-done | bytes 3932176 | tf_op jit(solution)/shard_map/reduce_scatter | solution.py:132
  861.4 13.8 fusion.16
  880.7 26.7 %convolution_convert_fusion.7 = bf16[1280,1280]{1,0:T(8,128)(2,1)} fusion(bf16[6144,1280]{1,0:T(8,128)(2,1)} %get-tuple-element.44, bf16[6144,1280]{1,0:T(8,128)(2,1)} %all-gather.9.cloned.1.call-done), kind=kOutput, calls=%fused_computation.59 | convolution fusion | flops 20134297600 | bytes 34734080 | tf_op jit(solution)/shard_map/tf,td->fd/dot_general | solution.py:124
  907.4 26.8 %convolution_convert_fusion.8 = bf16[1280,1280]{1,0:T(8,128)(2,1)} fusion(bf16[6144,1280]{1,0:T(8,128)(2,1)} %all-gather.7.cloned.1.call-done, bf16[6144,1280]{1,0:T(8,128)(2,1)} %get-tuple-element.49), kind=kOutput, calls=%fused_computation.60 | convolution fusion | flops 20134297600 | bytes 34734080 | tf_op jit(solution)/shard_map/td,tf->df/dot_general | solution.py:131
  934.1 46.6 %all-gather.11.cloned.1.call-done = bf16[6144,1280]{1,0:T(8,128)(2,1)} async-done(((bf16[1536,1280]{1,0:T(8,128)(2,1)}), bf16[6144,1280]{1,0:T(8,128)(2,1)}) %all-gather.11.cloned.1.call-update) | async-done | bytes 15728656 | tf_op jit(solution)/shard_map/all_gather | solution.py:143
  980.7 17.7 %convolution_convert_fusion.6 = bf16[6144,320]{0,1:T(8,128)(2,1)} fusion(bf16[6144,1280]{1,0:T(8,128)(2,1)} %all-gather.11.cloned.1.call-done, bf16[320,1280]{1,0:T(8,128)(2,1)S(1)} %copy-done.39), kind=kOutput, calls=%fused_computation.37 | convolution fusion | flops 5035130880 | bytes 20480000 | tf_op jit(solution)/shard_map/td,kd->tk/dot_general | solution.py:145
  998.4 11.6 reshape.115
  1010.1 11.7 copy.69
  1021.8 10.0 convert_bitcast_fusion
  1031.8 14.5 multiply_reduce_fusion
  1046.3 10.3 multiply_convert_fusion.3
  1066.5 9.7 fusion.26
  1076.2 18.5 %copy.77 = bf16[96,64,4,80]{3,2,1,0:T(4,128)(2,1)} copy(bf16[96,64,4,80]{3,1,2,0:T(8,128)(2,1)} %convert_bitcast_fusion) | data formatting | bytes 7864320 | tf_op jit(solution)/shard_map/convert_element_type | solution.py:158
  1094.7 10.8 reshape.110
  1105.5 18.3 %copy.73 = bf16[96,64,4,80]{3,2,1,0:T(4,128)(2,1)} copy(bf16[96,64,4,80]{3,1,2,0:T(8,128)(2,1)} %fusion.26) | data formatting | bytes 7864320 | tf_op jit(solution)/shard_map/convert_element_type | solution.py:163
  1123.8 10.8 reshape.108
  1134.6 18.5 %copy.75 = bf16[96,64,4,80]{3,2,1,0:T(4,128)(2,1)} copy(bf16[96,64,4,80]{3,1,2,0:T(8,128)(2,1)} %fusion.27) | data formatting | bytes 7864320 | tf_op jit(solution)/shard_map/convert_element_type | solution.py:167
  1153.1 10.8 reshape.109
  1163.9 20.7 %fusion.30 = bf16[1280,960]{0,1:T(8,128)(2,1)S(1)} fusion(bf16[6144,1280]{1,0:T(8,128)(2,1)} %all-gather.5.cloned.1.call-done, bf16[6144,320]{1,0:T(8,128)(2,1)} %reshape.110, bf16[6144,320]{1,0:T(8,128)(2,1)} %reshape.109, bf16[6144,320]{1,0:T(8,128)(2,1)} %reshape.108), kind=kOutput, calls=%fused_computation.68 | convolution fusion | flops 15136112640 | bytes 29982720 | tf_op jit(solution)/shard_map/td,tk->dk/dot_general | solution.py:176
  1186.0 13.1 convolution_convert_fusion.9
  1199.2 23.1 %convolution_convert_fusion.4 = bf16[6144,1280]{1,0:T(8,128)(2,1)} fusion(bf16[1280,960]{0,1:T(8,128)(2,1)} %constant_dynamic-update-slice_fusion, bf16[6144,320]{1,0:T(8,128)(2,1)} %reshape.110, bf16[6144,320]{1,0:T(8,128)(2,1)} %reshape.109, bf16[6144,320]{1,0:T(8,128)(2,1)} %reshape.108), kind=kOutput, calls=%fused_computation.8 | convolution fusion | flops 15142748160 | bytes 29982720 | tf_op jit(solution)/shard_map/tk,dk->td/dot_general | solution.py:183
  1223.0 22.7 %psum.89 = bf16[1280]{0:T(1024)(128)(2,1)S(1)} all-reduce(bf16[1280]{0:T(1024)(128)(2,1)S(1)} %copy-done.37), channel_id=1, replica_groups=mesh['dp'=8,'mp'=4] {'dp'}, use_global_device_ids=true, to_apply=%region_19.20 | all-reduce | flops 1280 | bytes 5120 | tf_op jit(solution)/shard_map/psum | solution.py:198
  1248.4 263.5 %all-reduce.4.cloned.1.call-done = (bf16[1280,320]{0,1:T(8,128)(2,1)}, bf16[1280,320]{0,1:T(8,128)(2,1)}, bf16[1280,320]{0,1:T(8,128)(2,1)}, bf16[320,1280]{1,0:...) async-done(((bf16[1280,320]{0,1:T(8,128)(2,1)}, bf16[1280,320]{0,1:T(8,128)(2,1)}, bf16[1280,320]{0,1:T(8,128)(2,1)}, bf16[320,1280]{1,0:T(8,128)(2,1)}, ...) | async-done | bytes 9830416 | tf_op jit(solution)/shard_map/psum | solution.py:193
  1529.8 103.7 %reduce-scatter.11.cloned.1.call-done = bf16[1536,1280]{1,0:T(8,128)(2,1)} async-done(((bf16[6144,1280]{1,0:T(8,128)(2,1)}), bf16[1536,1280]{1,0:T(8,128)(2,1)}) %reduce-scatter.11.cloned.1.call-update) | async-done | bytes 3932176 | tf_op jit(solution)/shard_map/reduce_scatter | solution.py:182
  1639.2 12.3 convert_reduce_fusion
  1651.5 40.0 %all-reduce = (f32[1280]{0:T(1024)}, f32[1280]{0:T(1024)}, f32[1280]{0:T(1024)}, f32[3]{0:T(128)S(1)}, f32[]{:T(128)}) all-reduce(f32[1280]{0:T(1024)S(1)} %get-tuple-element.37, f32[1280]{0:T(1024)S(1)} %get-tuple-element.16, f32[1280]{0:T(1024)S(1)} %copy-done.32, ...), channel_id=1, replica_groups=mesh['dp'=8,'mp'=4] {'dp','mp'}, use_global_device_ids=true, to_apply=%region_22.23 | all-reduce | flops 3844 | bytes 30752 | tf_op jit(solution)/shard_map/psum | solution.py:201
  (142 shorter events, 80.3 us)
Async XLA Ops:
  7.2 508.1 %copy-start = (bf16[1280,1280]{1,0:T(8,128)(2,1)S(1)}, bf16[1280,1280]{1,0:T(8,128)(2,1)}, u32[]{:S(2)}) copy-start(bf16[1280,1280]{1,0:T(8,128)(2,1)} %param.20) | copy-start | bytes 9830404
  7.2 112.4 %all-gather.5.cloned.1.call-start = ((), (), s32[]{:S(2)}) async-start(), calls=%async_computation.4 | async-start | bytes 19660800 | tf_op jit(solution)/shard_map/all_gather | solution.py:70
  8.1 3.1 copy-start.26
  8.1 8.8 copy-start.33
  16.8 389.7 %reduce-scatter.5.cloned.1.call-start = ((), (), s32[]{:S(2)}) async-start(), calls=%async_computation.5 | async-start | bytes 19660800 | tf_op jit(solution)/shard_map/reduce_scatter | solution.py:91
  17.4 121.3 %copy-start.18 = (s32[96,64]{0,1:T(8,128)}, s32[96,64]{0,1:T(8,128)S(1)}, u32[]{:S(2)}) copy-start(s32[96,64]{0,1:T(8,128)S(1)} %convert_reduce_fusion.1) | copy-start | bytes 73732
  225.8 8.2 copy-start.16
  225.8 9.2 slice-start
  225.8 9.2 slice-start.1
  234.9 8.7 copy-start.12
  286.4 0.7 copy-start.34
  286.5 228.8 %all-gather.7.cloned.1.call-start = ((), (), s32[]{:S(2)}) async-start(), calls=%async_computation.6 | async-start | bytes 19660800 | tf_op jit(solution)/shard_map/all_gather | solution.py:99
  287.1 128.0 %copy-start.20 = (f32[1280]{0:T(1024)}, f32[1280]{0:T(1024)S(1)}, u32[]{:S(2)}) copy-start(f32[1280]{0:T(1024)S(1)} %convert_element_type.159) | copy-start | bytes 15364
  406.5 5.4 copy-start.2
  406.5 5.6 copy-start.5
  412.1 3.7 copy-start.35
  415.2 201.5 %all-gather.9.cloned.1.call-start = ((), (), s32[]{:S(2)}) async-start(), calls=%async_computation.8 | async-start | bytes 19660800 | tf_op jit(solution)/shard_map/all_gather | solution.py:123
  415.8 323.3 %reduce-scatter.7.cloned.1.call-start = ((), (), s32[]{:S(2)}) async-start(), calls=%async_computation.7 | async-start | bytes 19660800 | tf_op jit(solution)/shard_map/reduce_scatter | solution.py:105
  515.3 32.7 %copy-start.38 = (bf16[1280,1280]{1,0:T(8,128)(2,1)S(1)}, bf16[1280,1280]{1,0:T(8,128)(2,1)}, u32[]{:S(2)}) copy-start(bf16[1280,1280]{1,0:T(8,128)(2,1)} %param.22) | copy-start | bytes 9830404
  573.9 287.5 %reduce-scatter.9.cloned.1.call-start = ((), (), s32[]{:S(2)}) async-start(), calls=%async_computation.9 | async-start | bytes 19660800 | tf_op jit(solution)/shard_map/reduce_scatter | solution.py:132
  681.1 0.7 copy-start.36
  681.1 0.8 copy-start.19
  681.1 180.3 %copy-start.21 = (f32[1280]{0:T(1024)S(1)}, f32[1280]{0:T(1024)}, u32[]{:S(2)}) copy-start(f32[1280]{0:T(1024)} %copy-done.20) | copy-start | bytes 15364
  681.1 180.3 %copy-start.24 = (f32[1536]{0:T(1024)S(1)}, f32[1536]{0:T(1024)}, u32[]{:S(2)}) copy-start(f32[1536]{0:T(1024)} %copy-done.23) | copy-start | bytes 18436
  681.1 299.6 %all-gather.11.cloned.1.call-start = ((), (), s32[]{:S(2)}) async-start(), calls=%async_computation.10 | async-start | bytes 19660800 | tf_op jit(solution)/shard_map/all_gather | solution.py:143
  861.4 13.9 copy-start.3
  861.4 13.9 copy-start.6
  861.4 13.9 copy-start.10
  861.4 13.9 copy-start.11
  875.3 5.3 copy-start.30
  880.6 631.3 %all-reduce.4.cloned.1.call-start = ((), (), s32[]{:S(2)}) async-start(), calls=%async_computation.12 | async-start | bytes 19660800 | tf_op jit(solution)/shard_map/psum | solution.py:193
  907.4 73.4 %copy-start.39 = (bf16[320,1280]{1,0:T(8,128)(2,1)S(1)}, bf16[320,1280]{1,0:T(8,128)(2,1)}, u32[]{:S(2)}) copy-start(bf16[320,1280]{1,0:T(8,128)(2,1)} %param.19) | copy-start | bytes 2457604
  1010.1 11.7 copy-start.9
  1010.1 11.7 copy-start.13
  1056.6 2.7 copy-start.8
  1199.1 434.4 %reduce-scatter.11.cloned.1.call-start = ((), (), s32[]{:S(2)}) async-start(), calls=%async_computation.11 | async-start | bytes 19660800 | tf_op jit(solution)/shard_map/reduce_scatter | solution.py:182
  1511.9 7.6 copy-start.17
  1511.9 8.8 copy-start.15
  1516.9 8.4 copy-start.14
  1520.7 112.8 %copy-start.27 = (f32[1280]{0:T(1024)S(1)}, f32[1280]{0:T(1024)}, u32[]{:S(2)}) copy-start(f32[1280]{0:T(1024)} %copy-done.26) | copy-start | bytes 15364
  1520.7 112.8 %copy-start.29 = (f32[1536]{0:T(1024)S(1)}, f32[1536]{0:T(1024)}, u32[]{:S(2)}) copy-start(f32[1536]{0:T(1024)} %copy-done.28) | copy-start | bytes 18436
  1525.3 113.8 %copy-start.22 = (f32[1280]{0:T(1024)S(1)}, f32[1280]{0:T(1024)}, u32[]{:S(2)}) copy-start(f32[1280]{0:T(1024)} %copy-done.20) | copy-start | bytes 15364
  1525.3 113.8 %copy-start.25 = (f32[1536]{0:T(1024)S(1)}, f32[1536]{0:T(1024)}, u32[]{:S(2)}) copy-start(f32[1536]{0:T(1024)} %copy-done.23) | copy-start | bytes 18436
  1525.3 113.8 %copy-start.31 = (f32[1536]{0:T(1024)S(1)}, f32[1536]{0:T(1024)}, u32[]{:S(2)}) copy-start(f32[1536]{0:T(1024)} %copy-done.30) | copy-start | bytes 18436
  1633.5 5.6 copy-start.4
  1633.5 5.6 copy-start.7
  1639.1 53.6 %copy-start.1 = (bf16[1280,1280]{1,0:T(8,128)(2,1)S(1)}, bf16[1280,1280]{1,0:T(8,128)(2,1)}, u32[]{:S(2)}) copy-start(bf16[1280,1280]{1,0:T(8,128)(2,1)} %param.20) | copy-start | bytes 9830404
  1639.2 12.3 copy-start.32
  (3 other events, 1.9 us)
Sparse Core Ops, SparseCore 0:
  16.9 102.6 all-gather.4
  286.6 119.8 reduce-scatter.4
  415.3 99.9 all-gather.6
  516.7 99.9 all-gather.8
  619.2 119.8 reduce-scatter.6
  741.5 119.8 reduce-scatter.8
  880.7 99.9 all-gather.10
  1199.3 312.5 all-reduce.3
  1514.7 118.8 reduce-scatter.10
where the time goes:
time: 1710 us; the launch traced here: 1700 us
  waiting for transfers between devices  948 us (55%)
  matrix products  346 us (20%)
  local copies, waits for them, and re-layouts  229 us (13%)
  other arithmetic  97.8 us (6%)
  blocking collectives  62.7 us (4%)
    psum x1, waiting for transfers between devices, per_device(): lax.psum(query_part.astype(jnp.bfloat16), 'dp').astype(jnp.float32)  263 us
    reduce_scatter x1, waiting for transfers between devices, per_device(): lax.psum_scatter(jnp.einsum('tf,df->td', preact_grad, up_weight, preferre...  122 us
    reduce_scatter x1, waiting for transfers between devices, per_device(): lax.psum_scatter(jnp.dot(mixed, out_weight, preferred_element_type=jnp.fl...  119 us
    reduce_scatter x1, waiting for transfers between devices, per_device(): lax.psum_scatter(jnp.einsum('tk,dk->td', joined_grad, joined_weight, pref...  104 us
    all_gather x1, waiting for transfers between devices, per_device(): second_rows = lax.all_gather(second_normed, 'mp', axis=0, tiled=True)  99.5 us
    all_gather x1, waiting for transfers between devices, per_device(): first_rows = lax.all_gather(first_normed, 'mp', axis=0, tiled=True)  93.4 us
    reduce_scatter x1, waiting for transfers between devices, per_device(): lax.psum_scatter(jnp.dot(active, down_weight, preferred_element_type=jnp....  56.3 us
    all_gather x1, waiting for transfers between devices, per_device(): branch_grad = lax.all_gather(branch_low, 'mp', axis=0, tiled=True)  46.6 us
  transfers between devices with their start and end apart: 9, of which 9 were waited for; matrix products, arithmetic and copies ran while one was open for 14% of the time, Pallas kernels for 0%

commit v1 on v0

v1 whole, which is shorter than its diff:
```python
import functools
import math

import jax
import jax.numpy as jnp
from jax import lax
from jax.experimental import pallas as pl
from jax.experimental.pallas import tpu as pltpu
from jax.sharding import PartitionSpec as P

HD = 80
L = 64
SLOTS = 32
LANES = 128
EPSILON = 1e-06
MASKED = -1e30
F32 = jnp.float32
BF = jnp.bfloat16
NN = (((1,), (0,)), ((), ()))
NT = (((1,), (1,)), ((), ()))
TN = (((0,), (0,)), ((), ()))
VMEM_BYTES = 60 << 20


def dot(a, b, dims=NN):
    return lax.dot_general(a, b, dims, preferred_element_type=F32)


def pick(n, *sizes):
    return next((s for s in sizes if n % s == 0), n)


def feed_body(chunk, rows, n2, n2t, g, gt, wua, wub, wda, wdb, hba, hbb, feed, n2g, dua, dub, dda, ddb, ba, bb, acc_f, acc_n, act, pg, wu, wd):
    step = pl.program_id(0)
    T, D = n2.shape
    ft = wua.shape[1]

    @pl.when(step == 0)
    def _():
        acc_f[...] = jnp.zeros_like(acc_f)
        acc_n[...] = jnp.zeros_like(acc_n)

    wu[:, :ft], wu[:, ft:] = wua[...], wub[...]
    wd[:ft, :], wd[ft:, :] = wda[...], wdb[...]
    hb = jnp.concatenate([hba[...], hbb[...]], axis=1).astype(F32)
    ba[...] = jnp.zeros_like(ba)
    bb[...] = jnp.zeros_like(bb)

    def one(i, _):
        s = pl.ds(pl.multiple_of(i * chunk, chunk), chunk)
        p = dot(n2[s, :], wu[...]) + hb
        ag = dot(g[s, :], wd[...], NT)
        sg = 0.5 * jnp.tanh(0.5 * p) + 0.5
        ps = p * sg
        a = ps.astype(BF)
        q = (ag * (sg + ps * (1.0 - sg))).astype(BF)
        act[s, :] = a
        pg[s, :] = q
        b = jnp.sum(q.astype(F32), axis=0, keepdims=True)
        ba[...] += b[:, :ft]
        bb[...] += b[:, ft:]
        acc_f[s, :] += dot(a, wd[...])
        acc_n[s, :] += dot(q, wu[...], NT)
        return 0

    lax.fori_loop(0, T // chunk, one, 0)

    def two(i, _):
        s = pl.ds(pl.multiple_of(i * rows, rows), rows)
        u = dot(n2t[s, :], pg[...]).astype(BF)
        dua[s, :], dub[s, :] = u[:, :ft], u[:, ft:]
        d = dot(gt[s, :], act[...]).astype(BF)
        dda[s, :], ddb[s, :] = d[:, :ft], d[:, ft:]
        return 0

    lax.fori_loop(0, D // rows, two, 0)

    @pl.when(step == pl.num_programs(0) - 1)
    def _():
        feed[...] = acc_f[...].astype(BF)
        n2g[...] = acc_n[...].astype(BF)


def feed_forward(n2, n2t, g, gt, ups, downs, biases):
    T, D = n2.shape
    F = ups[0].shape[1]
    ft = pick(F, 256)
    chunk, rows = pick(T, 768, 384, 128), pick(D, 640, 256)
    one = lambda s: pl.BlockSpec(s, lambda f: (0, 0), pipeline_mode=pl.Buffered(1))
    up = pl.BlockSpec((D, ft), lambda f: (0, f))
    down = pl.BlockSpec((ft, D), lambda f: (f, 0))
    bias = pl.BlockSpec((1, ft), lambda f: (0, f))
    return pl.pallas_call(
        functools.partial(feed_body, chunk, rows),
        grid=(F // ft,),
        in_specs=[one((T, D)), one((D, T)), one((T, D)), one((D, T)), up, up, down, down, bias, bias],
        out_specs=[one((T, D)), one((T, D)), up, up, up, up, bias, bias],
        out_shape=[jax.ShapeDtypeStruct((T, D), BF)] * 2
        + [jax.ShapeDtypeStruct((D, F), BF)] * 4
        + [jax.ShapeDtypeStruct((1, F), F32)] * 2,
        scratch_shapes=[
            pltpu.VMEM((T, D), F32),
            pltpu.VMEM((T, D), F32),
            pltpu.VMEM((T, 2 * ft), BF),
            pltpu.VMEM((T, 2 * ft), BF),
            pltpu.VMEM((D, 2 * ft), BF),
            pltpu.VMEM((2 * ft, D), BF),
        ],
        compiler_params=pltpu.CompilerParams(vmem_limit_bytes=VMEM_BYTES),
        cost_estimate=pl.CostEstimate(
            flops=24 * T * D * F, bytes_accessed=24 * T * D + 16 * D * F, transcendentals=2 * T * F
        ),
        name="feed_forward",
    )(n2, n2t, g, gt, *ups, *downs, *biases)


def windows(C):
    out=[]
    for h in range(C//HD):
        w=min(LANES*(HD*h//LANES),C-2*LANES)
        out.append((w,HD*h-w))
    return out
def head_masks(C):
    lane=lax.broadcasted_iota(jnp.int32,(1,2*LANES),1)
    return [jnp.where((lane>=lo)&(lane<lo+HD),1.0,0.0).astype(BF) for _,lo in windows(C)]
def softmaxes(qs,ks,allowed):
    s=[jnp.where(allowed,dot(q,k,NT)*(1.0/math.sqrt(HD)),MASKED) for q,k in zip(qs,ks)]
    e=[jnp.exp(x-jnp.max(x,axis=1,keepdims=True)) for x in s]
    return [x*(1.0/jnp.sum(x,axis=1,keepdims=True)) for x in e]
def allow(idc,idr,s,B):
    causal=lax.broadcasted_iota(jnp.int32,(B,B),1)<=lax.broadcasted_iota(jnp.int32,(B,B),0)
    return (idc[s,:]==idr[:,s])&causal
def put(tiles,w,val):
    for n in range(2):
        t=w//LANES+n; part=val[:,n*LANES:(n+1)*LANES]
        tiles[t]=part if tiles[t] is None else tiles[t]+part
def fwd_body(B,C,per,n1,w,idc,idr,qkv,mixed,mixedt):
    T=n1.shape[0]
    qkv[...]=dot(n1[...],w[...]).astype(BF)
    masks=head_masks(C); wins=[w for w,_ in windows(C)]
    def block(i,_):
        s=pl.ds(pl.multiple_of(i*B,B),B)
        ok=allow(idc,idr,s,B)
        tiles=[None]*(C//LANES)
        cut=lambda n,w: qkv[s,n*C+w:n*C+w+2*LANES]
        for g in range(0,len(wins),per):
            hs=range(g,min(g+per,len(wins)))
            p=softmaxes([cut(0,wins[h])*masks[h] for h in hs],[cut(1,wins[h]) for h in hs],ok)
            o=[dot(x.astype(BF),cut(2,wins[h])*masks[h]) for x,h in zip(p,hs)]
            for h,x in zip(hs,o): put(tiles,wins[h],x)
        mx=jnp.concatenate(tiles,axis=1)
        mixed[s,:]=mx.astype(BF); mixedt[:,s]=mx.T.astype(BF)
        return 0
    lax.fori_loop(0,T//B,block,0)
def att_fwd(n1,w,idc,idr,tt=512,B=128,per=8):
    T,D=n1.shape; C=w.shape[1]//3
    tt=pick(T,tt,384,256,128)
    return pl.pallas_call(functools.partial(fwd_body,B,C,per),grid=(T//tt,),
        in_specs=[pl.BlockSpec((tt,D),lambda i:(i,0)),pl.BlockSpec((D,3*C),lambda i:(0,0),pipeline_mode=pl.Buffered(1)),pl.BlockSpec((tt,1),lambda i:(i,0)),pl.BlockSpec((1,tt),lambda i:(0,i))],
        out_specs=[pl.BlockSpec((tt,3*C),lambda i:(i,0)),pl.BlockSpec((tt,C),lambda i:(i,0)),pl.BlockSpec((C,tt),lambda i:(0,i))],
        out_shape=[jax.ShapeDtypeStruct((T,3*C),BF),jax.ShapeDtypeStruct((T,C),BF),jax.ShapeDtypeStruct((C,T),BF)],
        compiler_params=pltpu.CompilerParams(vmem_limit_bytes=VMEM_BYTES),
        cost_estimate=pl.CostEstimate(flops=int(1.5*2*T*D*3*C),bytes_accessed=2*(T*D+4*C*D+5*T*C),transcendentals=T*B*C//HD),
        name="attend")(n1,w,idc,idr)
def bwd_body(B,C,per,rows,n1t,w,wo,hg,qkv,mixedt,idc,idr,n1g,dw,dwo,dqkv,dmix):
    step=pl.program_id(0); last=pl.num_programs(0)-1
    tt=qkv.shape[0]; D=hg.shape[1]; scale=1.0/math.sqrt(HD)
    base=pl.multiple_of(step*tt,tt)
    dmix[...]=dot(hg[pl.ds(base,tt),:],wo[...],NT).astype(BF)
    masks=head_masks(C); wins=[w for w,_ in windows(C)]
    def block(i,_):
        s=pl.ds(pl.multiple_of(i*B,B),B)
        ok=allow(idc,idr,s,B)
        dq=[None]*(C//LANES); dk=list(dq); dv=list(dq)
        cut=lambda n,w: qkv[s,n*C+w:n*C+w+2*LANES]
        for g in range(0,len(wins),per):
            hs=range(g,min(g+per,len(wins)))
            q=[cut(0,wins[h])*masks[h] for h in hs]
            gm=[dmix[s,wins[h]:wins[h]+2*LANES]*masks[h] for h in hs]
            p=softmaxes(q,[cut(1,wins[h]) for h in hs],ok)
            dp=[dot(x,cut(2,wins[h]),NT) for x,h in zip(gm,hs)]
            ds=[(a*(b-jnp.sum(a*b,axis=1,keepdims=True))).astype(BF) for a,b in zip(p,dp)]
            for h,a,b,c,d in zip(hs,p,gm,ds,q):
                put(dv,wins[h],dot(a.astype(BF),b,TN))
                put(dk,wins[h],dot(c,d,TN))
                put(dq,wins[h],dot(c,cut(1,wins[h])*masks[h]))
        o=pl.ds(pl.multiple_of(base+i*B,B),B)
        for n,(tiles,c) in enumerate(((dq,scale),(dk,scale),(dv,None))):
            a=jnp.concatenate(tiles,axis=1)
            dqkv[o,n*C:(n+1)*C]=(a if c is None else a*c).astype(BF)
        return 0
    lax.fori_loop(0,tt//B,block,0)
    n1g[...]=dot(dqkv[pl.ds(base,tt),:],w[...],NT).astype(n1g.dtype)
    @pl.when(step==last)
    def _():
        def two(i,_):
            s=pl.ds(pl.multiple_of(i*rows,rows),rows)
            dw[s,:]=dot(n1t[s,:],dqkv[...]).astype(dw.dtype)
            return 0
        lax.fori_loop(0,D//rows,two,0)
        dwo[...]=dot(mixedt[...],hg[...]).astype(dwo.dtype)
def att_bwd(n1t,w,wo,hg,qkv,mixedt,idc,idr,tt=512,B=128,rows=256,per=8):
    D,T=n1t.shape; C=w.shape[1]//3
    tt=pick(T,tt,384,256,128)
    one=lambda s: pl.BlockSpec(s,lambda i:(0,0),pipeline_mode=pl.Buffered(1))
    return pl.pallas_call(functools.partial(bwd_body,B,C,per,rows),grid=(T//tt,),
        in_specs=[one((D,T)),one((D,3*C)),one((C,D)),one((T,D)),pl.BlockSpec((tt,3*C),lambda i:(i,0)),one((C,T)),pl.BlockSpec((tt,1),lambda i:(i,0)),pl.BlockSpec((1,tt),lambda i:(0,i))],
        out_specs=[pl.BlockSpec((tt,D),lambda i:(i,0)),one((D,3*C)),one((C,D))],
        out_shape=[jax.ShapeDtypeStruct((T,D),BF),jax.ShapeDtypeStruct((D,3*C),BF),jax.ShapeDtypeStruct((C,D),BF)],
        scratch_shapes=[pltpu.VMEM((T,3*C),BF),pltpu.VMEM((tt,C),BF)],
        compiler_params=pltpu.CompilerParams(vmem_limit_bytes=VMEM_BYTES),
        cost_estimate=pl.CostEstimate(flops=int(1.5*2*T*D*8*C),bytes_accessed=2*(3*T*D+8*C*D+5*T*C),transcendentals=T*B*C//HD),
        name="attend_back")(n1t,w,wo,hg,qkv,mixedt,idc,idr)


def pairs(n, bit):
    return [(i, i ^ bit) for i in range(n)]


def swap(a, axis, bit):
    return lax.ppermute(a, axis, pairs(lax.axis_size(axis), bit))


def add(*arrays):
    return sum(a.astype(F32) for a in arrays).astype(BF)


def halve(a, axis, bit):
    n = a.shape[0] // 2
    here = (lax.axis_index(axis) // bit) % 2
    sent = lax.dynamic_slice_in_dim(a, (1 - here) * n, n)
    kept = lax.dynamic_slice_in_dim(a, here * n, n)
    return add(kept, swap(sent, axis, bit))


def double(a, axis, bit):
    here = (lax.axis_index(axis) // bit) % 2
    other = swap(a, axis, bit)
    return jnp.where(here == 0, jnp.concatenate([a, other]), jnp.concatenate([other, a]))


def dp_bits(first):
    bits = [1 << n for n in range(lax.axis_size("dp").bit_length() - 1)]
    return bits[first:] [:1] + [b for b in bits if b != bits[first]] if len(bits) > first else bits


def dp_sum(a, first=0):
    bits = dp_bits(first)
    for bit in bits:
        a = halve(a, "dp", bit)
    for bit in reversed(bits):
        a = double(a, "dp", bit)
    return a


def all_sum(a):
    for axis in ("mp", "dp"):
        bit = 1
        while bit < lax.axis_size(axis):
            a = a + swap(a, axis, bit)
            bit *= 2
    return a


def normalize(values, gain):
    scale_rows = lax.rsqrt(jnp.mean(values * values, axis=1, keepdims=True) + EPSILON)
    return scale_rows, (values * scale_rows * gain.astype(F32)).astype(BF)


def norm_back(values, scale_rows, gain, grad):
    weighted = gain.astype(F32) * grad
    inner = jnp.sum(weighted * values, axis=1, keepdims=True)
    gain_part = jnp.sum(grad * values * scale_rows, axis=0)
    back = weighted * scale_rows - values * (
        scale_rows * scale_rows * scale_rows * inner / values.shape[1]
    )
    return gain_part, back


def segments(lengths):
    slots = lengths.shape[1]
    upto = lax.broadcasted_iota(jnp.int32, (1, slots, slots), 2) <= lax.broadcasted_iota(
        jnp.int32, (1, slots, slots), 1
    )
    ends = jnp.sum(jnp.where(upto, lengths[:, None, :], 0), axis=2)
    places = lax.broadcasted_iota(jnp.int32, (lengths.shape[0], L, slots), 1)
    return jnp.sum((ends[:, None, :] <= places).astype(jnp.int32), axis=2)


def gather_groups(weights):
    if lax.axis_size("mp") == 4:
        other = [swap(w, "mp", 2) for w in weights]
        return [
            (weights, [swap(w, "mp", 1) for w in weights]),
            (other, [swap(w, "mp", 1) for w in other]),
        ]
    dims = (1, 1, 1, 0, 1, 0, 1)
    whole = [lax.all_gather(w, "mp", axis=d, tiled=True) for w, d in zip(weights, dims)]
    return [tuple(zip(*(jnp.split(w, 2, axis=d) for w, d in zip(whole, dims))))]


def scatter_groups(groups, dims):
    if len(groups) == 2:
        own, other = ([add(a, swap(b, "mp", 1)) for a, b in zip(*g)] for g in groups)
        return [add(a, swap(b, "mp", 2)) for a, b in zip(own, other)]
    return [
        lax.psum_scatter(jnp.concatenate(pair, axis=d), "mp", scatter_dimension=d, tiled=True)
        for pair, d in zip(zip(*groups[0]), dims)
    ]


def per_device(
    tokens,
    lengths,
    cotangent,
    query_weight,
    key_weight,
    value_weight,
    out_weight,
    up_weight,
    hidden_bias,
    down_weight,
    output_bias,
    first_gain,
    second_gain,
):
    T, D = tokens.shape
    width = query_weight.shape[1]
    rows = T // L
    n_mp = lax.axis_size("mp")
    mp = lax.axis_index("mp")
    segment_ids = segments(lax.dynamic_slice_in_dim(lengths, mp * rows, rows))
    valid = (segment_ids < SLOTS).reshape(-1, 1).astype(F32)
    ids = (segment_ids + L * lax.broadcasted_iota(jnp.int32, (rows, L), 0)).reshape(-1)
    id_col, id_row = ids[:, None], ids[None, :]

    bias_row = hidden_bias.reshape(1, -1)
    groups = gather_groups(
        [query_weight, key_weight, value_weight, out_weight, up_weight, down_weight, bias_row]
    )
    inputs = tokens.astype(F32)
    r1, n1 = normalize(inputs, first_gain)
    n1t = n1.T
    attention = 0.0
    kept = []
    for a, b in groups:
        w = jnp.concatenate([a[0], b[0], a[1], b[1], a[2], b[2]], axis=1)
        wo = jnp.concatenate([a[3], b[3]], axis=0)
        qkv, mixed, mixedt = att_fwd(n1, w, id_col, id_row)
        attention = attention + dot(mixed, wo)
        kept.append((w, wo, qkv, mixedt))
    hidden = inputs + attention
    r2, n2 = normalize(hidden, second_gain)
    n2t, gt = n2.T, cotangent.T
    feed = output_bias.astype(F32)
    n2_grad = 0.0
    feed_grads = []
    bias_parts = []
    for a, b in groups:
        f, n, dua, dub, dda, ddb, ba, bb = feed_forward(
            n2, n2t, cotangent, gt, (a[4], b[4]), (a[5], b[5]), (a[6], b[6])
        )
        feed = feed + f.astype(F32)
        n2_grad = n2_grad + n.astype(F32)
        feed_grads.append(((dua, dda), (dub, ddb)))
        bias_parts.append((ba, bb))
    up_part, down_part = scatter_groups(feed_grads, (1, 1))
    up_total = dp_sum(up_part, 0).astype(F32)
    down_total = dp_sum(down_part, 1).T.astype(F32)
    result = hidden + feed
    grad_out = cotangent.astype(F32)
    second_part, second_back = norm_back(hidden, r2, second_gain, n2_grad)
    hidden_grad = grad_out + second_back
    low_grad = hidden_grad.astype(BF)
    sums = jnp.stack(
        [
            jnp.sum(valid * attention * attention),
            jnp.sum(valid * feed * feed),
            jnp.sum(valid * result * result),
            jnp.sum(valid),
        ]
    )
    if len(groups) == 2:
        hidden_units = bias_row.shape[1]
        bias = jnp.zeros((1, n_mp * hidden_units), F32)
        for flip, part in ((0, bias_parts[0][0]), (1, bias_parts[0][1]), (2, bias_parts[1][0]), (3, bias_parts[1][1])):
            bias = lax.dynamic_update_slice(bias, part, (0, (mp ^ flip) * hidden_units))
    else:
        bias = jnp.concatenate(bias_parts[0], axis=1)
    small = all_sum(
        jnp.concatenate([bias[0], second_part, jnp.sum(grad_out, axis=0), sums])
    )
    n_bias = bias.shape[1]
    bias_total = lax.dynamic_slice_in_dim(small, mp * bias_row.shape[1], bias_row.shape[1])
    second_total = small[n_bias : n_bias + D]
    output_bias_total = small[n_bias + D : n_bias + 2 * D]
    sums = small[n_bias + 2 * D :]
    rms_stats = jnp.sqrt(sums[:3] / (sums[3] * D))

    n1_grad = 0.0
    att_grads = []
    for w, wo, qkv, mixedt in kept:
        n, dw, dwo = att_bwd(n1t, w, wo, low_grad, qkv, mixedt, id_col, id_row)
        n1_grad = n1_grad + n.astype(F32)
        C = wo.shape[0]
        h = C // 2
        att_grads.append(
            tuple(
                (
                    jnp.concatenate([dw[:, i * C + k * h : i * C + (k + 1) * h] for i in range(3)], axis=1),
                    dwo[k * h : (k + 1) * h],
                )
                for k in range(2)
            )
        )
    if len(groups) == 2:
        joined_part, out_part = scatter_groups(att_grads, None)
        parts = [joined_part]
    else:
        (ja, oa), (jb, ob) = att_grads[0]
        h = ja.shape[1] // 3
        both = [
            jnp.concatenate([ja[:, i * h : (i + 1) * h], jb[:, i * h : (i + 1) * h]], axis=1)
            for i in range(3)
        ]
        parts = [lax.psum_scatter(x, "mp", scatter_dimension=1, tiled=True) for x in both]
        out_part = lax.psum_scatter(
            jnp.concatenate([oa, ob]), "mp", scatter_dimension=0, tiled=True
        )
    joined = dp_sum(jnp.concatenate(parts, axis=1), 0).astype(F32)
    out_total = dp_sum(out_part, 1).astype(F32)
    first_part, first_back = norm_back(inputs, r1, first_gain, n1_grad)
    input_gradient = hidden_grad + first_back
    first_total = all_sum(first_part)
    return (
        result.astype(BF),
        input_gradient,
        joined[:, :width],
        joined[:, width : 2 * width],
        joined[:, 2 * width :],
        out_total,
        up_total,
        bias_total.reshape(-1),
        down_total,
        output_bias_total,
        first_total,
        second_total,
        rms_stats,
    )


def solution(mesh):
    return jax.shard_map(
        per_device,
        mesh=mesh,
        in_specs=(
            P(("dp", "mp"), None),
            P("dp", None),
            P(("dp", "mp"), None),
            P(None, "mp"),
            P(None, "mp"),
            P(None, "mp"),
            P("mp", None),
            P(None, "mp"),
            P("mp"),
            P("mp", None),
            P(),
            P(),
            P(),
        ),
        out_specs=(
            P(("dp", "mp"), None),
            P(("dp", "mp"), None),
            P(None, "mp"),
            P(None, "mp"),
            P(None, "mp"),
            P("mp", None),
            P(None, "mp"),
            P("mp"),
            P("mp", None),
            P(),
            P(),
            P(),
            P(),
        ),
        check_vma=False,
    )
```

time: 1710 us -> 1050 us (0.61)
  waiting for transfers between devices: 948 us -> 384 us
  matrix products: 346 us -> 19.9 us
  Pallas kernels: 0 us -> 306 us
  local copies, waits for them, and re-layouts: 229 us -> 150 us
  blocking collectives: 62.7 us -> 0 us
  starting transfers between devices: 0.37 us -> 56.6 us
  other arithmetic: 97.8 us -> 119 us
    reduce_scatter x4 -> x0, waiting for transfers between devices: 402 us -> none  [the longest x1 122 us: per_device(): lax.psum_scatter(jnp.einsum('tf,df->td', preact_grad, up_weight, preferre...]
    ppermute x0 -> x67, waiting for transfers between devices: none -> 384 us  [swap(): return lax.ppermute(a, axis, pairs(lax.axis_size(axis), bit))]
    dot_general x18 -> x2, matrix products: 346 us -> 19.9 us  [dot(): return lax.dot_general(a, b, dims, preferred_element_type=F32)]
    pallas_call x0 -> x6, Pallas kernels: none -> 306 us  [the longest x2 157 us: feed_forward(): pl.pallas_call(functools.partial(feed_body, chunk, rows), grid=(F // ft,)...]
    all_gather x4 -> x0, waiting for transfers between devices: 282 us -> none  [the longest x1 99.5 us: per_device(): second_rows = lax.all_gather(second_normed, 'mp', axis=0, tiled=True)]
    psum x1 -> x0, waiting for transfers between devices: 263 us -> none  [per_device(): lax.psum(query_part.astype(jnp.bfloat16), 'dp').astype(jnp.float32)]
    reshape x12 -> x1, local copies, waits for them, and re-layouts: 136 us -> 0.01 us  [per_device(): bias_row = hidden_bias.reshape(1, -1)]
    convert_element_type x6 -> x2, local copies, waits for them, and re-layouts: 73.9 us -> 4.98 us  [the longest x1 4.3 us: add(): return sum((a.astype(F32) for a in arrays)).astype(BF)]
  transfers between devices with their start and end apart: 9 -> 67, of which waited for: 9 -> 24; matrix products, arithmetic and copies ran while one was open for 14% -> 24% of each run, Pallas kernels for 0% -> 17%
where the time goes in v1:
time: 1050 us; the launch traced here: 1040 us
  waiting for transfers between devices  384 us (37%)
  Pallas kernels  306 us (29%)
  local copies, waits for them, and re-layouts  150 us (14%)
  other arithmetic  119 us (11%)
  starting transfers between devices  56.6 us (5%)
  matrix products  19.9 us (2%)
    ppermute x67, waiting for transfers between devices, swap(): return lax.ppermute(a, axis, pairs(lax.axis_size(axis), bit))  384 us
    pallas_call x2, Pallas kernels, feed_forward(): pl.pallas_call(functools.partial(feed_body, chunk, rows), grid=(F // ft,)...  157 us
    pallas_call x2, Pallas kernels, att_bwd(): pl.pallas_call(functools.partial(bwd_body, B, C, per, rows), grid=(T // t...  103 us
    ppermute x67, starting transfers between devices, swap(): return lax.ppermute(a, axis, pairs(lax.axis_size(axis), bit))  56.6 us
    pallas_call x2, Pallas kernels, att_fwd(): pl.pallas_call(functools.partial(fwd_body, B, C, per), grid=(T // tt,), i...  46 us
    convert_element_type x20, other arithmetic, add(): return sum((a.astype(F32) for a in arrays)).astype(BF)  36.2 us
    ppermute x14, local copies, waits for them, and re-layouts, swap(): return lax.ppermute(a, axis, pairs(lax.axis_size(axis), bit))  33.7 us
    unnamed x92, local copies, waits for them, and re-layouts  33.5 us
  transfers between devices with their start and end apart: 67, of which 24 were waited for; matrix products, arithmetic and copies ran while one was open for 24% of the time, Pallas kernels for 17%

profile of v1, /device:TPU:0, one launch (start us, length us, event | category | flops | bytes accessed | tf_op | source)
XLA Modules:
  0.0 1038.7 jit_solution(18329279216424185068)
XLA Ops:
  19.2 6.3 copy.167
  26.1 6.3 copy.170.n1t
  37.2 5.0 fusion.5.n1
  48.9 9.0 concatenate.99.w
  65.0 10.9 %collective-permute-done.10 = bf16[320,1280]{1,0:T(8,128)(2,1)} collective-permute-done((bf16[320,1280]{1,0:T(8,128)(2,1)}, bf16[320,1280]{1,0:T(8,128)(2,1)}, u32[]{:S(2)}, u32[]{:S(2)}) %collective-permute-start.10) | collective-permute-done | bytes 819232 | tf_op jit(solution)/shard_map/ppermute | solution.py:221
  78.0 23.0 %attend.2 = (bf16[1536,1920]{1,0:T(8,128)(2,1)}, bf16[1536,640]{1,0:T(8,128)(2,1)}, bf16[640,1536]{1,0:T(8,128)(2,1)}) custom-call(bf16[1536,1280]{1,0:T(8,128)(2,1)} %fusion.5.n1, bf16[1280,1920]{1,0:T(8,128)(2,1)} %concatenate.99.w, s32[1536,1]{1,0:T(8,128)} %add.361.idc, s32[1,1536]{1,0:T(1,128)} %add.291.idr), custom_call_target="tpu_custom_call" | custom-call | flops 11324620800 | bytes 20316160 | tf_op jit(solution)/shard_map/attend/pallas_call | solution.py:158
  103.7 8.5 fusion.29
  121.2 9.0 concatenate.101.w
  130.3 23.0 %attend.3 = (bf16[1536,1920]{1,0:T(8,128)(2,1)}, bf16[1536,640]{1,0:T(8,128)(2,1)}, bf16[640,1536]{1,0:T(8,128)(2,1)}) custom-call(bf16[1536,1280]{1,0:T(8,128)(2,1)} %fusion.5.n1, bf16[1280,1920]{1,0:T(8,128)(2,1)} %concatenate.101.w, s32[1536,1]{1,0:T(8,128)} %add.361.idc, s32[1,1536]{1,0:T(1,128)} %add.291.idr), custom_call_target="tpu_custom_call" | custom-call | flops 11324620800 | bytes 20316160 | tf_op jit(solution)/shard_map/attend/pallas_call | solution.py:158
  155.4 11.5 %multiply_reduce_fusion.2 = (f32[1536]{0:T(1024)S(1)}, f32[1536,1280]{1,0:T(8,128)S(1)}, f32[1536,1280]{1,0:T(8,128)}) fusion(bf16[1536,1280]{1,0:T(8,128)(2,1)S(1)} %copy-done.4, f32[1536,1280]{1,0:T(8,128)} %fusion.29, bf16[1536,640]{1,0:T(8,128)(2,1)} %get-tuple-element.42, bf16[640,1280]{1,0:T(8,128)(2,1)} %constant_dynamic-update-slice_fusion.2.wo), kind=kOutput, calls=%fused_computation.29 | convolution fusion | flops 2526411264 | bytes 31135744 | tf_op jit(solution)/shard_map/dot_general | solution.py:26
  169.9 46.2 %collective-permute-done.19.hba = bf16[1,1280]{1,0:T(2,128)(2,1)S(1)} collective-permute-done((bf16[1,1280]{1,0:T(2,128)(2,1)S(1)}, bf16[1,1280]{1,0:T(2,128)(2,1)S(1)}, u32[]{:S(2)}, u32[]{:S(2)}) %collective-permute-start.19) | collective-permute-done | bytes 2592 | tf_op jit(solution)/shard_map/ppermute | solution.py:221
  218.9 6.7 copy.168.n2t
  226.7 78.5 %feed_forward.2 = (bf16[1536,1280]{1,0:T(8,128)(2,1)}, bf16[1536,1280]{1,0:T(8,128)(2,1)}, bf16[1280,1280]{1,0:T(8,128)(2,1)}, bf16[1280,1280]{1,0:T(8,128)(2,1)...) custom-call(bf16[1536,1280]{1,0:T(8,128)(2,1)} %multiply_convert_fusion.n2, ...), custom_call_target="tpu_custom_call" | custom-call | flops 60397977600 | bytes 73400320 | tf_op jit(solution)/shard_map/feed_forward/pallas_call | solution.py:93
  310.6 78.7 %feed_forward.3 = (bf16[1536,1280]{1,0:T(8,128)(2,1)}, bf16[1536,1280]{1,0:T(8,128)(2,1)}, bf16[1280,1280]{1,0:T(8,128)(2,1)}, bf16[1280,1280]{1,0:T(8,128)(2,1)...) custom-call(bf16[1536,1280]{1,0:T(8,128)(2,1)} %multiply_convert_fusion.n2, ...), custom_call_target="tpu_custom_call" | custom-call | flops 60397977600 | bytes 73400320 | tf_op jit(solution)/shard_map/feed_forward/pallas_call | solution.py:93
  389.4 16.0 %fusion.2 = (f32[]{:T(128)}, f32[]{:T(128)}, f32[1536]{0:T(1024)S(1)}, f32[1280]{0:T(1024)S(1)}, f32[]{:T(128)}, /*index=5*/bf16[1536,1280]{1,0:T(8,128)(2,1)}) fusion(f32[1536]{0:T(1024)S(1)} %copy-done.25, f32[1536,1280]{1,0:T(8,128)} %copy-done.2, bf16[1536,1280]{1,0:T(8,128)(2,1)} %get-tuple-element.44, bf16[1536,1280]{1,0:T(8,128)(2,1)} %get-tuple-element.43, ...), kind=kLoop, calls=%fused_computation.14 | loop fusion | flops 47183104 | bytes 35423244 | tf_op jit(solution)/shard_map/reduce_sum | solution.py:379
  405.5 4.1 fusion.24.hg
  409.6 51.5 %attend_back.3 = (bf16[1536,1280]{1,0:T(8,128)(2,1)}, bf16[1280,1920]{1,0:T(8,128)(2,1)}, bf16[640,1280]{1,0:T(8,128)(2,1)}) custom-call(bf16[1280,1536]{1,0:T(8,128)(2,1)} %copy.170.n1t, bf16[1280,1920]{1,0:T(8,128)(2,1)} %concatenate.101.w, bf16[640,1280]{1,0:T(8,128)(2,1)} %constant_dynamic-update-slice_fusion.2.wo, bf16[1536,1280]{1,0:T(8,128)(2,1)} %fusion.24.hg, ...), custom_call_target="tpu_custom_call" | custom-call | flops 30198988800 | bytes 34734080 | tf_op jit(solution)/shard_map/attend_back/pallas_call | solution.py:206
  461.1 6.3 fusion.27
  471.1 51.4 %attend_back.2 = (bf16[1536,1280]{1,0:T(8,128)(2,1)}, bf16[1280,1920]{1,0:T(8,128)(2,1)}, bf16[640,1280]{1,0:T(8,128)(2,1)}) custom-call(bf16[1280,1536]{1,0:T(8,128)(2,1)} %copy.170.n1t, bf16[1280,1920]{1,0:T(8,128)(2,1)} %concatenate.99.w, bf16[640,1280]{1,0:T(8,128)(2,1)} %constant_dynamic-update-slice_fusion.wo, bf16[1536,1280]{1,0:T(8,128)(2,1)} %fusion.24.hg, ...), custom_call_target="tpu_custom_call" | custom-call | flops 30198988800 | bytes 34734080 | tf_op jit(solution)/shard_map/attend_back/pallas_call | solution.py:206
  522.5 6.2 fusion.26
  536.2 6.6 fusion.10
  545.6 12.2 %convert_reduce_fusion = (f32[1280]{0:T(1024)S(1)}, f32[1536,1280]{1,0:T(8,128)}) fusion(bf16[1536,1280]{1,0:T(8,128)(2,1)S(1)} %copy-done.7, f32[1536]{0:T(1024)S(1)} %fusion.21, bf16[1536,1280]{1,0:T(8,128)(2,1)S(1)} %copy-done.5, f32[1536]{0:T(1024)S(1)} %copy-done.22, bf16[1536,1280]{1,0:T(8,128)(2,1)} %get-tuple-element.52, ...), kind=kLoop, calls=%fused_computation.9 | loop fusion | flops 37354240 | bytes 39361536 | tf_op jit(solution)/shard_map/reduce_sum | solution.py:391
  571.9 4.7 add_convert_fusion.7
  576.6 4.3 copy.178
  583.0 53.8 %collective-permute-done.63 = f32[1280]{0:T(1024)S(1)} collective-permute-done((f32[1280]{0:T(1024)S(1)}, f32[1280]{0:T(1024)S(1)}, u32[]{:S(2)}, u32[]{:S(2)}) %collective-permute-start.63) | collective-permute-done | bytes 5152 | tf_op jit(solution)/shard_map/ppermute | solution.py:221
  670.8 4.4 copy.175
  676.9 4.4 add_convert_fusion.1
  682.8 4.4 copy.179
  687.2 4.4 add_convert_fusion.6
  696.0 5.5 add_convert_fusion.4
  703.5 21.0 %collective-permute-done.24 = bf16[640,960]{0,1:T(8,128)(2,1)} collective-permute-done((bf16[640,960]{0,1:T(8,128)(2,1)}, bf16[640,960]{0,1:T(8,128)(2,1)}, u32[]{:S(2)}, u32[]{:S(2)}) %collective-permute-start.24) | collective-permute-done | bytes 1228832 | tf_op jit(solution)/shard_map/ppermute | solution.py:221
  732.0 23.5 %collective-permute-done.55 = bf16[1280,1280]{1,0:T(8,128)(2,1)} collective-permute-done((bf16[1280,1280]{1,0:T(8,128)(2,1)}, bf16[1280,1280]{1,0:T(8,128)(2,1)}, u32[]{:S(2)}, u32[]{:S(2)}) %collective-permute-start.55) | collective-permute-done | bytes 3276832 | tf_op jit(solution)/shard_map/ppermute | solution.py:221
  755.5 4.2 add_convert_fusion
  760.1 64.8 %collective-permute-done.41 = bf16[1280,1280]{1,0:T(8,128)(2,1)} collective-permute-done((bf16[1280,1280]{1,0:T(8,128)(2,1)}, bf16[1280,1280]{1,0:T(8,128)(2,1)}, u32[]{:S(2)}, u32[]{:S(2)}) %collective-permute-start.41) | collective-permute-done | bytes 3276832 | tf_op jit(solution)/shard_map/ppermute | solution.py:221
  824.9 4.2 add_convert_fusion.3
  833.1 15.7 %collective-permute-done.26 = bf16[160,960]{1,0:T(8,128)(2,1)S(1)} collective-permute-done((bf16[160,960]{1,0:T(8,128)(2,1)S(1)}, bf16[160,960]{1,0:T(8,128)(2,1)S(1)}, u32[]{:S(2)}, u32[]{:S(2)}) %collective-permute-start.26) | collective-permute-done | bytes 307232 | tf_op jit(solution)/shard_map/ppermute | solution.py:221
  851.1 17.0 %collective-permute-done.42 = bf16[640,1280]{1,0:T(8,128)(2,1)S(1)} collective-permute-done((bf16[640,1280]{1,0:T(8,128)(2,1)S(1)}, bf16[640,1280]{1,0:T(8,128)(2,1)S(1)}, u32[]{:S(2)}, u32[]{:S(2)}) %collective-permute-start.42) | collective-permute-done | bytes 1638432 | tf_op jit(solution)/shard_map/ppermute | solution.py:221
  871.0 13.0 %collective-permute-done.57 = bf16[320,1280]{1,0:T(8,128)(2,1)S(1)} collective-permute-done((bf16[320,1280]{1,0:T(8,128)(2,1)S(1)}, bf16[320,1280]{1,0:T(8,128)(2,1)S(1)}, u32[]{:S(2)}, u32[]{:S(2)}) %collective-permute-start.57) | collective-permute-done | bytes 819232 | tf_op jit(solution)/shard_map/ppermute | solution.py:221
  886.7 11.9 %collective-permute-done.43 = bf16[320,1280]{1,0:T(8,128)(2,1)S(1)} collective-permute-done((bf16[320,1280]{1,0:T(8,128)(2,1)S(1)}, bf16[320,1280]{1,0:T(8,128)(2,1)S(1)}, u32[]{:S(2)}, u32[]{:S(2)}) %collective-permute-start.43) | collective-permute-done | bytes 819232 | tf_op jit(solution)/shard_map/ppermute | solution.py:221
  898.8 7.7 collective-permute-done.58
  915.2 21.6 %collective-permute-done.59 = bf16[160,1280]{1,0:T(8,128)(2,1)} collective-permute-done((bf16[160,1280]{1,0:T(8,128)(2,1)S(1)}, bf16[160,1280]{1,0:T(8,128)(2,1)}, u32[]{:S(2)}, u32[]{:S(2)}) %collective-permute-start.59) | collective-permute-done | bytes 409632 | tf_op jit(solution)/shard_map/ppermute | solution.py:221
  938.7 6.6 collective-permute-done.44
  947.0 17.3 %collective-permute-done.45 = bf16[160,1280]{1,0:T(8,128)(2,1)S(1)} collective-permute-done((bf16[160,1280]{1,0:T(8,128)(2,1)S(1)}, bf16[160,1280]{1,0:T(8,128)(2,1)S(1)}, u32[]{:S(2)}, u32[]{:S(2)}) %collective-permute-start.45) | collective-permute-done | bytes 409632 | tf_op jit(solution)/shard_map/ppermute | solution.py:221
  973.0 12.9 %collective-permute-done.46 = bf16[320,1280]{1,0:T(8,128)(2,1)} collective-permute-done((bf16[320,1280]{1,0:T(8,128)(2,1)S(1)}, bf16[320,1280]{1,0:T(8,128)(2,1)}, u32[]{:S(2)}, u32[]{:S(2)}) %collective-permute-start.46) | collective-permute-done | bytes 819232 | tf_op jit(solution)/shard_map/ppermute | solution.py:221
  999.2 20.8 %collective-permute-done.61 = bf16[640,1280]{1,0:T(8,128)(2,1)} collective-permute-done((bf16[640,1280]{1,0:T(8,128)(2,1)}, bf16[640,1280]{1,0:T(8,128)(2,1)}, u32[]{:S(2)}, u32[]{:S(2)}) %collective-permute-start.61) | collective-permute-done | bytes 1638432 | tf_op jit(solution)/shard_map/ppermute | solution.py:221
  1019.9 5.1 convert_bitcast_fusion
  1025.1 8.1 copy.188
  1033.2 5.1 fusion.14
  (316 shorter events, 192.7 us)
Async XLA Ops:
  0.7 34.5 %collective-permute-start = (bf16[1280,320]{0,1:T(8,128)(2,1)}, bf16[1280,320]{0,1:T(8,128)(2,1)}, u32[]{:S(2)}, u32[]{:S(2)}) collective-permute-start(bf16[1280,320]{0,1:T(8,128)(2,1)} %param.16), channel_id=1, source_target_pairs={{0,1},{1,0},{2,3},{3,2},{4,5},{5,4},{6,7},{7,6},{8,9},{9,8},{10,11... | collective-permute-start | bytes 2457608 | tf_op jit(solution)/shard_map/ppermute | solution.py:221
  1.2 56.7 %collective-permute-start.4 = (bf16[1280,320]{0,1:T(8,128)(2,1)}, bf16[1280,320]{0,1:T(8,128)(2,1)}, u32[]{:S(2)}, u32[]{:S(2)}) collective-permute-start(bf16[1280,320]{0,1:T(8,128)(2,1)} %param.16), channel_id=1, source_target_pairs={{0,2},{1,3},{2,0},{3,1},{4,6},{5,7},{6,4},{7,5},{8,10},{9,11},{10,... | collective-permute-start | bytes 2457608 | tf_op jit(solution)/shard_map/ppermute | solution.py:221
  3.8 33.2 %collective-permute-start.1 = (bf16[1280,320]{0,1:T(8,128)(2,1)}, bf16[1280,320]{0,1:T(8,128)(2,1)}, u32[]{:S(2)}, u32[]{:S(2)}) collective-permute-start(bf16[1280,320]{0,1:T(8,128)(2,1)} %param.17), channel_id=1, source_target_pairs={{0,1},{1,0},{2,3},{3,2},{4,5},{5,4},{6,7},{7,6},{8,9},{9,8},{10,11... | collective-permute-start | bytes 2457608 | tf_op jit(solution)/shard_map/ppermute | solution.py:221
  3.9 57.3 %collective-permute-start.6 = (bf16[1280,320]{0,1:T(8,128)(2,1)}, bf16[1280,320]{0,1:T(8,128)(2,1)}, u32[]{:S(2)}, u32[]{:S(2)}) collective-permute-start(bf16[1280,320]{0,1:T(8,128)(2,1)} %param.17), channel_id=1, source_target_pairs={{0,2},{1,3},{2,0},{3,1},{4,6},{5,7},{6,4},{7,5},{8,10},{9,11},{10,... | collective-permute-start | bytes 2457608 | tf_op jit(solution)/shard_map/ppermute | solution.py:221
  4.2 42.4 %collective-permute-start.2 = (bf16[1280,320]{0,1:T(8,128)(2,1)}, bf16[1280,320]{0,1:T(8,128)(2,1)}, u32[]{:S(2)}, u32[]{:S(2)}) collective-permute-start(bf16[1280,320]{0,1:T(8,128)(2,1)} %param.18), channel_id=1, source_target_pairs={{0,1},{1,0},{2,3},{3,2},{4,5},{5,4},{6,7},{7,6},{8,9},{9,8},{10,11... | collective-permute-start | bytes 2457608 | tf_op jit(solution)/shard_map/ppermute | solution.py:221
  35.2 27.9 %collective-permute-start.8 = (bf16[1280,320]{0,1:T(8,128)(2,1)}, bf16[1280,320]{0,1:T(8,128)(2,1)}, u32[]{:S(2)}, u32[]{:S(2)}) collective-permute-start(bf16[1280,320]{0,1:T(8,128)(2,1)} %param.18), channel_id=1, source_target_pairs={{0,2},{1,3},{2,0},{3,1},{4,6},{5,7},{6,4},{7,5},{8,10},{9,11},{10,... | collective-permute-start | bytes 2457608 | tf_op jit(solution)/shard_map/ppermute | solution.py:221
  37.0 38.9 %collective-permute-start.10 = (bf16[320,1280]{1,0:T(8,128)(2,1)}, bf16[320,1280]{1,0:T(8,128)(2,1)}, u32[]{:S(2)}, u32[]{:S(2)}) collective-permute-start(bf16[320,1280]{1,0:T(8,128)(2,1)} %param.19), channel_id=1, source_target_pairs={{0,2},{1,3},{2,0},{3,1},{4,6},{5,7},{6,4},{7,5},{8,10},{9,11},{10,... | collective-permute-start | bytes 2457608 | tf_op jit(solution)/shard_map/ppermute | solution.py:221
  46.7 54.3 %collective-permute-start.3 = (bf16[320,1280]{1,0:T(8,128)(2,1)}, bf16[320,1280]{1,0:T(8,128)(2,1)}, u32[]{:S(2)}, u32[]{:S(2)}) collective-permute-start(bf16[320,1280]{1,0:T(8,128)(2,1)} %param.19), channel_id=1, source_target_pairs={{0,1},{1,0},{2,3},{3,2},{4,5},{5,4},{6,7},{7,6},{8,9},{9,8},{10,11... | collective-permute-start | bytes 2457608 | tf_op jit(solution)/shard_map/ppermute | solution.py:221
  57.9 168.2 %collective-permute-start.15 = (bf16[1280,1280]{1,0:T(8,128)(2,1)}, bf16[1280,1280]{1,0:T(8,128)(2,1)}, u32[]{:S(2)}, u32[]{:S(2)}) collective-permute-start(bf16[1280,1280]{1,0:T(8,128)(2,1)} %wua.1), channel_id=1, source_target_pairs={{0,2},{1,3},{2,0},{3,1},{4,6},{5,7},{6,4},{7,5},{8,10},{9,11},{10,... | collective-permute-start | bytes 9830408 | tf_op jit(solution)/shard_map/ppermute | solution.py:221
  61.2 165.4 %collective-permute-start.12 = (bf16[1280,1280]{1,0:T(8,128)(2,1)}, bf16[1280,1280]{1,0:T(8,128)(2,1)}, u32[]{:S(2)}, u32[]{:S(2)}) collective-permute-start(bf16[1280,1280]{1,0:T(8,128)(2,1)} %wua.1), channel_id=1, source_target_pairs={{0,1},{1,0},{2,3},{3,2},{4,5},{5,4},{6,7},{7,6},{8,9},{9,8},{10,11... | collective-permute-start | bytes 9830408 | tf_op jit(solution)/shard_map/ppermute | solution.py:221
  63.1 49.1 %collective-permute-start.5 = (bf16[1280,320]{0,1:T(8,128)(2,1)}, bf16[1280,320]{0,1:T(8,128)(2,1)}, u32[]{:S(2)}, u32[]{:S(2)}) collective-permute-start(bf16[1280,320]{0,1:T(8,128)(2,1)} %collective-permute-done.4), channel_id=1, source_target_pairs={{0,1},{1,0},{2,3},{3,2},{4,5},{5,4},{6,7},{7,6},{8,9},{9,8},{10,11... | collective-permute-start | bytes 2457608 | tf_op jit(solution)/shard_map/ppermute | solution.py:221
  75.9 40.4 %collective-permute-start.7 = (bf16[1280,320]{0,1:T(8,128)(2,1)}, bf16[1280,320]{0,1:T(8,128)(2,1)}, u32[]{:S(2)}, u32[]{:S(2)}) collective-permute-start(bf16[1280,320]{0,1:T(8,128)(2,1)} %collective-permute-done.6), channel_id=1, source_target_pairs={{0,1},{1,0},{2,3},{3,2},{4,5},{5,4},{6,7},{7,6},{8,9},{9,8},{10,11... | collective-permute-start | bytes 2457608 | tf_op jit(solution)/shard_map/ppermute | solution.py:221
  112.1 114.1 %collective-permute-start.17 = (bf16[1280,1280]{1,0:T(8,128)(2,1)}, bf16[1280,1280]{1,0:T(8,128)(2,1)}, u32[]{:S(2)}, u32[]{:S(2)}) collective-permute-start(bf16[1280,1280]{1,0:T(8,128)(2,1)} %wda.1), channel_id=1, source_target_pairs={{0,2},{1,3},{2,0},{3,1},{4,6},{5,7},{6,4},{7,5},{8,10},{9,11},{10,... | collective-permute-start | bytes 9830408 | tf_op jit(solution)/shard_map/ppermute | solution.py:221
  116.3 110.3 %collective-permute-start.13 = (bf16[1280,1280]{1,0:T(8,128)(2,1)}, bf16[1280,1280]{1,0:T(8,128)(2,1)}, u32[]{:S(2)}, u32[]{:S(2)}) collective-permute-start(bf16[1280,1280]{1,0:T(8,128)(2,1)} %wda.1), channel_id=1, source_target_pairs={{0,1},{1,0},{2,3},{3,2},{4,5},{5,4},{6,7},{7,6},{8,9},{9,8},{10,11... | collective-permute-start | bytes 9830408 | tf_op jit(solution)/shard_map/ppermute | solution.py:221
  118.5 34.7 %collective-permute-start.11 = (bf16[320,1280]{1,0:T(8,128)(2,1)}, bf16[320,1280]{1,0:T(8,128)(2,1)}, u32[]{:S(2)}, u32[]{:S(2)}) collective-permute-start(bf16[320,1280]{1,0:T(8,128)(2,1)} %collective-permute-done.10), channel_id=1, source_target_pairs={{0,1},{1,0},{2,3},{3,2},{4,5},{5,4},{6,7},{7,6},{8,9},{9,8},{10,11... | collective-permute-start | bytes 2457608 | tf_op jit(solution)/shard_map/ppermute | solution.py:221
  153.3 62.8 %collective-permute-start.19 = (bf16[1,1280]{1,0:T(2,128)(2,1)S(1)}, bf16[1,1280]{1,0:T(2,128)(2,1)S(1)}, u32[]{:S(2)}, u32[]{:S(2)}) collective-permute-start(bf16[1,1280]{1,0:T(2,128)(2,1)S(1)} %reshape.146.hba), channel_id=1, source_target_pairs={{0,2},{1,3},{2,0},{3,1},{4,6},{5,7},{6,4},{7,5},{8,10},{9,11},{10,... | collective-permute-start | bytes 7688 | tf_op jit(solution)/shard_map/ppermute | solution.py:221
  225.6 84.5 %collective-permute-start.20 = (bf16[1,1280]{1,0:T(2,128)(2,1)S(1)}, bf16[1,1280]{1,0:T(2,128)(2,1)S(1)}, u32[]{:S(2)}, u32[]{:S(2)}) collective-permute-start(bf16[1,1280]{1,0:T(2,128)(2,1)S(1)} %collective-permute-done.19.hba), channel_id=1, source_target_pairs={{0,1},{1,0},{2,3},{3,2},{4,5},{5,4},{6,7},{7,6},{8,9},{9,8},{10,11... | collective-permute-start | bytes 7688 | tf_op jit(solution)/shard_map/ppermute | solution.py:221
  226.1 83.9 %collective-permute-start.16 = (bf16[1280,1280]{1,0:T(8,128)(2,1)}, bf16[1280,1280]{1,0:T(8,128)(2,1)}, u32[]{:S(2)}, u32[]{:S(2)}) collective-permute-start(bf16[1280,1280]{1,0:T(8,128)(2,1)} %collective-permute-done.15.wua), channel_id=1, source_target_pairs={{0,1},{1,0},{2,3},{3,2},{4,5},{5,4},{6,7},{7,6},{8,9},{9,8},{10,11... | collective-permute-start | bytes 9830408 | tf_op jit(solution)/shard_map/ppermute | solution.py:221
  226.2 83.8 %collective-permute-start.18 = (bf16[1280,1280]{1,0:T(8,128)(2,1)}, bf16[1280,1280]{1,0:T(8,128)(2,1)}, u32[]{:S(2)}, u32[]{:S(2)}) collective-permute-start(bf16[1280,1280]{1,0:T(8,128)(2,1)} %collective-permute-done.17.wda), channel_id=1, source_target_pairs={{0,1},{1,0},{2,3},{3,2},{4,5},{5,4},{6,7},{7,6},{8,9},{9,8},{10,11... | collective-permute-start | bytes 9830408 | tf_op jit(solution)/shard_map/ppermute | solution.py:221
  471.0 95.3 %collective-permute-start.22 = (bf16[1280,960]{0,1:T(8,128)(2,1)}, bf16[1280,960]{0,1:T(8,128)(2,1)}, u32[]{:S(2)}, u32[]{:S(2)}) collective-permute-start(bf16[1280,960]{0,1:T(8,128)(2,1)} %copy.176), channel_id=1, source_target_pairs={{0,1},{1,0},{2,3},{3,2},{4,5},{5,4},{6,7},{7,6},{8,9},{9,8},{10,11... | collective-permute-start | bytes 7372808 | tf_op jit(solution)/shard_map/ppermute | solution.py:221
  532.3 138.5 %collective-permute-start.21 = (bf16[1280,960]{0,1:T(8,128)(2,1)}, bf16[1280,960]{0,1:T(8,128)(2,1)}, u32[]{:S(2)}, u32[]{:S(2)}) collective-permute-start(bf16[1280,960]{0,1:T(8,128)(2,1)} %copy.174), channel_id=1, source_target_pairs={{0,1},{1,0},{2,3},{3,2},{4,5},{5,4},{6,7},{7,6},{8,9},{9,8},{10,11... | collective-permute-start | bytes 7372808 | tf_op jit(solution)/shard_map/ppermute | solution.py:221
  535.5 28.6 %collective-permute-start.30 = (bf16[320,1280]{1,0:T(8,128)(2,1)S(1)}, bf16[320,1280]{1,0:T(8,128)(2,1)S(1)}, u32[]{:S(2)}, u32[]{:S(2)}) collective-permute-start(bf16[320,1280]{1,0:T(8,128)(2,1)S(1)} %slice.88), channel_id=1, source_target_pairs={{0,1},{1,0},{2,3},{3,2},{4,5},{5,4},{6,7},{7,6},{8,9},{9,8},{10,11... | collective-permute-start | bytes 2457608 | tf_op jit(solution)/shard_map/ppermute | solution.py:221
  536.0 139.2 %collective-permute-start.54 = (bf16[1280,1280]{1,0:T(8,128)(2,1)}, bf16[1280,1280]{1,0:T(8,128)(2,1)}, u32[]{:S(2)}, u32[]{:S(2)}) collective-permute-start(bf16[1280,1280]{1,0:T(8,128)(2,1)} %get-tuple-element.68), channel_id=1, source_target_pairs={{0,1},{1,0},{2,3},{3,2},{4,5},{5,4},{6,7},{7,6},{8,9},{9,8},{10,11... | collective-permute-start | bytes 9830408 | tf_op jit(solution)/shard_map/ppermute | solution.py:221
  567.1 100.1 %collective-permute-start.33 = (bf16[160,1280]{1,0:T(8,128)(2,1)S(1)}, bf16[160,1280]{1,0:T(8,128)(2,1)S(1)}, u32[]{:S(2)}, u32[]{:S(2)}) collective-permute-start(bf16[160,1280]{1,0:T(8,128)(2,1)S(1)} %constant_dynamic-slice_fusion.7), channel_id=1, source_target_pairs={{0,8},{4,12},{8,0},{12,4},{16,24},{20,28},{24,16},{28,20},{1,9},{5... | collective-permute-start | bytes 1228808 | tf_op jit(solution)/shard_map/ppermute | solution.py:221
  580.9 100.5 %collective-permute-start.23 = (bf16[1280,960]{0,1:T(8,128)(2,1)}, bf16[1280,960]{0,1:T(8,128)(2,1)}, u32[]{:S(2)}, u32[]{:S(2)}) collective-permute-start(bf16[1280,960]{0,1:T(8,128)(2,1)} %copy.178), channel_id=1, source_target_pairs={{0,2},{1,3},{2,0},{3,1},{4,6},{5,7},{6,4},{7,5},{8,10},{9,11},{10,... | collective-permute-start | bytes 7372808 | tf_op jit(solution)/shard_map/ppermute | solution.py:221
  582.4 54.4 %collective-permute-start.63 = (f32[1280]{0:T(1024)S(1)}, f32[1280]{0:T(1024)S(1)}, u32[]{:S(2)}, u32[]{:S(2)}) collective-permute-start(f32[1280]{0:T(1024)S(1)} %add.356), channel_id=1, source_target_pairs={{0,2},{1,3},{2,0},{3,1},{4,6},{5,7},{6,4},{7,5},{8,10},{9,11},{10,... | collective-permute-start | bytes 15368 | tf_op jit(solution)/shard_map/ppermute | solution.py:221
  665.4 30.0 %collective-permute-start.40 = (bf16[1280,1280]{1,0:T(8,128)(2,1)}, bf16[1280,1280]{1,0:T(8,128)(2,1)}, u32[]{:S(2)}, u32[]{:S(2)}) collective-permute-start(bf16[1280,1280]{1,0:T(8,128)(2,1)} %get-tuple-element.60), channel_id=1, source_target_pairs={{0,1},{1,0},{2,3},{3,2},{4,5},{5,4},{6,7},{7,6},{8,9},{9,8},{10,11... | collective-permute-start | bytes 9830408 | tf_op jit(solution)/shard_map/ppermute | solution.py:221
  668.0 92.1 %collective-permute-start.39 = (bf16[1280,1280]{1,0:T(8,128)(2,1)}, bf16[1280,1280]{1,0:T(8,128)(2,1)}, u32[]{:S(2)}, u32[]{:S(2)}) collective-permute-start(bf16[1280,1280]{1,0:T(8,128)(2,1)} %get-tuple-element.58), channel_id=1, source_target_pairs={{0,1},{1,0},{2,3},{3,2},{4,5},{5,4},{6,7},{7,6},{8,9},{9,8},{10,11... | collective-permute-start | bytes 9830408 | tf_op jit(solution)/shard_map/ppermute | solution.py:221
  670.8 60.7 %collective-permute-start.53 = (bf16[1280,1280]{1,0:T(8,128)(2,1)}, bf16[1280,1280]{1,0:T(8,128)(2,1)}, u32[]{:S(2)}, u32[]{:S(2)}) collective-permute-start(bf16[1280,1280]{1,0:T(8,128)(2,1)} %get-tuple-element.66), channel_id=1, source_target_pairs={{0,1},{1,0},{2,3},{3,2},{4,5},{5,4},{6,7},{7,6},{8,9},{9,8},{10,11... | collective-permute-start | bytes 9830408 | tf_op jit(solution)/shard_map/ppermute | solution.py:221
  675.3 26.2 %collective-permute-start.34 = (bf16[80,1280]{1,0:T(8,128)(2,1)S(1)}, bf16[80,1280]{1,0:T(8,128)(2,1)}, u32[]{:S(2)}, u32[]{:S(2)}) collective-permute-start(bf16[80,1280]{1,0:T(8,128)(2,1)S(1)} %constant_dynamic-slice_fusion.6), channel_id=1, source_target_pairs={{0,4},{4,0},{8,12},{12,8},{16,20},{20,16},{24,28},{28,24},{1,5},{5... | collective-permute-start | bytes 614408 | tf_op jit(solution)/shard_map/ppermute | solution.py:221
  681.4 74.1 %collective-permute-start.55 = (bf16[1280,1280]{1,0:T(8,128)(2,1)}, bf16[1280,1280]{1,0:T(8,128)(2,1)}, u32[]{:S(2)}, u32[]{:S(2)}) collective-permute-start(bf16[1280,1280]{1,0:T(8,128)(2,1)} %add_convert_fusion.1), channel_id=1, source_target_pairs={{0,2},{1,3},{2,0},{3,1},{4,6},{5,7},{6,4},{7,5},{8,10},{9,11},{10,... | collective-permute-start | bytes 9830408 | tf_op jit(solution)/shard_map/ppermute | solution.py:221
  695.4 29.2 %collective-permute-start.24 = (bf16[640,960]{0,1:T(8,128)(2,1)}, bf16[640,960]{0,1:T(8,128)(2,1)}, u32[]{:S(2)}, u32[]{:S(2)}) collective-permute-start(bf16[640,960]{0,1:T(8,128)(2,1)} %copy.180), channel_id=1, source_target_pairs={{0,4},{4,0},{8,12},{12,8},{16,20},{20,16},{24,28},{28,24},{1,5},{5... | collective-permute-start | bytes 3686408 | tf_op jit(solution)/shard_map/ppermute | solution.py:221
  701.4 123.5 %collective-permute-start.41 = (bf16[1280,1280]{1,0:T(8,128)(2,1)}, bf16[1280,1280]{1,0:T(8,128)(2,1)}, u32[]{:S(2)}, u32[]{:S(2)}) collective-permute-start(bf16[1280,1280]{1,0:T(8,128)(2,1)} %add_convert_fusion.4), channel_id=1, source_target_pairs={{0,2},{1,3},{2,0},{3,1},{4,6},{5,7},{6,4},{7,5},{8,10},{9,11},{10,... | collective-permute-start | bytes 9830408 | tf_op jit(solution)/shard_map/ppermute | solution.py:221
  724.6 108.0 %collective-permute-start.35 = (bf16[40,1280]{1,0:T(8,128)(2,1)S(1)}, bf16[40,1280]{1,0:T(8,128)(2,1)S(1)}, u32[]{:S(2)}, u32[]{:S(2)}) collective-permute-start(bf16[40,1280]{1,0:T(8,128)(2,1)S(1)} %constant_dynamic-slice_fusion.5), channel_id=1, source_target_pairs={{0,16},{4,20},{8,24},{12,28},{16,0},{20,4},{24,8},{28,12},{1,17},{... | collective-permute-start | bytes 307208 | tf_op jit(solution)/shard_map/ppermute | solution.py:221
  731.4 98.3 %collective-permute-start.25 = (bf16[320,960]{1,0:T(8,128)(2,1)S(1)}, bf16[320,960]{1,0:T(8,128)(2,1)S(1)}, u32[]{:S(2)}, u32[]{:S(2)}) collective-permute-start(bf16[320,960]{1,0:T(8,128)(2,1)S(1)} %constant_dynamic-slice_fusion.9), channel_id=1, source_target_pairs={{0,8},{4,12},{8,0},{12,4},{16,24},{20,28},{24,16},{28,20},{1,9},{5... | collective-permute-start | bytes 1843208 | tf_op jit(solution)/shard_map/ppermute | solution.py:221
  759.8 89.1 %collective-permute-start.56 = (bf16[640,1280]{1,0:T(8,128)(2,1)S(1)}, bf16[640,1280]{1,0:T(8,128)(2,1)S(1)}, u32[]{:S(2)}, u32[]{:S(2)}) collective-permute-start(bf16[640,1280]{1,0:T(8,128)(2,1)S(1)} %constant_dynamic-slice_fusion.1), channel_id=1, source_target_pairs={{0,8},{4,12},{8,0},{12,4},{16,24},{20,28},{24,16},{28,20},{1,9},{5... | collective-permute-start | bytes 4915208 | tf_op jit(solution)/shard_map/ppermute | solution.py:221
  829.3 38.8 %collective-permute-start.42 = (bf16[640,1280]{1,0:T(8,128)(2,1)S(1)}, bf16[640,1280]{1,0:T(8,128)(2,1)S(1)}, u32[]{:S(2)}, u32[]{:S(2)}) collective-permute-start(bf16[640,1280]{1,0:T(8,128)(2,1)S(1)} %constant_dynamic-slice_fusion.4), channel_id=1, source_target_pairs={{0,4},{4,0},{8,12},{12,8},{16,20},{20,16},{24,28},{28,24},{1,5},{5... | collective-permute-start | bytes 4915208 | tf_op jit(solution)/shard_map/ppermute | solution.py:221
  832.6 78.4 %collective-permute-start.36 = (bf16[40,1280]{1,0:T(8,128)(2,1)S(1)}, bf16[40,1280]{1,0:T(8,128)(2,1)S(1)}, u32[]{:S(2)}, u32[]{:S(2)}) collective-permute-start(bf16[40,1280]{1,0:T(8,128)(2,1)S(1)} %add_convert_fusion.23), channel_id=1, source_target_pairs={{0,16},{4,20},{8,24},{12,28},{16,0},{20,4},{24,8},{28,12},{1,17},{... | collective-permute-start | bytes 307208 | tf_op jit(solution)/shard_map/ppermute | solution.py:221
  849.5 34.5 %collective-permute-start.57 = (bf16[320,1280]{1,0:T(8,128)(2,1)S(1)}, bf16[320,1280]{1,0:T(8,128)(2,1)S(1)}, u32[]{:S(2)}, u32[]{:S(2)}) collective-permute-start(bf16[320,1280]{1,0:T(8,128)(2,1)S(1)} %constant_dynamic-slice_fusion), channel_id=1, source_target_pairs={{0,4},{4,0},{8,12},{12,8},{16,20},{20,16},{24,28},{28,24},{1,5},{5... | collective-permute-start | bytes 2457608 | tf_op jit(solution)/shard_map/ppermute | solution.py:221
  868.6 30.0 %collective-permute-start.43 = (bf16[320,1280]{1,0:T(8,128)(2,1)S(1)}, bf16[320,1280]{1,0:T(8,128)(2,1)S(1)}, u32[]{:S(2)}, u32[]{:S(2)}) collective-permute-start(bf16[320,1280]{1,0:T(8,128)(2,1)S(1)} %constant_dynamic-slice_fusion.3), channel_id=1, source_target_pairs={{0,8},{4,12},{8,0},{12,4},{16,24},{20,28},{24,16},{28,20},{1,9},{5... | collective-permute-start | bytes 2457608 | tf_op jit(solution)/shard_map/ppermute | solution.py:221
  869.1 42.4 %collective-permute-start.28 = (bf16[320,960]{1,0:T(8,128)(2,1)S(1)}, bf16[320,960]{1,0:T(8,128)(2,1)S(1)}, u32[]{:S(2)}, u32[]{:S(2)}) collective-permute-start(bf16[320,960]{1,0:T(8,128)(2,1)S(1)} %maximum_select_fusion.9), channel_id=1, source_target_pairs={{0,8},{4,12},{8,0},{12,4},{16,24},{20,28},{24,16},{28,20},{1,9},{5... | collective-permute-start | bytes 1843208 | tf_op jit(solution)/shard_map/ppermute | solution.py:221
  906.7 30.1 %collective-permute-start.59 = (bf16[160,1280]{1,0:T(8,128)(2,1)S(1)}, bf16[160,1280]{1,0:T(8,128)(2,1)}, u32[]{:S(2)}, u32[]{:S(2)}) collective-permute-start(bf16[160,1280]{1,0:T(8,128)(2,1)S(1)} %add_convert_fusion.18), channel_id=1, source_target_pairs={{0,16},{4,20},{8,24},{12,28},{16,0},{20,4},{24,8},{28,12},{1,17},{... | collective-permute-start | bytes 1228808 | tf_op jit(solution)/shard_map/ppermute | solution.py:221
  911.0 34.4 %collective-permute-start.44 = (bf16[160,1280]{1,0:T(8,128)(2,1)}, bf16[160,1280]{1,0:T(8,128)(2,1)S(1)}, u32[]{:S(2)}, u32[]{:S(2)}) collective-permute-start(bf16[160,1280]{1,0:T(8,128)(2,1)} %constant_dynamic-slice_fusion.2), channel_id=1, source_target_pairs={{0,16},{4,20},{8,24},{12,28},{16,0},{20,4},{24,8},{28,12},{1,17},{... | collective-permute-start | bytes 1228808 | tf_op jit(solution)/shard_map/ppermute | solution.py:221
  911.1 35.0 %collective-permute-start.37 = (bf16[80,1280]{1,0:T(8,128)(2,1)S(1)}, bf16[80,1280]{1,0:T(8,128)(2,1)S(1)}, u32[]{:S(2)}, u32[]{:S(2)}) collective-permute-start(bf16[80,1280]{1,0:T(8,128)(2,1)S(1)} %maximum_select_fusion.11), channel_id=1, source_target_pairs={{0,4},{4,0},{8,12},{12,8},{16,20},{20,16},{24,28},{28,24},{1,5},{5... | collective-permute-start | bytes 614408 | tf_op jit(solution)/shard_map/ppermute | solution.py:221
  913.5 56.2 %collective-permute-start.29 = (bf16[640,960]{0,1:T(8,128)(2,1)}, bf16[640,960]{0,1:T(8,128)(2,1)}, u32[]{:S(2)}, u32[]{:S(2)}) collective-permute-start(bf16[640,960]{0,1:T(8,128)(2,1)} %copy.182), channel_id=1, source_target_pairs={{0,4},{4,0},{8,12},{12,8},{16,20},{20,16},{24,28},{28,24},{1,5},{5... | collective-permute-start | bytes 3686408 | tf_op jit(solution)/shard_map/ppermute | solution.py:221
  938.1 26.5 %collective-permute-start.60 = (bf16[320,1280]{1,0:T(8,128)(2,1)S(1)}, bf16[320,1280]{1,0:T(8,128)(2,1)S(1)}, u32[]{:S(2)}, u32[]{:S(2)}) collective-permute-start(bf16[320,1280]{1,0:T(8,128)(2,1)S(1)} %maximum_select_fusion.8), channel_id=1, source_target_pairs={{0,4},{4,0},{8,12},{12,8},{16,20},{20,16},{24,28},{28,24},{1,5},{5... | collective-permute-start | bytes 2457608 | tf_op jit(solution)/shard_map/ppermute | solution.py:221
  966.4 53.5 %collective-permute-start.61 = (bf16[640,1280]{1,0:T(8,128)(2,1)}, bf16[640,1280]{1,0:T(8,128)(2,1)}, u32[]{:S(2)}, u32[]{:S(2)}) collective-permute-start(bf16[640,1280]{1,0:T(8,128)(2,1)} %maximum_select_fusion.4), channel_id=1, source_target_pairs={{0,8},{4,12},{8,0},{12,4},{16,24},{20,28},{24,16},{28,20},{1,9},{5... | collective-permute-start | bytes 4915208 | tf_op jit(solution)/shard_map/ppermute | solution.py:221
  988.9 44.3 %collective-permute-start.47 = (bf16[640,1280]{1,0:T(8,128)(2,1)}, bf16[640,1280]{1,0:T(8,128)(2,1)}, u32[]{:S(2)}, u32[]{:S(2)}) collective-permute-start(bf16[640,1280]{1,0:T(8,128)(2,1)} %maximum_select_fusion.3), channel_id=1, source_target_pairs={{0,4},{4,0},{8,12},{12,8},{16,20},{20,16},{24,28},{28,24},{1,5},{5... | collective-permute-start | bytes 4915208 | tf_op jit(solution)/shard_map/ppermute | solution.py:221
  (60 other events, 1163.0 us)

commit v2 on v0

v2 whole, which is shorter than its diff:
```python
import functools
import math

import jax
import jax.numpy as jnp
from jax import lax
from jax.experimental import pallas as pl
from jax.experimental.pallas import tpu as pltpu
from jax.sharding import PartitionSpec as P

HD = 80
L = 64
SLOTS = 32
LANES = 128
EPSILON = 1e-06
MASKED = -1e30
F32 = jnp.float32
BF = jnp.bfloat16
NN = (((1,), (0,)), ((), ()))
NT = (((1,), (1,)), ((), ()))
TN = (((0,), (0,)), ((), ()))
VMEM_BYTES = 60 << 20


def dot(a, b, dims=NN):
    return lax.dot_general(a, b, dims, preferred_element_type=F32)


def pick(n, *sizes):
    return next((s for s in sizes if n % s == 0), n)


def whole(shape):
    return pl.BlockSpec(shape, lambda *i: (0,) * len(shape), pipeline_mode=pl.Buffered(1))


def cost(flops, nbytes, exps=0):
    return pl.CostEstimate(flops=int(flops), bytes_accessed=int(nbytes), transcendentals=int(exps))


def row_sum(x):
    return jnp.sum(x, axis=0, keepdims=True)


def rms(x):
    return lax.rsqrt(jnp.mean(x * x, axis=1, keepdims=True) + EPSILON)


MESH = pl.DeviceIdType.MESH
CORE, Y = ("mp", 1), ("mp", 2)


def bit_of(axis, bit):
    return lax.rem(lax.axis_index(axis) // bit, 2)


def flip(axis, bit):
    return {axis: lax.axis_index(axis) + bit - 2 * bit * bit_of(axis, bit)}


class Traffic:
    def __init__(self, number, partners, arrays, buffers):
        self.number, self.partners = number, partners
        self.arrays, self.buffers = arrays, buffers
        self.events, self.slots, self.refs = [], {}, {}

    def on(self, step, place, *actions):
        self.events += [(step, place, f) for f in actions]
        return self

    def run(self, step, place):
        for at, where, action in self.events:
            if where == place:
                pl.when(step == at)(functools.partial(action, self))

    def greet(self):
        sem = pltpu.get_barrier_semaphore()
        for p in self.partners:
            pl.semaphore_signal(sem, inc=1, device_id=flip(*p), device_id_type=MESH)
        pl.semaphore_wait(sem, len(self.partners))

    def copy(self, name, src, dst, to):
        i = self.slots.setdefault(name, len(self.slots))
        return pltpu.make_async_remote_copy(
            src_ref=src,
            dst_ref=dst,
            send_sem=self.sems.at[0, i],
            recv_sem=self.sems.at[1, i],
            device_id=flip(*to),
            device_id_type=MESH,
        )

    def local(self, name, src, dst):
        i = self.slots.setdefault(name, len(self.slots))
        return pltpu.make_async_copy(src, dst, self.sems.at[0, i])


COPIES = 40


def launch(body, name, grid, args, in_specs, outs, out_specs, scratch, cost_estimate, traffic=None):
    n_args, n_outs = len(args), len(outs)
    names, arrays, buffers = [], [], []
    if traffic is not None:
        names = [*traffic.arrays, *traffic.buffers]
        arrays = list(traffic.arrays.values())
        buffers = [jax.ShapeDtypeStruct(s, BF) for s in traffic.buffers.values()]
        scratch = [*scratch, pltpu.SemaphoreType.DMA((2, COPIES))]

    def kernel(*refs):
        hook = lambda place: None
        inputs, refs = refs[:n_args], refs[n_args:]
        moved, refs = refs[: len(arrays)], refs[len(arrays) :]
        results, refs = refs[:n_outs], refs[n_outs:]
        landing, refs = refs[: len(buffers)], refs[len(buffers) :]
        if traffic is not None:
            step = pl.program_id(0)
            for d in range(1, len(grid)):
                step = step * grid[d] + pl.program_id(d)
            traffic.refs = dict(zip(names, [*moved, *landing]))
            traffic.sems, refs = refs[-1], refs[:-1]
            if traffic.partners:
                pl.when(step == 0)(traffic.greet)
            hook = lambda place: traffic.run(step, place)
        body(hook, *inputs, *results, *refs)

    anywhere = pl.BlockSpec(memory_space=pl.ANY)
    out = pl.pallas_call(
        kernel,
        grid=grid,
        in_specs=[*in_specs, *[anywhere] * len(arrays)],
        out_specs=[*out_specs, *[anywhere] * len(buffers)],
        out_shape=[*outs, *buffers],
        scratch_shapes=scratch,
        compiler_params=pltpu.CompilerParams(
            vmem_limit_bytes=VMEM_BYTES,
            **({} if traffic is None or not traffic.partners else dict(collective_id=traffic.number, has_side_effects=True)),
        ),
        cost_estimate=cost_estimate,
        name=name,
    )(*args, *arrays)
    return out[:n_outs], dict(zip(names[len(arrays) :], out[n_outs:]))


def add_rows(sources, target, rows):
    columns = target.shape[1]
    tile = pl.BlockSpec((pick(rows, 80, 64, 16), columns), lambda i: (i, 0))

    def body(*refs):
        refs[-1][...] = sum(r[...].astype(F32) for r in refs[:-1]).astype(BF)

    pltpu.emit_pipeline(
        body, grid=(rows // tile.block_shape[0],), in_specs=[tile] * len(sources), out_specs=[tile]
    )(*[r.at[pl.ds(pl.multiple_of(o, 16), rows), :] for r, o in sources], target)


class Stream:
    def __init__(self, tag, mine, theirs, rows, columns, order, base=0):
        self.tag, self.mine, self.theirs, self.base = tag, mine, theirs, base
        self.rows, self.columns, self.order = rows, columns, order

    def name(self, what):
        return self.tag + what

    def buffers(self, *what):
        size = lambda w: self.rows if w[0] in "cf" else self.rows >> len(self.order) if w[0] in "ey" else self.rows >> (int(w[1]) + 1)
        return {self.name(w): (size(w), self.columns) for w in what}

    def place(self, stages):
        first, n = 0, self.rows
        for bit in self.order[:stages]:
            n //= 2
            first = first + bit_of("dp", bit) * n
        return first, n

    def sources(self, t, first, arrived):
        out = [(t.refs[self.mine], first + self.base), (t.refs[self.name("c")], first)]
        for j in range(arrived):
            out.append((t.refs[self.name(f"r{j}")], first - self.place(j + 1)[0]))
        return out

    def core(self, t):
        src = t.refs[self.theirs].at[pl.ds(self.base, self.rows), :]
        return t.copy(self.name("c"), src, t.refs[self.name("c")], CORE)

    def start_core(self, t):
        self.core(t).start()

    def wait_core(self, t):
        self.core(t).wait()

    def exchange(self, t, j):
        return t.copy(self.name(f"r{j}"), t.refs[self.name(f"s{j}")], t.refs[self.name(f"r{j}")], ("dp", self.order[j]))

    def start(self, j):
        def action(t):
            first, n = self.place(j)
            n //= 2
            sent = first + (1 - bit_of("dp", self.order[j])) * n
            add_rows(self.sources(t, sent, j), t.refs[self.name(f"s{j}")], n)
            self.exchange(t, j).start()

        return action

    def wait(self, j):
        return lambda t: self.exchange(t, j).wait()

    def keep(self, t):
        first, n = self.place(len(self.order))
        add_rows(self.sources(t, first, len(self.order)), t.refs[self.name("e")], n)

    def cross(self, t):
        return t.copy(self.name("y"), t.refs[self.name("e")], t.refs[self.name("y")], Y)

    def start_cross(self, t):
        self.cross(t).start()

    def wait_cross(self, t):
        self.cross(t).wait()

    def total(self, other):
        def action(t):
            first, n = self.place(len(self.order))
            target = t.refs[self.name("f")].at[pl.ds(pl.multiple_of(first, 16), n), :]
            add_rows([(t.refs[self.name("e")], 0), (t.refs[other.name("y")], 0)], target, n)

        return action

    def spread(self, t, j):
        first, n = self.place(j + 1)
        part = t.refs[self.name("f")].at[pl.ds(pl.multiple_of(first, 16), n), :]
        return t.copy(self.name(f"f{j}"), part, part, ("dp", self.order[j]))

    def start_spread(self, j):
        return lambda t: self.spread(t, j).start()

    def wait_spread(self, j):
        return lambda t: self.spread(t, j).wait()


class Gather:
    def __init__(self, tag, rows, columns):
        self.tag, self.rows, self.columns = tag, rows, columns
        self.n = rows // 4

    def buffers(self, *what):
        return {self.tag + w: (self.n if w == "q" else self.rows, self.columns) for w in what}

    def quarter(self, ref, flip_x=0, flip_z=0, first=0, rows=None):
        x, z = bit_of("dp", 1), bit_of("dp", 2)
        x, z = (1 - x if flip_x else x), (1 - z if flip_z else z)
        start = pl.multiple_of((2 * z + x) * self.n + first, 16)
        return ref.at[pl.ds(start, self.n if rows is None else rows), :]

    def copies(self, t, step):
        own, o = t.refs[self.tag], t.refs.get(self.tag + "o")
        name = self.tag + step
        if step == "s":
            return [t.copy(name, own, t.refs[name], CORE)]
        if step == "y":
            return [t.copy(name, self.quarter(own), t.refs[self.tag + "q"], Y)]
        if step == "a":
            q = t.refs[self.tag + "q"]
            return [t.copy(name + str(b), q, self.quarter(o), ("dp", b)) for b in (1, 2)] + [
                t.local(name + "l", q, self.quarter(o))
            ]
        if step == "b":
            top = (self.n // 2 + 15) // 16 * 16
            to_x = self.quarter(o, flip_z=1, rows=top)
            to_z = self.quarter(o, flip_x=1, first=top, rows=self.n - top)
            return [t.copy(name + "1", to_x, to_x, ("dp", 1)), t.copy(name + "2", to_z, to_z, ("dp", 2))]
        return [t.copy(name, o, t.refs[self.tag + "p"], CORE)]

    def start(self, step):
        def action(t):
            for c in self.copies(t, step):
                c.start()

        return action

    def wait(self, step):
        def action(t):
            for c in self.copies(t, step):
                c.wait()

        return action


def windows(C):
    out = []
    for h in range(C // HD):
        w = min(LANES * (HD * h // LANES), C - 2 * LANES)
        out.append((w, HD * h - w))
    return out


def head_masks(C):
    lane = lax.broadcasted_iota(jnp.int32, (1, 2 * LANES), 1)
    return [jnp.where((lane >= lo) & (lane < lo + HD), 1.0, 0.0).astype(BF) for _, lo in windows(C)]


def softmaxes(qs, ks, allowed):
    s = [jnp.where(allowed, dot(q, k, NT) * (1.0 / math.sqrt(HD)), MASKED) for q, k in zip(qs, ks)]
    e = [jnp.exp(x - jnp.max(x, axis=1, keepdims=True)) for x in s]
    return [x * (1.0 / jnp.sum(x, axis=1, keepdims=True)) for x in e]


def allow(idc, idr, s, B):
    causal = lax.broadcasted_iota(jnp.int32, (B, B), 1) <= lax.broadcasted_iota(
        jnp.int32, (B, B), 0
    )
    return (idc[s, :] == idr[:, s]) & causal


def put(tiles, w, val):
    for n in range(2):
        t = w // LANES + n
        part = val[:, n * LANES : (n + 1) * LANES]
        tiles[t] = part if tiles[t] is None else tiles[t] + part


def fwd_body(B, C, pairs, traffic, hook, x, gain, idc, idr, qkv, mixed, w, n1, ab, sem):
    group = pl.program_id(0)
    tt = x.shape[0]
    first = pl.program_id(1) == 0
    hook("start")
    h = C // 2
    for g, pair in enumerate(pairs):

        @pl.when(first & (group == g))
        def _():
            for side in range(2):
                c = pltpu.make_async_copy(traffic.refs[pair[side]], ab, sem)
                c.start()
                c.wait()
                a = ab[...]
                for i in range(3):
                    w[0, :, i * C + side * h : i * C + (side + 1) * h] = a[:, i * h : (i + 1) * h]

    t = x[...].astype(F32)
    normed = (t * rms(t) * gain[...].astype(F32)).astype(BF)

    @pl.when(group == 0)
    def _():
        n1[...] = normed

    qkv[0] = dot(normed, w[0]).astype(BF)
    hook("middle")
    masks = head_masks(C)
    wins = [w0 for w0, _ in windows(C)]

    def block(i, _):
        s = pl.ds(pl.multiple_of(i * B, B), B)
        ok = allow(idc, idr, s, B)
        tiles = [None] * (C // LANES)
        cut = lambda n, w0: qkv[0, s, n * C + w0 : n * C + w0 + 2 * LANES]
        for g in range(0, len(wins), 8):
            hs = range(g, min(g + 8, len(wins)))
            p = softmaxes([cut(0, wins[h]) * masks[h] for h in hs], [cut(1, wins[h]) for h in hs], ok)
            o = [dot(a.astype(BF), cut(2, wins[h]) * masks[h]) for a, h in zip(p, hs)]
            for h, a in zip(hs, o):
                put(tiles, wins[h], a)
        mixed[0, s, :] = jnp.concatenate(tiles, axis=1).astype(BF)
        return 0

    lax.fori_loop(0, tt // B, block, 0)
    hook("end")


def attend(x, gain, idc, idr, h, pairs, traffic):
    T, D = x.shape
    C, G = 2 * h, len(pairs)
    tt, B = pick(T, 512, 384, 256, 128), 128
    by_group = lambda c: pl.BlockSpec((1, tt, c), lambda g, i: (g, i, 0))
    return launch(
        functools.partial(fwd_body, B, C, pairs, traffic),
        "attend",
        (G, T // tt),
        (x, gain, idc, idr),
        [
            pl.BlockSpec((tt, D), lambda g, i: (i, 0)),
            whole((1, D)),
            pl.BlockSpec((tt, 1), lambda g, i: (i, 0)),
            pl.BlockSpec((1, tt), lambda g, i: (0, i)),
        ],
        [
            jax.ShapeDtypeStruct((G, T, 3 * C), BF),
            jax.ShapeDtypeStruct((G, T, C), BF),
            jax.ShapeDtypeStruct((G, D, 3 * C), BF),
            jax.ShapeDtypeStruct((T, D), BF),
        ],
        [
            by_group(3 * C),
            by_group(C),
            pl.BlockSpec((1, D, 3 * C), lambda g, i: (g, 0, 0)),
            pl.BlockSpec((tt, D), lambda g, i: (jnp.where(g == 0, i, T // tt - 1), 0)),
        ],
        [pltpu.VMEM((D, 3 * h), BF), pltpu.SemaphoreType.DMA],
        cost(9 * T * D * C * G, 2 * G * (T * D + 4 * C * D + 5 * T * C), G * T * B * C // HD),
        traffic,
    )


def back_body(B, C, hook, hg, wo, qkv, idc, idr, dqkv, dmix):
    tt = hg.shape[0]
    scale = 1.0 / math.sqrt(HD)
    hook("start")
    dmix[...] = dot(hg[...], wo[0], NT).astype(BF)
    masks = head_masks(C)
    wins = [w0 for w0, _ in windows(C)]

    def block(i, _):
        s = pl.ds(pl.multiple_of(i * B, B), B)
        ok = allow(idc, idr, s, B)
        dq = [None] * (C // LANES)
        dk, dv = list(dq), list(dq)
        cut = lambda n, w0: qkv[0, s, n * C + w0 : n * C + w0 + 2 * LANES]
        for g in range(0, len(wins), 8):
            hs = range(g, min(g + 8, len(wins)))
            q = [cut(0, wins[h]) * masks[h] for h in hs]
            gm = [dmix[s, wins[h] : wins[h] + 2 * LANES] * masks[h] for h in hs]
            p = softmaxes(q, [cut(1, wins[h]) for h in hs], ok)
            dp = [dot(a, cut(2, wins[h]), NT) for a, h in zip(gm, hs)]
            ds = [(a * (b - jnp.sum(a * b, axis=1, keepdims=True))).astype(BF) for a, b in zip(p, dp)]
            for h, a, b, c, d in zip(hs, p, gm, ds, q):
                put(dv, wins[h], dot(a.astype(BF), b, TN))
                put(dk, wins[h], dot(c, d, TN))
                put(dq, wins[h], dot(c, cut(1, wins[h]) * masks[h]))
        for n, tiles in enumerate((dq, dk, dv)):
            a = jnp.concatenate(tiles, axis=1)
            dqkv[0, s, n * C : (n + 1) * C] = (a if n == 2 else a * scale).astype(BF)
        return 0

    lax.fori_loop(0, tt // B, block, 0)
    hook("end")


def attend_back(hg, wo, qkv, idc, idr, traffic):
    T, D = hg.shape
    G, C, _ = wo.shape
    tt, B = pick(T, 512, 384, 256, 128), 128
    by_group = pl.BlockSpec((1, tt, 3 * C), lambda g, i: (g, i, 0))
    return launch(
        functools.partial(back_body, B, C),
        "attend_back",
        (G, T // tt),
        (hg, wo, qkv, idc, idr),
        [
            pl.BlockSpec((tt, D), lambda g, i: (i, 0)),
            pl.BlockSpec((1, C, D), lambda g, i: (g, 0, 0)),
            by_group,
            pl.BlockSpec((tt, 1), lambda g, i: (i, 0)),
            pl.BlockSpec((1, tt), lambda g, i: (0, i)),
        ],
        [jax.ShapeDtypeStruct((G, T, 3 * C), BF)],
        [by_group],
        [pltpu.VMEM((tt, C), BF)],
        cost(12 * T * D * C * G, 2 * G * (T * D + C * D + 6 * T * C), G * T * B * C // HD),
        traffic,
    )


def weight_body(C, G, hook, n1, low, dqkv, mixed, *dw):
    hook("start")
    h = C // 2
    u = dot(n1[...], dqkv[0], TN).astype(BF)
    o = dot(low[...], mixed[0], TN).astype(BF)
    for g in range(G):

        @pl.when(pl.program_id(0) == g)
        def _():
            for side in range(2):
                to = dw[2 * g + side]
                for i in range(3):
                    to[:, i * h : (i + 1) * h] = u[:, i * C + side * h : i * C + (side + 1) * h]
                to[:, 3 * h : 4 * h] = o[:, side * h : (side + 1) * h]

    hook("end")


def weight_grads(n1, low, dqkv, mixed, traffic):
    T, D = n1.shape
    G, _, C = mixed.shape
    rows = pick(D, 256)
    steps = D // rows

    def out(g):
        place = lambda n, i: (jnp.where(n == g, i, jnp.where(n < g, 0, steps - 1)), 0)
        return pl.BlockSpec((rows, 2 * C), place)

    columns = pl.BlockSpec((T, rows), lambda g, i: (0, i))
    return launch(
        functools.partial(weight_body, C, G),
        "weight_grads",
        (G, steps),
        (n1, low, dqkv, mixed),
        [
            columns,
            columns,
            pl.BlockSpec((1, T, 3 * C), lambda g, i: (g, 0, 0)),
            pl.BlockSpec((1, T, C), lambda g, i: (g, 0, 0)),
        ],
        [jax.ShapeDtypeStruct((D, 2 * C), BF)] * (2 * G),
        [out(g) for g in range(G) for _ in range(2)],
        [],
        cost(8 * T * D * C * G, 2 * G * (2 * T * D + 4 * T * C + 4 * D * C)),
        traffic,
    )


def project_body(x, gain, valid, mixed, wo, hidden, n2, square):
    @pl.when(pl.program_id(0) == 0)
    def _():
        square[...] = jnp.zeros_like(square)

    a = sum(dot(mixed[g], wo[g]) for g in range(wo.shape[0]))
    h = x[...].astype(F32) + a
    hidden[...] = h
    n2[...] = (h * rms(h) * gain[...].astype(F32)).astype(BF)
    square[...] += row_sum(valid[...] * a * a)


def project(x, gain, valid, mixed, wo):
    T, D = x.shape
    G, C, _ = wo.shape
    tt = pick(T, 256, 128)
    tile = lambda c: pl.BlockSpec((tt, c), lambda i: (i, 0))
    out, _ = launch(
        lambda hook, *refs: project_body(*refs),
        "project",
        (T // tt,),
        (x, gain, valid, mixed, wo),
        [tile(D), whole((1, D)), tile(1), pl.BlockSpec((G, tt, C), lambda i: (0, i, 0)), whole(wo.shape)],
        [jax.ShapeDtypeStruct((T, D), F32), jax.ShapeDtypeStruct((T, D), BF), jax.ShapeDtypeStruct((1, D), F32)],
        [tile(D), tile(D), pl.BlockSpec((1, D), lambda i: (0, 0))],
        [],
        cost(2 * T * D * D, 12 * T * D),
    )
    return out


def feed_body(
    hook, n2, g, hba, hbb, upa, upb, downa, downb, feed, n2g, dua, dub, dda, ddb, ba, bb, acc_f, acc_n, act, pg, wu, wd
):
    step = pl.program_id(0)
    T, D = n2.shape
    ft = hba.shape[1]
    chunk = pick(T, 768, 384, 128)
    hook("start")

    @pl.when(step == 0)
    def _():
        acc_f[...] = jnp.zeros_like(acc_f)
        acc_n[...] = jnp.zeros_like(acc_n)

    wu[:, :ft], wu[:, ft:] = upa[...], upb[...]
    wd[:ft, :], wd[ft:, :] = downa[...], downb[...]
    hb = jnp.concatenate([hba[...], hbb[...]], axis=1).astype(F32)
    ba[...] = jnp.zeros_like(ba)
    bb[...] = jnp.zeros_like(bb)

    def one(i, _):
        s = pl.ds(pl.multiple_of(i * chunk, chunk), chunk)
        p = dot(n2[s, :], wu[...]) + hb
        ag = dot(g[s, :], wd[...], NT)
        sg = 0.5 * jnp.tanh(0.5 * p) + 0.5
        ps = p * sg
        a = ps.astype(BF)
        q = (ag * (sg + ps * (1.0 - sg))).astype(BF)
        act[s, :] = a
        pg[s, :] = q
        b = row_sum(q.astype(F32))
        ba[...] += b[:, :ft]
        bb[...] += b[:, ft:]
        acc_f[s, :] += dot(a, wd[...])
        acc_n[s, :] += dot(q, wu[...], NT)
        return 0

    lax.fori_loop(0, T // chunk, one, 0)
    hook("middle")
    u = dot(n2[...], pg[...], TN).astype(BF)
    dua[...], dub[...] = u[:, :ft], u[:, ft:]
    d = dot(act[...], g[...], TN).astype(BF)
    dda[...], ddb[...] = d[:ft], d[ft:]

    @pl.when(step == pl.num_programs(0) - 1)
    def _():
        feed[...] = acc_f[...].astype(BF)
        n2g[...] = acc_n[...].astype(BF)

    hook("end")


def feed_forward(n2, g, biases, ups, downs, traffic=None):
    T, D = n2.shape
    F = biases[0].shape[1]
    ft = pick(F, 256)
    up = pl.BlockSpec((D, ft), lambda f: (0, f))
    down = pl.BlockSpec((ft, D), lambda f: (f, 0))
    bias = pl.BlockSpec((1, ft), lambda f: (0, f))
    return launch(
        feed_body,
        "feed_forward",
        (F // ft,),
        (n2, g, *biases, *ups, *downs),
        [whole((T, D)), whole((T, D)), bias, bias, up, up, down, down],
        [jax.ShapeDtypeStruct((T, D), BF)] * 2
        + [jax.ShapeDtypeStruct((D, F), BF)] * 2
        + [jax.ShapeDtypeStruct((F, D), BF)] * 2
        + [jax.ShapeDtypeStruct((1, F), F32)] * 2,
        [whole((T, D)), whole((T, D)), up, up, down, down, bias, bias],
        [
            pltpu.VMEM((T, D), F32),
            pltpu.VMEM((T, D), F32),
            pltpu.VMEM((T, 2 * ft), BF),
            pltpu.VMEM((T, 2 * ft), BF),
            pltpu.VMEM((D, 2 * ft), BF),
            pltpu.VMEM((2 * ft, D), BF),
        ],
        cost(24 * T * D * F, 16 * T * D + 16 * D * F, 2 * T * F),
        traffic,
    )


def middle_body(n, *refs):
    hidden, g, gain, out_bias, valid = refs[:5]
    feeds, grads = refs[5 : 5 + n], refs[5 + n : 5 + 2 * n]
    out, low, sums = refs[5 + 2 * n :]

    @pl.when(pl.program_id(0) == 0)
    def _():
        sums[...] = jnp.zeros_like(sums)

    h, go = hidden[...], g[...].astype(F32)
    f = sum(a[...].astype(F32) for a in feeds) + out_bias[...].astype(F32)
    ng = sum(a[...].astype(F32) for a in grads)
    result = h + f
    out[...] = result.astype(BF)
    r2 = rms(h)
    wg = ng * gain[...].astype(F32)
    inner = jnp.sum(wg * h, axis=1, keepdims=True)
    low[...] = (go + wg * r2 - h * (r2 * r2 * r2 * inner / h.shape[1])).astype(BF)
    v = valid[...]
    for i, a in enumerate((ng * h * r2, go, v * f * f, v * result * result)):
        sums[i : i + 1, :] += row_sum(a)


def middle(hidden, g, gain, out_bias, valid, feeds, grads):
    T, D = hidden.shape
    tt = pick(T, 256, 128)
    tile = lambda c: pl.BlockSpec((tt, c), lambda i: (i, 0))
    n = len(feeds)
    out, _ = launch(
        lambda hook, *refs: middle_body(n, *refs),
        "middle",
        (T // tt,),
        (hidden, g, gain, out_bias, valid, *feeds, *grads),
        [tile(D), tile(D), whole((1, D)), whole((1, D)), tile(1)] + [tile(D)] * (2 * n),
        [jax.ShapeDtypeStruct((T, D), BF), jax.ShapeDtypeStruct((T, D), BF), jax.ShapeDtypeStruct((8, D), F32)],
        [tile(D), tile(D), pl.BlockSpec((8, D), lambda i: (0, 0))],
        [],
        cost(40 * T * D, (10 + 4 * n) * T * D),
    )
    return out


def last_body(hook, x, gain, low, dqkv, w, out, part):
    hook("start")

    @pl.when(pl.program_id(0) == 0)
    def _():
        part[...] = jnp.zeros_like(part)

    ng = sum(dot(dqkv[g], w[g], NT) for g in range(w.shape[0]))
    t = x[...].astype(F32)
    r1 = rms(t)
    wg = ng * gain[...].astype(F32)
    inner = jnp.sum(wg * t, axis=1, keepdims=True)
    out[...] = low[...].astype(F32) + wg * r1 - t * (r1 * r1 * r1 * inner / t.shape[1])
    part[...] += row_sum(ng * t * r1)
    hook("end")


def last(x, gain, low, dqkv, w, traffic):
    T, D = x.shape
    G, _, K = w.shape
    tt = pick(T, 256, 128)
    tile = lambda c: pl.BlockSpec((tt, c), lambda i: (i, 0))
    return launch(
        last_body,
        "last",
        (T // tt,),
        (x, gain, low, dqkv, w),
        [tile(D), whole((1, D)), tile(D), pl.BlockSpec((G, tt, K), lambda i: (0, i, 0)), whole(w.shape)],
        [jax.ShapeDtypeStruct((T, D), F32), jax.ShapeDtypeStruct((1, D), F32)],
        [tile(D), pl.BlockSpec((1, D), lambda i: (0, 0))],
        [],
        cost(6 * T * D * D, 8 * T * D + 6 * D * D),
        traffic,
    )


def swap(a, axis, bit):
    return lax.ppermute(a, axis, [(i, i ^ bit) for i in range(lax.axis_size(axis))])


def all_sum(a):
    for axis in ("mp", "dp"):
        bit = 1
        while bit < lax.axis_size(axis):
            a = a + swap(a, axis, bit)
            bit *= 2
    return a


def segments(lengths):
    slots = lengths.shape[1]
    upto = lax.broadcasted_iota(jnp.int32, (1, slots, slots), 2) <= lax.broadcasted_iota(
        jnp.int32, (1, slots, slots), 1
    )
    ends = jnp.sum(jnp.where(upto, lengths[:, None, :], 0), axis=2)
    places = lax.broadcasted_iota(jnp.int32, (lengths.shape[0], L, slots), 1)
    return jnp.sum((ends[:, None, :] <= places).astype(jnp.int32), axis=2)


def merge(*dicts):
    return {k: v for d in dicts for k, v in d.items()}


def fused(x, cotangent, weights, gains, out_bias, valid, ids, mp):
    T, D = x.shape
    joined, wo, up, down, bias = weights
    h = wo.shape[0]
    hidden_units = up.shape[1]
    near, far, deep = ("dp", 1), ("dp", 2), ("dp", 4)

    J, W = Gather("j", D, 3 * h), Gather("w", h, D)
    U, V = Gather("u", D, hidden_units), Gather("v", hidden_units, D)
    both, four = (J, W), (J, W, U, V)
    steps = T // pick(T, 512, 384, 256, 128)
    t = Traffic(
        1,
        [CORE, Y, near, far],
        dict(j=joined, w=wo, u=up, v=down),
        merge(*[g.buffers("s", "q", "o", "p") for g in both], *[g.buffers("s", "q") for g in (U, V)]),
    )
    t.on(0, "start", *[g.start(s) for s in "sy" for g in both], J.wait("s"))
    t.on(1, "start", *[g.wait("y") for g in both], *[g.start("a") for g in both])
    t.on(1, "start", *[g.start(s) for s in "ys" for g in (U, V)])
    t.on(steps, "start", *[g.wait("a") for g in both], *[g.start("b") for g in both])
    t.on(steps, "start", *[g.wait("b") for g in both], *[g.start("p") for g in both], J.wait("p"))
    t.on(2 * steps - 1, "end", W.wait("s"), W.wait("p"), *[g.wait(s) for s in "ys" for g in (U, V)])
    (qkv, mixed, w, n1), got = attend(x, gains[0], *ids, h, [("j", "js"), ("jo", "jp")], t)
    wo_all = jnp.stack([jnp.concatenate([wo, got["ws"]]), jnp.concatenate([got["wo"], got["wp"]])])
    hidden, n2, att_square = project(x, gains[1], valid, mixed, wo_all)

    bias_o = swap(bias, "mp", 2)
    t = Traffic(
        2,
        [CORE, near, far],
        dict(uq=got["uq"], vq=got["vq"], u=up, v=down),
        merge(*[g.buffers("o", "p") for g in (U, V)]),
    )
    fs = hidden_units // pick(hidden_units, 256)
    t.on(0, "start", *[g.start("a") for g in (U, V)])
    t.on(3, "start", *[g.wait("a") for g in (U, V)], *[g.start("b") for g in (U, V)])
    t.on(fs - 1, "middle", *[g.wait("b") for g in (U, V)], *[g.start("p") for g in (U, V)])
    t.on(fs - 1, "end", *[g.wait("p") for g in (U, V)])
    own, far_weights = feed_forward(
        n2, cotangent, (bias, swap(bias, "mp", 1)), (up, got["us"]), (down, got["vs"]), t
    )

    a, b = (1, 2, 4), (2, 1, 4)
    U0, D0 = Stream("u0", "u0a", "u0b", D, hidden_units, a), Stream("d0", "d0a", "d0b", hidden_units, D, b)
    U1, D1 = Stream("u1", "u1a", "u1b", D, hidden_units, a), Stream("d1", "d1a", "d1b", hidden_units, D, b)
    half = D // 2
    att = [
        [Stream(f"j{n}{m}", f"j{n}a", f"j{n}b", half, 4 * h, (a, b)[m], m * half) for m in range(2)]
        for n in range(2)
    ]
    first = (U0, D0)
    second = (U1, D1)
    t = Traffic(
        3,
        [CORE, near, far],
        dict(u0a=own[2], u0b=own[3], d0a=own[4], d0b=own[5]),
        merge(*[s.buffers("c", "s0", "r0", "s1", "r1") for s in first]),
    )
    t.on(0, "start", *[s.start_core for s in first])
    t.on(1, "start", *[s.wait_core for s in first], *[s.start(0) for s in first])
    t.on(fs - 1, "start", *[s.wait(0) for s in first], *[s.start(1) for s in first])
    t.on(fs - 1, "end", *[s.wait(1) for s in first])
    other, left = feed_forward(
        n2,
        cotangent,
        (bias_o, swap(bias_o, "mp", 1)),
        (far_weights["uo"], far_weights["up"]),
        (far_weights["vo"], far_weights["vp"]),
        t,
    )
    feeds = [own, other]
    out, low, sums = middle(
        hidden, cotangent, gains[1], out_bias, valid, [f[0] for f in feeds], [f[1] for f in feeds]
    )

    held = dict(u0a=own[2], d0a=own[4], u1a=other[2], u1b=other[3], d1a=other[4], d1b=other[5])
    held |= {k: left[k] for k in left if k[2] in "cr"}
    t = Traffic(
        4,
        [CORE, near, far, deep],
        held,
        merge(*[s.buffers("s2", "r2", "e") for s in first], *[s.buffers("c", "s0", "r0") for s in second]),
    )
    t.on(0, "start", *[s.start_core for s in second], *[s.start(2) for s in first])
    t.on(1, "start", *[s.wait_core for s in second], *[s.start(0) for s in second])
    t.on(3, "start", *[s.wait(2) for s in first], *[s.keep for s in first])
    t.on(2 * steps - 1, "end", *[s.wait(0) for s in second])
    (dqkv,), left = attend_back(low, wo_all, qkv, *ids, t)
    e0 = {k: left[k] for k in ("u0e", "d0e")}

    held = dict(u1a=other[2], d1a=other[4]) | {k: left[k] for k in left if k[:2] in ("u1", "d1") and k[2] in "cr"}
    t = Traffic(
        5, [near, far, deep], held, merge(*[s.buffers("s1", "r1", "s2", "r2", "e") for s in second])
    )
    ws = D // pick(D, 256)
    t.on(0, "start", *[s.start(1) for s in second])
    t.on(ws + 1, "start", *[s.wait(1) for s in second], *[s.start(2) for s in second])
    t.on(2 * ws - 1, "end", *[s.wait(2) for s in second], *[s.keep for s in second])
    dw, left = weight_grads(n1, low, dqkv, mixed, t)

    held = dict(j0a=dw[0], j0b=dw[1], j1a=dw[2], j1b=dw[3], u1e=left["u1e"], d1e=left["d1e"]) | e0
    flat = [s for pair in att for s in pair]
    t = Traffic(
        6,
        [CORE, Y, near, far, deep],
        held,
        merge(
            *[s.buffers("f") for s in first],
            *[s.buffers("y") for s in second],
            *[s.buffers("c", "s0", "r0", "s1", "r1", "s2", "r2", "e") for s in flat],
            *[s.buffers("f") for s in att[0]],
            *[s.buffers("y") for s in att[1]],
        ),
    )
    ls = T // pick(T, 256, 128)
    t.on(0, "start", *[s.start_core for s in flat], *[s.start_cross for s in second])
    t.on(1, "start", *[s.wait_core for s in flat], *[s.start(0) for s in flat])
    t.on(3, "start", *[s.wait_cross for s in second])
    t.on(3, "start", *[f(s) for s, o in zip(first, second) for f in (lambda s: s.total(o), lambda s: s.start_spread(2))])
    end = [s.wait(0) for s in flat] + [s.start(1) for s in flat]
    end += [f for s in first for f in (s.wait_spread(2), s.start_spread(1))]
    end += [s.wait(1) for s in flat] + [s.start(2) for s in flat]
    end += [f for s in first for f in (s.wait_spread(1), s.start_spread(0))]
    end += [s.wait(2) for s in flat] + [s.keep for s in flat]
    end += [s.start_cross for s in att[1]] + [s.wait_cross for s in att[1]]
    end += [f for s, o in zip(*att) for f in (s.total(o), s.start_spread(2))]
    for j in (2, 1):
        end += [f for s in att[0] for f in (s.wait_spread(j), s.start_spread(j - 1))]
    end += [s.wait_spread(0) for s in (*att[0], *first)]
    t.on(ls - 1, "end", *end)
    (input_gradient, first_part), done = last(x, gains[0], low, dqkv, w, t)
    joined_total = jnp.concatenate([done["j00f"], done["j01f"]])
    units = jnp.zeros((1, lax.axis_size("mp") * hidden_units), F32)
    for change, part in ((0, own[6]), (1, own[7]), (2, other[6]), (3, other[7])):
        units = lax.dynamic_update_slice(units, part, (0, (mp ^ change) * hidden_units))
    return (out, input_gradient, joined_total, done["u0f"], done["d0f"]), (units, sums, att_square, first_part)


def gathered(x, cotangent, weights, gains, out_bias, valid, ids):
    D = x.shape[1]
    joined, wo, up, down, bias = weights
    every = lambda a, d: lax.all_gather(a, "mp", axis=d, tiled=True)
    two = lambda a, d: tuple(jnp.split(every(a, d), 2, axis=d))
    sides = [jnp.concatenate(p, axis=1) for p in zip(*(two(a, 1) for a in jnp.split(joined, 3, axis=1)))]
    plain = Traffic(0, [], dict(a=sides[0], b=sides[1]), {})
    (qkv, mixed, w, n1), _ = attend(x, gains[0], *ids, sides[0].shape[1] // 3, [("a", "b")], plain)
    wo_all = every(wo, 0)[None]
    hidden, n2, att_square = project(x, gains[1], valid, mixed, wo_all)
    f, _ = feed_forward(n2, cotangent, two(bias, 1), two(up, 1), two(down, 0))
    out, low, sums = middle(hidden, cotangent, gains[1], out_bias, valid, [f[0]], [f[1]])
    (dqkv,), _ = attend_back(low, wo_all, qkv, *ids, None)
    dw, _ = weight_grads(n1, low, dqkv, mixed, None)
    (input_gradient, first_part), _ = last(x, gains[0], low, dqkv, w, None)

    def total(pair, d):
        part = lax.psum_scatter(jnp.concatenate(pair, axis=d), "mp", scatter_dimension=d, tiled=True)
        return lax.psum(part, "dp")

    cut = [jnp.split(a, 4, axis=1) for a in dw]
    joined_total = jnp.concatenate([total(pair, 1) for pair in zip(*cut)], axis=1)
    grads = (out, input_gradient, joined_total, total(f[2:4], 1), total(f[4:6], 0))
    return grads, (jnp.concatenate(f[6:], axis=1), sums, att_square, first_part)


def per_device(
    tokens,
    lengths,
    cotangent,
    query_weight,
    key_weight,
    value_weight,
    out_weight,
    up_weight,
    hidden_bias,
    down_weight,
    output_bias,
    first_gain,
    second_gain,
):
    T, D = tokens.shape
    h = query_weight.shape[1]
    rows = T // L
    mp = lax.axis_index("mp")
    segment_ids = segments(lax.dynamic_slice_in_dim(lengths, mp * rows, rows))
    valid = (segment_ids < SLOTS).reshape(-1, 1).astype(F32)
    ids = (segment_ids + L * lax.broadcasted_iota(jnp.int32, (rows, L), 0)).reshape(-1)
    ids = (ids[:, None], ids[None, :])
    joined = jnp.concatenate([query_weight, key_weight, value_weight], axis=1)
    bias = hidden_bias.reshape(1, -1)
    gains = (first_gain.reshape(1, -1), second_gain.reshape(1, -1))
    weights = (joined, out_weight, up_weight, down_weight, bias)
    rest = (gains, output_bias.reshape(1, -1), valid, ids)
    if lax.axis_size("mp") == 4 and lax.axis_size("dp") == 8:
        grads, parts = fused(tokens, cotangent, weights, *rest, mp)
    else:
        grads, parts = gathered(tokens, cotangent, weights, *rest)
    out, input_gradient, joined_total, up_total, down_total = grads
    units, sums, att_square, first_part = parts
    n = units.shape[1]
    squares = jnp.stack([jnp.sum(att_square), jnp.sum(sums[2]), jnp.sum(sums[3]), jnp.sum(valid)])
    small = all_sum(jnp.concatenate([units[0], sums[0], sums[1], squares]))
    squares = small[n + 2 * D :]
    joined_total = joined_total.astype(F32)
    return (
        out,
        input_gradient,
        joined_total[:, :h],
        joined_total[:, h : 2 * h],
        joined_total[:, 2 * h : 3 * h],
        joined_total[:, 3 * h :].T,
        up_total.astype(F32),
        lax.dynamic_slice_in_dim(small, mp * bias.shape[1], bias.shape[1]),
        down_total.astype(F32),
        small[n + D : n + 2 * D],
        all_sum(first_part[0]),
        small[n : n + D],
        jnp.sqrt(squares[:3] / (squares[3] * D)),
    )


def solution(mesh):
    return jax.shard_map(
        per_device,
        mesh=mesh,
        in_specs=(
            P(("dp", "mp"), None),
            P("dp", None),
            P(("dp", "mp"), None),
            P(None, "mp"),
            P(None, "mp"),
            P(None, "mp"),
            P("mp", None),
            P(None, "mp"),
            P("mp"),
            P("mp", None),
            P(),
            P(),
            P(),
        ),
        out_specs=(
            P(("dp", "mp"), None),
            P(("dp", "mp"), None),
            P(None, "mp"),
            P(None, "mp"),
            P(None, "mp"),
            P("mp", None),
            P(None, "mp"),
            P("mp"),
            P("mp", None),
            P(),
            P(),
            P(),
            P(),
        ),
        check_vma=False,
    )
```

time: 1710 us -> 799 us (0.47)
  waiting for transfers between devices: 948 us -> 5.8 us
  Pallas kernels: 0 us -> 705 us
  matrix products: 346 us -> 0 us
  local copies, waits for them, and re-layouts: 229 us -> 34.9 us
  other arithmetic: 97.8 us -> 26.5 us
  blocking collectives: 62.7 us -> 0 us
    pallas_call x0 -> x8, Pallas kernels: none -> 705 us  [launch(): pl.pallas_call(kernel, grid=grid, in_specs=[*in_specs, *[anywhere] * len(...]
    reduce_scatter x4 -> x0, waiting for transfers between devices: 402 us -> none  [the longest x1 122 us: per_device(): lax.psum_scatter(jnp.einsum('tf,df->td', preact_grad, up_weight, preferre...]
    dot_general x18 -> x0, matrix products: 346 us -> none  [the longest x1 38.4 us: per_device(): jnp.einsum('td,fd->tf', grad_rows, down_weight, preferred_element_type=jn...]
    all_gather x4 -> x0, waiting for transfers between devices: 282 us -> none  [the longest x1 99.5 us: per_device(): second_rows = lax.all_gather(second_normed, 'mp', axis=0, tiled=True)]
    psum x1 -> x0, waiting for transfers between devices: 263 us -> none  [per_device(): lax.psum(query_part.astype(jnp.bfloat16), 'dp').astype(jnp.float32)]
    reshape x12 -> x4, local copies, waits for them, and re-layouts: 136 us -> 3.93 us  [the longest x2 2.57 us: per_device(): gains = (first_gain.reshape(1, -1), second_gain.reshape(1, -1))]
    convert_element_type x6 -> x1, local copies, waits for them, and re-layouts: 73.9 us -> 1.62 us  [per_device(): valid = (segment_ids < SLOTS).reshape(-1, 1).astype(F32)]
    psum x2 -> x0, blocking collectives: 62.7 us -> none  [the longest x1 40 us: per_device(): lax.psum((first_gain_part, second_gain_part, output_bias_part, squares, c...]
  transfers between devices with their start and end apart: 9 -> 13, of which waited for: 9 -> 3; matrix products, arithmetic and copies ran while one was open for 14% -> 6% of each run, Pallas kernels for 0% -> 74%
where the time goes in v2:
time: 799 us; the launch traced here: 788 us
  Pallas kernels  705 us (88%)
  local copies, waits for them, and re-layouts  34.9 us (4%)
  other arithmetic  26.5 us (3%)
  starting transfers between devices  13.4 us (2%)
    pallas_call x8, Pallas kernels, launch(): pl.pallas_call(kernel, grid=grid, in_specs=[*in_specs, *[anywhere] * len(...  705 us
    unnamed x32, local copies, waits for them, and re-layouts  18.1 us
  transfers between devices with their start and end apart: 13, of which 3 were waited for; matrix products, arithmetic and copies ran while one was open for 6% of the time, Pallas kernels for 74%

profile of v2, /device:TPU:0, one launch (start us, length us, event | category | flops | bytes accessed | tf_op | source)
XLA Modules:
  0.0 787.9 jit_solution(11128304176896659986)
XLA Ops:
  0.7 0.8 reshape.122.refs_2_
  1.4 3.0 collective-permute-start.1
  5.4 0.7 add.74.refs_3_.refs_4_
  6.0 1.6 add.90.refs_2_.refs_3_
  7.7 1.3 reshape.120.refs_1_
  8.9 1.3 reshape.119.refs_1_.refs_2_
  10.2 1.6 reshape.124.refs_2_.refs_4_
  11.8 1.5 copy.47
  14.0 1.6 copy.49
  15.6 2.5 pad_maximum_fusion.1.refs_4_
  18.1 95.3 %attend.1 = (bf16[2,1536,1920]{2,1,0:T(8,128)(2,1)}, bf16[2,1536,640]{2,1,0:T(8,128)(2,1)}, bf16[2,1280,1920]{2,1,0:T(8,128)(2,1)}, bf16[1536,1280]{1,0:T(8,128)...) custom-call(bf16[1536,1280]{1,0:T(8,128)(2,1)} %refs_0_.5, ...), custom_call_target="tpu_custom_call" | custom-call | flops 22649241600 | bytes 40632320 | tf_op jit(solution)/shard_map/attend/pallas_call | solution.py:128
  113.5 1.9 maximum_bitcast_fusion
  115.3 2.0 pad_maximum_fusion.refs_4_.refs_1_
  117.3 12.9 %project.1 = (f32[1536,1280]{1,0:T(8,128)}, bf16[1536,1280]{1,0:T(8,128)(2,1)}, f32[1,1280]{1,0:T(1,128)}) custom-call(bf16[1536,1280]{1,0:T(8,128)(2,1)} %refs_0_.5, bf16[1,1280]{1,0:T(2,128)(2,1)} %reshape.119.refs_1_.refs_2_, f32[1536,1]{1,0:T(8,128)} %reshape.124.refs_2_.refs_4_, bf16[2,1536,640]{2,1,0:T(8,128)(2,1)} %get-tuple-element.75.refs_3_, ...), custom_call_target="tpu_custom_call" | custom-call | flops 5033164800 | bytes 23592960 | tf_op jit(solution)/shard_map/project/pallas_call | solution.py:128
  131.4 1.3 reduce_sum.56
  133.7 94.0 %feed_forward.2 = (bf16[1536,1280]{1,0:T(8,128)(2,1)}, bf16[1536,1280]{1,0:T(8,128)(2,1)}, bf16[1280,1280]{1,0:T(8,128)(2,1)}, bf16[1280,1280]{1,0:T(8,128)(2,1)...) custom-call(bf16[1536,1280]{1,0:T(8,128)(2,1)} %get-tuple-element.80, ...), custom_call_target="tpu_custom_call" | custom-call | flops 60397977600 | bytes 57671680 | tf_op jit(solution)/shard_map/feed_forward/pallas_call | solution.py:128
  227.7 0.7 reduce.3
  228.4 0.7 reduce.4
  230.4 105.2 %feed_forward.3 = (bf16[1536,1280]{1,0:T(8,128)(2,1)}, bf16[1536,1280]{1,0:T(8,128)(2,1)}, bf16[1280,1280]{1,0:T(8,128)(2,1)}, bf16[1280,1280]{1,0:T(8,128)(2,1)...) custom-call(bf16[1536,1280]{1,0:T(8,128)(2,1)} %get-tuple-element.80, ...), custom_call_target="tpu_custom_call" | custom-call | flops 60397977600 | bytes 57671680 | tf_op jit(solution)/shard_map/feed_forward/pallas_call | solution.py:128
  335.6 0.7 reduce.5
  336.4 0.7 reduce.6
  337.1 15.9 %middle.1 = (bf16[1536,1280]{1,0:T(8,128)(2,1)}, bf16[1536,1280]{1,0:T(8,128)(2,1)}, f32[8,1280]{1,0:T(8,128)}) custom-call(f32[1536,1280]{1,0:T(8,128)} %get-tuple-element.79.refs_0_, bf16[1536,1280]{1,0:T(8,128)(2,1)} %refs_1_.5, bf16[1,1280]{1,0:T(2,128)(2,1)} %reshape.119.refs_1_.refs_2_, bf16[1,1280]{1,0:T(2,128)(2,1)} %reshape.121.refs_3_, ...), custom_call_target="tpu_custom_call" | custom-call | flops 78643200 | bytes 35389440 | tf_op jit(solution)/shard_map/middle/pallas_call | solution.py:128
  353.0 1.6 slice_reduce_fusion
  355.2 2.6 concatenate.19
  357.8 81.6 %attend_back.1 = (bf16[2,1536,1920]{2,1,0:T(8,128)(2,1)}, bf16[160,1280]{1,0:T(8,128)(2,1)}, bf16[160,1280]{1,0:T(8,128)(2,1)}, bf16[160,1280]{1,0:T(8,128)(2,1)...) custom-call(bf16[1536,1280]{1,0:T(8,128)(2,1)} %get-tuple-element.98, ...), custom_call_target="tpu_custom_call" | custom-call | flops 30198988800 | bytes 34734080 | tf_op jit(solution)/shard_map/attend_back/pallas_call | solution.py:128
  439.4 1.5 collective-permute-start.4
  440.9 78.6 %weight_grads.1 = (bf16[1280,1280]{1,0:T(8,128)(2,1)}, bf16[1280,1280]{1,0:T(8,128)(2,1)}, bf16[1280,1280]{1,0:T(8,128)(2,1)}, bf16[1280,1280]{1,0:T(8,128)(2,1)...) custom-call(bf16[1536,1280]{1,0:T(8,128)(2,1)} %get-tuple-element.11, ...), custom_call_target="tpu_custom_call" | custom-call | flops 20132659200 | bytes 44564480 | tf_op jit(solution)/shard_map/weight_grads/pallas_call | solution.py:128
  519.6 0.7 collective-permute-start.5
  520.3 221.7 %last.1 = (f32[1536,1280]{1,0:T(8,128)}, f32[1,1280]{1,0:T(1,128)}, bf16[1280,1280]{1,0:T(8,128)(2,1)}, bf16[1280,1280]{1,0:T(8,128)(2,1)}, bf16[160,1280]{1,0:T...) custom-call(bf16[1536,1280]{1,0:T(8,128)(2,1)} %refs_0_.5, ...), custom_call_target="tpu_custom_call" | custom-call | flops 15099494400 | bytes 25559040 | tf_op jit(solution)/shard_map/last/pallas_call | solution.py:128
  742.0 0.7 reduce.9
  742.8 1.2 collective-permute-done.8
  743.9 1.3 collective-permute-start.9
  745.2 2.4 collective-permute-done.9
  747.6 1.4 collective-permute-start.10
  749.0 2.3 collective-permute-done.10
  751.3 2.0 collective-permute-start.6
  753.4 2.4 maximum_convert_fusion
  755.8 1.7 collective-permute-start.12
  757.5 1.3 collective-permute-start.7
  758.9 3.7 slice_bitcast_fusion
  762.6 2.7 copy.57
  765.3 2.7 copy.56
  768.0 2.7 copy.55
  770.8 1.7 copy.54
  772.4 5.4 convert_element_type.23
  777.9 3.3 convert_element_type.25
  783.6 0.7 fusion.2
  784.3 3.2 copy.63
  (68 shorter events, 7.6 us)
Async XLA Ops:
  0.6 3.8 copy-start
  0.7 12.7 %copy-start.4 = (bf16[1280,320]{0,1:T(8,128)(2,1)S(1)}, bf16[1280,320]{0,1:T(8,128)(2,1)}, u32[]{:S(2)}) copy-start(bf16[1280,320]{0,1:T(8,128)(2,1)} %param.17) | copy-start | bytes 2457604
  1.4 14.2 %copy-start.5 = (bf16[1,1280]{1,0:T(2,128)(2,1)}, bf16[1,1280]{1,0:T(2,128)(2,1)S(1)}, u32[]{:S(2)}) copy-start(bf16[1,1280]{1,0:T(2,128)(2,1)S(1)} %reshape.122.refs_2_) | copy-start | bytes 7684
  1.4 131.3 %collective-permute-start.1 = (bf16[1,1280]{1,0:T(2,128)(2,1)S(1)}, bf16[1,1280]{1,0:T(2,128)(2,1)S(1)}, u32[]{:S(2)}, u32[]{:S(2)}) collective-permute-start(bf16[1,1280]{1,0:T(2,128)(2,1)S(1)} %reshape.122.refs_2_), channel_id=1, source_target_pairs={{0,2},{1,3},{2,0},{3,1},{4,6},{5,7},{6,4},{7,5},{8,10},{9,11},{10,... | collective-permute-start | bytes 7688 | tf_op jit(solution)/shard_map/ppermute | solution.py:704
  4.4 128.7 %collective-permute-start = (bf16[1,1280]{1,0:T(2,128)(2,1)S(1)}, bf16[1,1280]{1,0:T(2,128)(2,1)S(1)}, u32[]{:S(2)}, u32[]{:S(2)}) collective-permute-start(bf16[1,1280]{1,0:T(2,128)(2,1)S(1)} %reshape.122.refs_2_), channel_id=1, source_target_pairs={{0,1},{1,0},{2,3},{3,2},{4,5},{5,4},{6,7},{7,6},{8,9},{9,8},{10,11... | collective-permute-start | bytes 7688 | tf_op jit(solution)/shard_map/ppermute | solution.py:704
  18.1 95.4 %copy-start.3 = (bf16[320,1280]{1,0:T(8,128)(2,1)S(1)}, bf16[320,1280]{1,0:T(8,128)(2,1)}, u32[]{:S(2)}) copy-start(bf16[320,1280]{1,0:T(8,128)(2,1)} %refs_5_.1) | copy-start | bytes 2457604
  117.3 13.5 %copy-start.6 = (bf16[1280]{0:T(1024)(128)(2,1)S(1)}, bf16[1280]{0:T(1024)(128)(2,1)}, u32[]{:S(2)}) copy-start(bf16[1280]{0:T(1024)(128)(2,1)} %param.23) | copy-start | bytes 7684
  132.7 95.0 %copy-start.7 = (bf16[1,1280]{1,0:T(2,128)(2,1)}, bf16[1,1280]{1,0:T(2,128)(2,1)S(1)}, u32[]{:S(2)}) copy-start(bf16[1,1280]{1,0:T(2,128)(2,1)S(1)} %collective-permute-done.1.refs_2_) | copy-start | bytes 7684
  132.7 97.1 %collective-permute-start.2 = (bf16[1,1280]{1,0:T(2,128)(2,1)S(1)}, bf16[1,1280]{1,0:T(2,128)(2,1)S(1)}, u32[]{:S(2)}, u32[]{:S(2)}) collective-permute-start(bf16[1,1280]{1,0:T(2,128)(2,1)S(1)} %collective-permute-done.1.refs_2_), channel_id=1, source_target_pairs={{0,1},{1,0},{2,3},{3,2},{4,5},{5,4},{6,7},{7,6},{8,9},{9,8},{10,11... | collective-permute-start | bytes 7688 | tf_op jit(solution)/shard_map/ppermute | solution.py:704
  133.1 0.6 copy-start.8
  229.8 0.6 copy-start.9
  357.8 81.6 %collective-permute-start.3 = (f32[7684]{0:T(1024)S(1)}, f32[7684]{0:T(1024)S(1)}, u32[]{:S(2)}, u32[]{:S(2)}) collective-permute-start(f32[7684]{0:T(1024)S(1)} %concatenate.19), channel_id=1, source_target_pairs={{0,1},{1,0},{2,3},{3,2},{4,5},{5,4},{6,7},{7,6},{8,9},{9,8},{10,11... | collective-permute-start | bytes 92216 | tf_op jit(solution)/shard_map/ppermute | solution.py:704
  439.4 80.1 %collective-permute-start.4 = (f32[7684]{0:T(1024)S(1)}, f32[7684]{0:T(1024)S(1)}, u32[]{:S(2)}, u32[]{:S(2)}) collective-permute-start(f32[7684]{0:T(1024)S(1)} %add.79), channel_id=1, source_target_pairs={{0,2},{1,3},{2,0},{3,1},{4,6},{5,7},{6,4},{7,5},{8,10},{9,11},{10,... | collective-permute-start | bytes 92216 | tf_op jit(solution)/shard_map/ppermute | solution.py:704
  519.6 231.7 %collective-permute-start.5 = (f32[7684]{0:T(1024)S(1)}, f32[7684]{0:T(1024)S(1)}, u32[]{:S(2)}, u32[]{:S(2)}) collective-permute-start(f32[7684]{0:T(1024)S(1)} %add.80), channel_id=1, source_target_pairs={{0,4},{4,0},{8,12},{12,8},{16,20},{20,16},{24,28},{28,24},{1,5},{5... | collective-permute-start | bytes 92216 | tf_op jit(solution)/shard_map/ppermute | solution.py:704
  742.7 1.2 collective-permute-start.8
  743.9 3.7 collective-permute-start.9
  747.6 3.7 collective-permute-start.10
  751.3 4.5 collective-permute-start.11
  751.3 6.2 collective-permute-start.6
  755.8 25.4 %collective-permute-start.12 = (f32[1280]{0:T(1024)S(1)}, f32[1280]{0:T(1024)S(1)}, u32[]{:S(2)}, u32[]{:S(2)}) collective-permute-start(f32[1280]{0:T(1024)S(1)} %add.88), channel_id=1, source_target_pairs={{0,16},{4,20},{8,24},{12,28},{16,0},{20,4},{24,8},{28,12},{1,17},{... | collective-permute-start | bytes 15368 | tf_op jit(solution)/shard_map/ppermute | solution.py:704
  757.5 24.3 %collective-permute-start.7 = (f32[7684]{0:T(1024)S(1)}, f32[7684]{0:T(1024)S(1)}, u32[]{:S(2)}, u32[]{:S(2)}) collective-permute-start(f32[7684]{0:T(1024)S(1)} %add.82), channel_id=1, source_target_pairs={{0,16},{4,20},{8,24},{12,28},{16,0},{20,4},{24,8},{28,12},{1,17},{... | collective-permute-start | bytes 92216 | tf_op jit(solution)/shard_map/ppermute | solution.py:704
  772.4 5.5 copy-start.2
  772.4 11.8 %slice-start = ((s8[7864320]{0:T(1024)(128)(4,1)}), s8[4194304]{0:T(1024)(128)(4,1)S(1)}, s32[]{:S(2)}) async-start(s8[7864320]{0:T(1024)(128)(4,1)} %bitcast.11), calls=%async_computation | async-start | bytes 8388608
  777.9 6.4 slice-start.1
  784.3 3.2 copy-start.1

commit v3 on v2

--- a/solution.py
+++ b/solution.py
@@ -59,9 +59,9 @@
 
 
 class Traffic:
-    def __init__(self, number, partners, arrays, buffers):
+    def __init__(self, number, partners, arrays, buffers, scratch=None):
         self.number, self.partners = number, partners
-        self.arrays, self.buffers = arrays, buffers
+        self.arrays, self.buffers, self.scratch = arrays, buffers, scratch or {}
         self.events, self.slots, self.refs = [], {}, {}
 
     def on(self, step, place, *actions):
@@ -95,7 +95,7 @@
         return pltpu.make_async_copy(src, dst, self.sems.at[0, i])
 
 
-COPIES = 40
+COPIES = 48
 
 
 def launch(body, name, grid, args, in_specs, outs, out_specs, scratch, cost_estimate, traffic=None):
@@ -105,7 +105,8 @@
         names = [*traffic.arrays, *traffic.buffers]
         arrays = list(traffic.arrays.values())
         buffers = [jax.ShapeDtypeStruct(s, BF) for s in traffic.buffers.values()]
-        scratch = [*scratch, pltpu.SemaphoreType.DMA((2, COPIES))]
+        names += [*traffic.scratch]
+        scratch = [*scratch, *traffic.scratch.values(), pltpu.SemaphoreType.DMA((2, COPIES))]
 
     def kernel(*refs):
         hook = lambda place: None
@@ -117,8 +118,10 @@
             step = pl.program_id(0)
             for d in range(1, len(grid)):
                 step = step * grid[d] + pl.program_id(d)
-            traffic.refs = dict(zip(names, [*moved, *landing]))
             traffic.sems, refs = refs[-1], refs[:-1]
+            n = len(refs) - len(traffic.scratch)
+            traffic.refs = dict(zip(names, [*moved, *landing, *refs[n:]]))
+            refs = refs[:n]
             if traffic.partners:
                 pl.when(step == 0)(traffic.greet)
             hook = lambda place: traffic.run(step, place)
@@ -139,12 +142,12 @@
         cost_estimate=cost_estimate,
         name=name,
     )(*args, *arrays)
-    return out[:n_outs], dict(zip(names[len(arrays) :], out[n_outs:]))
+    return out[:n_outs], dict(zip(names[len(arrays) : len(arrays) + len(buffers)], out[n_outs:]))
 
 
 def add_rows(sources, target, rows):
     columns = target.shape[1]
-    tile = pl.BlockSpec((pick(rows, 80, 64, 16), columns), lambda i: (i, 0))
+    tile = pl.BlockSpec((rows // 2 if rows // 2 % 16 == 0 else rows, columns), lambda i: (i, 0))
 
     def body(*refs):
         refs[-1][...] = sum(r[...].astype(F32) for r in refs[:-1]).astype(BF)
@@ -155,15 +158,16 @@
 
 
 class Stream:
-    def __init__(self, tag, mine, theirs, rows, columns, order, base=0):
+    def __init__(self, tag, mine, theirs, rows, columns, order, cut, base=0, joins=None):
         self.tag, self.mine, self.theirs, self.base = tag, mine, theirs, base
         self.rows, self.columns, self.order = rows, columns, order
+        self.cut, self.joins = cut, joins
 
     def name(self, what):
         return self.tag + what
 
     def buffers(self, *what):
-        size = lambda w: self.rows if w[0] in "cf" else self.rows >> len(self.order) if w[0] in "ey" else self.rows >> (int(w[1]) + 1)
+        size = lambda w: self.rows if w[0] in "cf" else self.rows >> self.cut if w[0] in "ey" else self.rows >> (int(w[1]) + 1)
         return {self.name(w): (size(w), self.columns) for w in what}
 
     def place(self, stages):
@@ -177,6 +181,8 @@
         out = [(t.refs[self.mine], first + self.base), (t.refs[self.name("c")], first)]
         for j in range(arrived):
             out.append((t.refs[self.name(f"r{j}")], first - self.place(j + 1)[0]))
+        if self.joins is not None and arrived >= self.cut:
+            out.append((t.refs[self.joins + "y"], first - self.place(self.cut)[0]))
         return out
 
     def core(self, t):
@@ -206,8 +212,8 @@
         return lambda t: self.exchange(t, j).wait()
 
     def keep(self, t):
-        first, n = self.place(len(self.order))
-        add_rows(self.sources(t, first, len(self.order)), t.refs[self.name("e")], n)
+        first, n = self.place(self.cut)
+        add_rows(self.sources(t, first, self.cut), t.refs[self.name("e")], n)
 
     def cross(self, t):
         return t.copy(self.name("y"), t.refs[self.name("e")], t.refs[self.name("y")], Y)
@@ -218,13 +224,10 @@
     def wait_cross(self, t):
         self.cross(t).wait()
 
-    def total(self, other):
-        def action(t):
-            first, n = self.place(len(self.order))
-            target = t.refs[self.name("f")].at[pl.ds(pl.multiple_of(first, 16), n), :]
-            add_rows([(t.refs[self.name("e")], 0), (t.refs[other.name("y")], 0)], target, n)
-
-        return action
+    def total(self, t):
+        first, n = self.place(len(self.order))
+        target = t.refs[self.name("f")].at[pl.ds(pl.multiple_of(first, 16), n), :]
+        add_rows(self.sources(t, first, len(self.order)), target, n)
 
     def spread(self, t, j):
         first, n = self.place(j + 1)
@@ -236,6 +239,66 @@
 
     def wait_spread(self, j):
         return lambda t: self.spread(t, j).wait()
+
+
+def sum_rows(sources, target, rows):
+    step = pick(rows, 80, 64, 32, 16)
+
+    def one(i, _):
+        part = lambda o: pl.ds(pl.multiple_of(o + i * step, 16), step)
+        target[part(0), :] = sum(r[part(o), :].astype(F32) for r, o in sources).astype(BF)
+        return 0
+
+    lax.fori_loop(0, rows // step, one, 0)
+
+
+class Near(Stream):
+    def scratch(self, *what):
+        size = lambda w: self.rows if w == "m" else self.buffers(w)[self.name(w)][0]
+        return {self.name(w): pltpu.VMEM((size(w), self.columns), BF) for w in what}
+
+    def sources(self, t, first, arrived):
+        out = super().sources(t, first, arrived)
+        return [(t.refs[self.name("m")], first), *out[1:]]
+
+    def load(self, t):
+        src = t.refs[self.mine].at[pl.ds(self.base, self.rows), :]
+        return t.local(self.name("m"), src, t.refs[self.name("m")])
+
+    def start_load(self, t):
+        self.load(t).start()
+
+    def wait_load(self, t):
+        self.load(t).wait()
+
+    def start(self, j):
+        def action(t):
+            first, n = self.place(j)
+            n //= 2
+            sent = first + (1 - bit_of("dp", self.order[j])) * n
+            sum_rows(self.sources(t, sent, j), t.refs[self.name(f"s{j}")], n)
+            self.exchange(t, j).start()
+
+        return action
+
+    def keep(self, t):
+        first, n = self.place(self.cut)
+        sum_rows(self.sources(t, first, self.cut), t.refs[self.name("e")], n)
+
+    def total(self, t):
+        first, n = self.place(len(self.order))
+        target = t.refs[self.name("f")].at[pl.ds(pl.multiple_of(first, 16), n), :]
+        sum_rows(self.sources(t, first, len(self.order)), target, n)
+
+    def store(self, t):
+        out = t.refs["joined"].at[pl.ds(self.base, self.rows), :]
+        return t.local(self.name("o"), t.refs[self.name("f")], out)
+
+    def start_store(self, t):
+        self.store(t).start()
+
+    def wait_store(self, t):
+        self.store(t).wait()
 
 
 class Gather:
@@ -622,7 +685,8 @@
     )
 
 
-def middle_body(n, *refs):
+def middle_body(n, hook, *refs):
+    hook("start")
     hidden, g, gain, out_bias, valid = refs[:5]
     feeds, grads = refs[5 : 5 + n], refs[5 + n : 5 + 2 * n]
     out, low, sums = refs[5 + 2 * n :]
@@ -643,15 +707,16 @@
     v = valid[...]
     for i, a in enumerate((ng * h * r2, go, v * f * f, v * result * result)):
         sums[i : i + 1, :] += row_sum(a)
-
-
-def middle(hidden, g, gain, out_bias, valid, feeds, grads):
+    hook("end")
+
+
+def middle(hidden, g, gain, out_bias, valid, feeds, grads, traffic=None):
     T, D = hidden.shape
     tt = pick(T, 256, 128)
     tile = lambda c: pl.BlockSpec((tt, c), lambda i: (i, 0))
     n = len(feeds)
-    out, _ = launch(
-        lambda hook, *refs: middle_body(n, *refs),
+    return launch(
+        functools.partial(middle_body, n),
         "middle",
         (T // tt,),
         (hidden, g, gain, out_bias, valid, *feeds, *grads),
@@ -660,11 +725,11 @@
         [tile(D), tile(D), pl.BlockSpec((8, D), lambda i: (0, 0))],
         [],
         cost(40 * T * D, (10 + 4 * n) * T * D),
-    )
-    return out
-
-
-def last_body(hook, x, gain, low, dqkv, w, out, part):
+        traffic,
+    )
+
+
+def last_body(traffic, hook, x, gain, low, dqkv, w, out, part, summed=None):
     hook("start")
 
     @pl.when(pl.program_id(0) == 0)
@@ -678,39 +743,62 @@
     inner = jnp.sum(wg * t, axis=1, keepdims=True)
     out[...] = low[...].astype(F32) + wg * r1 - t * (r1 * r1 * r1 * inner / t.shape[1])
     part[...] += row_sum(ng * t * r1)
+    if traffic is not None:
+        traffic.refs["part"], traffic.refs["summed"] = part, summed
     hook("end")
 
 
-def last(x, gain, low, dqkv, w, traffic):
+def last(x, gain, low, dqkv, w, traffic=None, small=None):
     T, D = x.shape
     G, _, K = w.shape
+    rows = [] if small is None else [small]
     tt = pick(T, 256, 128)
     tile = lambda c: pl.BlockSpec((tt, c), lambda i: (i, 0))
     return launch(
-        last_body,
+        functools.partial(last_body, traffic),
         "last",
         (T // tt,),
         (x, gain, low, dqkv, w),
         [tile(D), whole((1, D)), tile(D), pl.BlockSpec((G, tt, K), lambda i: (0, i, 0)), whole(w.shape)],
-        [jax.ShapeDtypeStruct((T, D), F32), jax.ShapeDtypeStruct((1, D), F32)],
-        [tile(D), pl.BlockSpec((1, D), lambda i: (0, 0))],
+        [jax.ShapeDtypeStruct((n, D), F32) for n in (T, 1, *rows)],
+        [tile(D), *[pl.BlockSpec((n, D), lambda i: (0, 0)) for n in (1, *rows)]],
         [],
         cost(6 * T * D * D, 8 * T * D + 6 * D * D),
         traffic,
     )
 
 
+def finish_body(h, joined, up, down, q, k, v, o, up_out, down_out):
+    j = joined[...].astype(F32).T
+    for i, ref in enumerate((q, k, v, o)):
+        ref[...] = j[i * h : (i + 1) * h]
+    up_out[...] = up[...].astype(F32)
+    down_out[...] = down[...].astype(F32)
+
+
+def finish(joined, up, down):
+    D, F = up.shape
+    h = joined.shape[1] // 4
+    rows = pick(D, 256)
+    steps = D // rows
+    tile = lambda n, c: pl.BlockSpec((n // steps, c), lambda i: (i, 0))
+    ups = [tile(D, F), tile(F, D)]
+    out, _ = launch(
+        lambda hook, *refs: finish_body(h, *refs),
+        "finish",
+        (steps,),
+        (joined, up, down),
+        [tile(D, 4 * h), *ups],
+        [jax.ShapeDtypeStruct((h, D), F32)] * 4 + [jax.ShapeDtypeStruct(a.shape, F32) for a in (up, down)],
+        [pl.BlockSpec((h, rows), lambda i: (0, i))] * 4 + ups,
+        [],
+        cost(D * D, 6 * (4 * h * D + 2 * D * F)),
+    )
+    return out
+
+
 def swap(a, axis, bit):
     return lax.ppermute(a, axis, [(i, i ^ bit) for i in range(lax.axis_size(axis))])
-
-
-def all_sum(a):
-    for axis in ("mp", "dp"):
-        bit = 1
-        while bit < lax.axis_size(axis):
-            a = a + swap(a, axis, bit)
-            bit *= 2
-    return a
 
 
 def segments(lengths):
@@ -763,19 +851,25 @@
     )
     fs = hidden_units // pick(hidden_units, 256)
     t.on(0, "start", *[g.start("a") for g in (U, V)])
-    t.on(3, "start", *[g.wait("a") for g in (U, V)], *[g.start("b") for g in (U, V)])
-    t.on(fs - 1, "middle", *[g.wait("b") for g in (U, V)], *[g.start("p") for g in (U, V)])
+    t.on(2, "middle", *[g.wait("a") for g in (U, V)], *[g.start("b") for g in (U, V)])
+    t.on(3, "middle", *[g.wait("b") for g in (U, V)], *[g.start("p") for g in (U, V)])
     t.on(fs - 1, "end", *[g.wait("p") for g in (U, V)])
     own, far_weights = feed_forward(
         n2, cotangent, (bias, swap(bias, "mp", 1)), (up, got["us"]), (down, got["vs"]), t
     )
 
     a, b = (1, 2, 4), (2, 1, 4)
-    U0, D0 = Stream("u0", "u0a", "u0b", D, hidden_units, a), Stream("d0", "d0a", "d0b", hidden_units, D, b)
-    U1, D1 = Stream("u1", "u1a", "u1b", D, hidden_units, a), Stream("d1", "d1a", "d1b", hidden_units, D, b)
+    U0, D0 = (
+        Stream("u0", "u0a", "u0b", D, hidden_units, a, 2, joins="u1"),
+        Stream("d0", "d0a", "d0b", hidden_units, D, b, 2, joins="d1"),
+    )
+    U1, D1 = Stream("u1", "u1a", "u1b", D, hidden_units, a, 2), Stream("d1", "d1a", "d1b", hidden_units, D, b, 2)
     half = D // 2
     att = [
-        [Stream(f"j{n}{m}", f"j{n}a", f"j{n}b", half, 4 * h, (a, b)[m], m * half) for m in range(2)]
+        [
+            Near(f"j{n}{m}", f"j{n}a", f"j{n}b", half, 4 * h, (a, b)[m], 1, m * half, None if n else f"j1{m}")
+            for m in range(2)
+        ]
         for n in range(2)
     ]
     first = (U0, D0)
@@ -787,8 +881,8 @@
         merge(*[s.buffers("c", "s0", "r0", "s1", "r1") for s in first]),
     )
     t.on(0, "start", *[s.start_core for s in first])
-    t.on(1, "start", *[s.wait_core for s in first], *[s.start(0) for s in first])
-    t.on(fs - 1, "start", *[s.wait(0) for s in first], *[s.start(1) for s in first])
+    t.on(0, "middle", *[s.wait_core for s in first], *[s.start(0) for s in first])
+    t.on(3, "start", *[s.wait(0) for s in first], *[s.start(1) for s in first])
     t.on(fs - 1, "end", *[s.wait(1) for s in first])
     other, left = feed_forward(
         n2,
@@ -799,71 +893,105 @@
         t,
     )
     feeds = [own, other]
-    out, low, sums = middle(
-        hidden, cotangent, gains[1], out_bias, valid, [f[0] for f in feeds], [f[1] for f in feeds]
-    )
-
-    held = dict(u0a=own[2], d0a=own[4], u1a=other[2], u1b=other[3], d1a=other[4], d1b=other[5])
-    held |= {k: left[k] for k in left if k[2] in "cr"}
     t = Traffic(
-        4,
-        [CORE, near, far, deep],
-        held,
-        merge(*[s.buffers("s2", "r2", "e") for s in first], *[s.buffers("c", "s0", "r0") for s in second]),
-    )
-    t.on(0, "start", *[s.start_core for s in second], *[s.start(2) for s in first])
-    t.on(1, "start", *[s.wait_core for s in second], *[s.start(0) for s in second])
-    t.on(3, "start", *[s.wait(2) for s in first], *[s.keep for s in first])
-    t.on(2 * steps - 1, "end", *[s.wait(0) for s in second])
-    (dqkv,), left = attend_back(low, wo_all, qkv, *ids, t)
-    e0 = {k: left[k] for k in ("u0e", "d0e")}
-
-    held = dict(u1a=other[2], d1a=other[4]) | {k: left[k] for k in left if k[:2] in ("u1", "d1") and k[2] in "cr"}
+        7,
+        [CORE],
+        dict(u1b=other[3], d1b=other[5]),
+        merge(*[s.buffers("c") for s in second]),
+    )
+    ls = T // pick(T, 256, 128)
+    t.on(0, "start", *[s.start_core for s in second]).on(ls - 1, "end", *[s.wait_core for s in second])
+    (out, low, sums), cores = middle(
+        hidden, cotangent, gains[1], out_bias, valid, [f[0] for f in feeds], [f[1] for f in feeds], t
+    )
+
+    held = dict(u1a=other[2], d1a=other[4]) | cores
+    t = Traffic(4, [near, far], held, merge(*[s.buffers("s0", "r0", "s1", "r1") for s in second]))
+    t.on(0, "start", *[s.start(0) for s in second])
+    t.on(2 * steps - 2, "start", *[s.wait(0) for s in second], *[s.start(1) for s in second])
+    t.on(2 * steps - 1, "end", *[s.wait(1) for s in second])
+    (dqkv,), arrived = attend_back(low, wo_all, qkv, *ids, t)
+
     t = Traffic(
-        5, [near, far, deep], held, merge(*[s.buffers("s1", "r1", "s2", "r2", "e") for s in second])
+        5, [Y], held | {k: v for k, v in arrived.items() if k[2] == "r"}, merge(*[s.buffers("e", "y") for s in second])
     )
     ws = D // pick(D, 256)
-    t.on(0, "start", *[s.start(1) for s in second])
-    t.on(ws + 1, "start", *[s.wait(1) for s in second], *[s.start(2) for s in second])
-    t.on(2 * ws - 1, "end", *[s.wait(2) for s in second], *[s.keep for s in second])
-    dw, left = weight_grads(n1, low, dqkv, mixed, t)
-
-    held = dict(j0a=dw[0], j0b=dw[1], j1a=dw[2], j1b=dw[3], u1e=left["u1e"], d1e=left["d1e"]) | e0
-    flat = [s for pair in att for s in pair]
-    t = Traffic(
-        6,
-        [CORE, Y, near, far, deep],
-        held,
-        merge(
-            *[s.buffers("f") for s in first],
-            *[s.buffers("y") for s in second],
-            *[s.buffers("c", "s0", "r0", "s1", "r1", "s2", "r2", "e") for s in flat],
-            *[s.buffers("f") for s in att[0]],
-            *[s.buffers("y") for s in att[1]],
-        ),
-    )
-    ls = T // pick(T, 256, 128)
-    t.on(0, "start", *[s.start_core for s in flat], *[s.start_cross for s in second])
-    t.on(1, "start", *[s.wait_core for s in flat], *[s.start(0) for s in flat])
-    t.on(3, "start", *[s.wait_cross for s in second])
-    t.on(3, "start", *[f(s) for s, o in zip(first, second) for f in (lambda s: s.total(o), lambda s: s.start_spread(2))])
-    end = [s.wait(0) for s in flat] + [s.start(1) for s in flat]
-    end += [f for s in first for f in (s.wait_spread(2), s.start_spread(1))]
-    end += [s.wait(1) for s in flat] + [s.start(2) for s in flat]
-    end += [f for s in first for f in (s.wait_spread(1), s.start_spread(0))]
-    end += [s.wait(2) for s in flat] + [s.keep for s in flat]
-    end += [s.start_cross for s in att[1]] + [s.wait_cross for s in att[1]]
-    end += [f for s, o in zip(*att) for f in (s.total(o), s.start_spread(2))]
-    for j in (2, 1):
-        end += [f for s in att[0] for f in (s.wait_spread(j), s.start_spread(j - 1))]
-    end += [s.wait_spread(0) for s in (*att[0], *first)]
-    t.on(ls - 1, "end", *end)
-    (input_gradient, first_part), done = last(x, gains[0], low, dqkv, w, t)
-    joined_total = jnp.concatenate([done["j00f"], done["j01f"]])
+    t.on(0, "start", *[f for s in second for f in (s.keep, s.start_cross)])
+    t.on(2 * ws - 1, "end", *[s.wait_cross for s in second])
+    dw, crossed = weight_grads(n1, low, dqkv, mixed, t)
+
     units = jnp.zeros((1, lax.axis_size("mp") * hidden_units), F32)
     for change, part in ((0, own[6]), (1, own[7]), (2, other[6]), (3, other[7])):
         units = lax.dynamic_update_slice(units, part, (0, (mp ^ change) * hidden_units))
-    return (out, input_gradient, joined_total, done["u0f"], done["d0f"]), (units, sums, att_square, first_part)
+    count = jnp.where(jnp.arange(D) == 0, jnp.sum(valid), 0.0)[None]
+    rows = jnp.concatenate([units.reshape(-1, D), sums[:4], att_square, count])
+    n_rows = rows.shape[0] + 1
+    tall = (n_rows + 7) // 8 * 8
+    small = jnp.pad(rows, ((1, tall - n_rows), (0, 0)))
+
+    held = dict(j0a=dw[0], j0b=dw[1], j1a=dw[2], j1b=dw[3], u1y=crossed["u1y"], d1y=crossed["d1y"], small=small)
+    held |= dict(u0a=own[2], d0a=own[4]) | {k: v for k, v in left.items() if k[2] in "cr"}
+    flat = [s for pair in att for s in pair]
+    bits = [CORE, Y, near, far, deep]
+    t = Traffic(
+        6,
+        bits,
+        held,
+        merge(*[s.buffers("s2", "r2", "f") for s in first], dict(joined=(D, 4 * h))),
+        merge(
+            *[s.scratch("m", "c", "s0", "r0") for s in flat],
+            *[s.scratch("s1", "r1", "s2", "r2", "f") for s in att[0]],
+            *[s.scratch("e", "y") for s in att[1]],
+            {f"t{n}": pltpu.VMEM((tall, D), F32) for n in range(2 * len(bits) + 1)},
+        ),
+    )
+
+    def load_small(t):
+        return t.local("small", t.refs["small"], t.refs["t0"])
+
+    def first_small(t):
+        load_small(t).wait()
+        t.refs["t0"][0:1, :] = t.refs["part"][...]
+
+    def exchange_small(t, n):
+        return t.copy(f"t{n}", t.refs[f"t{2 * n}"], t.refs[f"t{2 * n + 1}"], bits[n])
+
+    def store_small(t):
+        t.refs["summed"][...] = t.refs[f"t{2 * len(bits)}"][...]
+
+    def start_small(n):
+        return lambda t: exchange_small(t, n).start()
+
+    def end_small(n):
+        def action(t):
+            exchange_small(t, n).wait()
+            t.refs[f"t{2 * n + 2}"][...] = t.refs[f"t{2 * n}"][...] + t.refs[f"t{2 * n + 1}"][...]
+
+        return action
+
+    t.on(0, "start", *[s.start_core for s in flat], *[s.start_load for s in flat])
+    t.on(0, "start", lambda t: load_small(t).start(), *[s.start(2) for s in first])
+    t.on(1, "start", *[s.wait_load for s in flat], *[s.wait_core for s in flat], *[s.start(0) for s in flat])
+    end = [first_small, start_small(0)]
+    end += [f for s in first for f in (s.wait(2), s.total, s.start_spread(2))]
+    end += [end_small(0), start_small(1)]
+    end += [f for s in att[1] for f in (s.wait(0), s.keep, s.start_cross)] + [s.wait(0) for s in att[0]]
+    end += [end_small(1), start_small(2)]
+    end += [f for s in first for f in (s.wait_spread(2), s.start_spread(1))]
+    end += [s.wait_cross for s in att[1]] + [s.start(1) for s in att[0]]
+    end += [end_small(2), start_small(3)]
+    end += [f for s in att[0] for f in (s.wait(1), s.start(2))]
+    end += [f for s in first for f in (s.wait_spread(1), s.start_spread(0))]
+    end += [f for s in att[0] for f in (s.wait(2), s.total, s.start_spread(2))]
+    end += [end_small(3), start_small(4)]
+    for j in (2, 1):
+        end += [f for s in att[0] for f in (s.wait_spread(j), s.start_spread(j - 1))]
+    end += [end_small(4), store_small]
+    end += [f for s in att[0] for f in (s.wait_spread(0), s.start_store)]
+    end += [s.wait_spread(0) for s in first] + [s.wait_store for s in att[0]]
+    t.on(ls - 1, "end", *end)
+    (input_gradient, _, summed), done = last(x, gains[0], low, dqkv, w, t, tall)
+    return (out, input_gradient, done["joined"], done["u0f"], done["d0f"]), summed
 
 
 def gathered(x, cotangent, weights, gains, out_bias, valid, ids):
@@ -877,10 +1005,10 @@
     wo_all = every(wo, 0)[None]
     hidden, n2, att_square = project(x, gains[1], valid, mixed, wo_all)
     f, _ = feed_forward(n2, cotangent, two(bias, 1), two(up, 1), two(down, 0))
-    out, low, sums = middle(hidden, cotangent, gains[1], out_bias, valid, [f[0]], [f[1]])
+    (out, low, sums), _ = middle(hidden, cotangent, gains[1], out_bias, valid, [f[0]], [f[1]])
     (dqkv,), _ = attend_back(low, wo_all, qkv, *ids, None)
     dw, _ = weight_grads(n1, low, dqkv, mixed, None)
-    (input_gradient, first_part), _ = last(x, gains[0], low, dqkv, w, None)
+    (input_gradient, first_part), _ = last(x, gains[0], low, dqkv, w)
 
     def total(pair, d):
         part = lax.psum_scatter(jnp.concatenate(pair, axis=d), "mp", scatter_dimension=d, tiled=True)
@@ -889,7 +1017,9 @@
     cut = [jnp.split(a, 4, axis=1) for a in dw]
     joined_total = jnp.concatenate([total(pair, 1) for pair in zip(*cut)], axis=1)
     grads = (out, input_gradient, joined_total, total(f[2:4], 1), total(f[4:6], 0))
-    return grads, (jnp.concatenate(f[6:], axis=1), sums, att_square, first_part)
+    units = jnp.concatenate(f[6:], axis=1).reshape(-1, D)
+    count = jnp.where(jnp.arange(D) == 0, jnp.sum(valid), 0.0)[None]
+    return grads, lax.psum(jnp.concatenate([first_part, units, sums[:4], att_square, count]), ("dp", "mp"))
 
 
 def per_device(
@@ -908,7 +1038,6 @@
     second_gain,
 ):
     T, D = tokens.shape
-    h = query_weight.shape[1]
     rows = T // L
     mp = lax.axis_index("mp")
     segment_ids = segments(lax.dynamic_slice_in_dim(lengths, mp * rows, rows))
@@ -921,30 +1050,28 @@
     weights = (joined, out_weight, up_weight, down_weight, bias)
     rest = (gains, output_bias.reshape(1, -1), valid, ids)
     if lax.axis_size("mp") == 4 and lax.axis_size("dp") == 8:
-        grads, parts = fused(tokens, cotangent, weights, *rest, mp)
+        grads, small = fused(tokens, cotangent, weights, *rest, mp)
     else:
-        grads, parts = gathered(tokens, cotangent, weights, *rest)
+        grads, small = gathered(tokens, cotangent, weights, *rest)
     out, input_gradient, joined_total, up_total, down_total = grads
-    units, sums, att_square, first_part = parts
-    n = units.shape[1]
-    squares = jnp.stack([jnp.sum(att_square), jnp.sum(sums[2]), jnp.sum(sums[3]), jnp.sum(valid)])
-    small = all_sum(jnp.concatenate([units[0], sums[0], sums[1], squares]))
-    squares = small[n + 2 * D :]
-    joined_total = joined_total.astype(F32)
+    n = hidden_bias.shape[0] * lax.axis_size("mp") // D + 1
+    squares = jnp.sum(small[n + 2 : n + 6], axis=1)
+    mean = lambda i: jnp.sqrt(squares[i] / (squares[3] * D))
+    q, k, v, o, up_total, down_total = finish(joined_total, up_total, down_total)
     return (
         out,
         input_gradient,
-        joined_total[:, :h],
-        joined_total[:, h : 2 * h],
-        joined_total[:, 2 * h : 3 * h],
-        joined_total[:, 3 * h :].T,
-        up_total.astype(F32),
-        lax.dynamic_slice_in_dim(small, mp * bias.shape[1], bias.shape[1]),
-        down_total.astype(F32),
-        small[n + D : n + 2 * D],
-        all_sum(first_part[0]),
-        small[n : n + D],
-        jnp.sqrt(squares[:3] / (squares[3] * D)),
+        q.T,
+        k.T,
+        v.T,
+        o,
+        up_total,
+        lax.dynamic_slice_in_dim(small[1:n].reshape(-1), mp * bias.shape[1], bias.shape[1]),
+        down_total,
+        small[n + 1],
+        small[0],
+        small[n],
+        jnp.stack([mean(2), mean(0), mean(1)]),
     )
 
 

time: 799 us -> 714 us (0.89)
  Pallas kernels: 705 us -> 660 us
  other arithmetic: 26.5 us -> 11.3 us
  starting transfers between devices: 13.4 us -> 3.04 us
  local copies, waits for them, and re-layouts: 34.9 us -> 26.4 us
    pallas_call x8 -> x9, Pallas kernels: 705 us -> 660 us  [launch(): pl.pallas_call(kernel, grid=grid, in_specs=[*in_specs, *[anywhere] * len(...]
    convert_element_type x3 -> x0, other arithmetic: 11.2 us -> none  [the longest x1 5.45 us: per_device(): up_total.astype(F32)]
    ppermute x13 -> x3, starting transfers between devices: 13.4 us -> 3.04 us  [swap(): lax.ppermute(a, axis, [(i, i ^ bit) for i in range(lax.axis_size(axis))])]
    unnamed x32 -> x33, local copies, waits for them, and re-layouts: 18.1 us -> 12.8 us
  transfers between devices with their start and end apart: 13 -> 3, of which waited for: 3 -> 1; matrix products, arithmetic and copies ran while one was open for 6% -> 3% of each run, Pallas kernels for 74% -> 29%
where the time goes in v3:
time: 714 us; the launch traced here: 705 us
  Pallas kernels  660 us (92%)
  local copies, waits for them, and re-layouts  26.4 us (4%)
  other arithmetic  11.3 us (2%)
    pallas_call x9, Pallas kernels, launch(): pl.pallas_call(kernel, grid=grid, in_specs=[*in_specs, *[anywhere] * len(...  660 us
  transfers between devices with their start and end apart: 3, of which 1 were waited for; matrix products, arithmetic and copies ran while one was open for 3% of the time, Pallas kernels for 29%

profile of v3, /device:TPU:0, one launch (start us, length us, event | category | flops | bytes accessed | tf_op | source)
XLA Modules:
  0.0 705.0 jit_solution(4866769987981575083)
XLA Ops:
  0.7 0.8 reshape.139.refs_2_
  1.4 0.5 collective-permute-start
  1.9 2.6 collective-permute-start.1
  4.5 0.1 constant_dynamic-slice_fusion
  4.6 0.1 copy.38
  4.7 0.5 select_reduce_fusion
  5.1 0.2 convert_reduce_fusion
  5.4 0.1 broadcast_add_fusion
  5.4 1.6 add.49.refs_2_.refs_3_
  7.0 0.7 add.44.refs_3_.refs_4_
  7.7 0.6 fusion.1
  8.3 1.3 reshape.136.refs_1_.refs_2_
  9.6 1.6 reshape.143.refs_2_.refs_4_
  11.2 1.3 reshape.137.refs_1_
  12.5 1.5 copy.41
  14.1 0.6 copy.40
  14.7 1.6 copy.39
  16.3 2.5 pad_maximum_fusion.1.refs_4_
  18.8 94.7 %attend.1 = (bf16[2,1536,1920]{2,1,0:T(8,128)(2,1)}, bf16[2,1536,640]{2,1,0:T(8,128)(2,1)}, bf16[2,1280,1920]{2,1,0:T(8,128)(2,1)}, bf16[1536,1280]{1,0:T(8,128)...) custom-call(bf16[1536,1280]{1,0:T(8,128)(2,1)} %refs_0_.5, ...), custom_call_target="tpu_custom_call" | custom-call | flops 22649241600 | bytes 40632320 | tf_op jit(solution)/shard_map/attend/pallas_call | solution.py:131
  113.5 1.9 maximum_bitcast_fusion
  115.4 2.0 pad_maximum_fusion.refs_4_.refs_1_
  117.4 12.9 %project.1 = (f32[1536,1280]{1,0:T(8,128)}, bf16[1536,1280]{1,0:T(8,128)(2,1)}, f32[1,1280]{1,0:T(1,128)}) custom-call(bf16[1536,1280]{1,0:T(8,128)(2,1)} %refs_0_.5, bf16[1,1280]{1,0:T(2,128)(2,1)} %reshape.136.refs_1_.refs_2_, f32[1536,1]{1,0:T(8,128)} %reshape.143.refs_2_.refs_4_, bf16[2,1536,640]{2,1,0:T(8,128)(2,1)} %get-tuple-element.80.refs_3_, ...), custom_call_target="tpu_custom_call" | custom-call | flops 5033164800 | bytes 23592960 | tf_op jit(solution)/shard_map/project/pallas_call | solution.py:131
  130.3 0.6 compare_select_fusion
  130.9 0.6 reshape.138.refs_3_
  131.5 0.6 copy-done.12
  132.1 99.2 %feed_forward.2 = (bf16[1536,1280]{1,0:T(8,128)(2,1)}, bf16[1536,1280]{1,0:T(8,128)(2,1)}, bf16[1280,1280]{1,0:T(8,128)(2,1)}, bf16[1280,1280]{1,0:T(8,128)(2,1)...) custom-call(bf16[1536,1280]{1,0:T(8,128)(2,1)} %get-tuple-element.85, ...), custom_call_target="tpu_custom_call" | custom-call | flops 60397977600 | bytes 57671680 | tf_op jit(solution)/shard_map/feed_forward/pallas_call | solution.py:131
  231.3 0.7 constant_dynamic-update-slice_fusion.3
  232.1 0.7 constant_dynamic-update-slice_fusion.2
  232.8 0.5 collective-permute-done.2.refs_3_
  233.2 0.6 copy-done.13
  233.8 96.4 %feed_forward.3 = (bf16[1536,1280]{1,0:T(8,128)(2,1)}, bf16[1536,1280]{1,0:T(8,128)(2,1)}, bf16[1280,1280]{1,0:T(8,128)(2,1)}, bf16[1280,1280]{1,0:T(8,128)(2,1)...) custom-call(bf16[1536,1280]{1,0:T(8,128)(2,1)} %get-tuple-element.85, ...), custom_call_target="tpu_custom_call" | custom-call | flops 60397977600 | bytes 57671680 | tf_op jit(solution)/shard_map/feed_forward/pallas_call | solution.py:131
  330.3 17.6 %middle.1 = (bf16[1536,1280]{1,0:T(8,128)(2,1)}, bf16[1536,1280]{1,0:T(8,128)(2,1)}, f32[8,1280]{1,0:T(8,128)}, bf16[1280,1280]{1,0:T(8,128)(2,1)}, bf16[1280,1280]{1,0:T(8,128)(2,1)}) custom-call(f32[1536,1280]{1,0:T(8,128)} %get-tuple-element.84.refs_0_, bf16[1536,1280]{1,0:T(8,128)(2,1)} %refs_1_.5, bf16[1,1280]{1,0:T(2,128)(2,1)} %reshape.136.refs_1_.refs_2_, ...), custom_call_target="tpu_custom_call" | custom-call | flops 78643200 | bytes 35389440 | tf_op jit(solution)/shard_map/middle/pallas_call | solution.py:131
  347.9 0.8 slice.32
  348.7 0.5 broadcast.63
  349.2 0.7 reduce.10
  349.9 0.7 select_maximum_fusion.refs_11_
  350.6 74.3 %attend_back.1 = (bf16[2,1536,1920]{2,1,0:T(8,128)(2,1)}, bf16[640,1280]{1,0:T(8,128)(2,1)}, bf16[640,1280]{1,0:T(8,128)(2,1)}, bf16[320,1280]{1,0:T(8,128)(2,1)...) custom-call(bf16[1536,1280]{1,0:T(8,128)(2,1)} %get-tuple-element.10, ...), custom_call_target="tpu_custom_call" | custom-call | flops 30198988800 | bytes 34734080 | tf_op jit(solution)/shard_map/attend_back/pallas_call | solution.py:131
  424.9 46.2 %weight_grads.1 = (bf16[1280,1280]{1,0:T(8,128)(2,1)}, bf16[1280,1280]{1,0:T(8,128)(2,1)}, bf16[1280,1280]{1,0:T(8,128)(2,1)}, bf16[1280,1280]{1,0:T(8,128)(2,1)...) custom-call(bf16[1536,1280]{1,0:T(8,128)(2,1)} %get-tuple-element.11, ...), custom_call_target="tpu_custom_call" | custom-call | flops 20132659200 | bytes 44564480 | tf_op jit(solution)/shard_map/weight_grads/pallas_call | solution.py:131
  471.1 206.5 %last.1 = (f32[1536,1280]{1,0:T(8,128)}, f32[1,1280]{1,0:T(1,128)}, f32[16,1280]{1,0:T(8,128)}, bf16[160,1280]{1,0:T(8,128)(2,1)}, bf16[160,1280]{1,0:T(8,128)(2...) custom-call(bf16[1536,1280]{1,0:T(8,128)(2,1)} %refs_0_.5, ...), custom_call_target="tpu_custom_call" | custom-call | flops 15099494400 | bytes 25559040 | tf_op jit(solution)/shard_map/last/pallas_call | solution.py:131
  677.7 1.0 slice_reduce_fusion
  678.7 1.5 slice_reduce_fusion.1
  680.2 0.7 dynamic_slice.7
  680.9 0.6 fusion.2
  684.3 11.8 %finish.1 = (f32[320,1280]{1,0:T(8,128)}, f32[320,1280]{1,0:T(8,128)}, f32[320,1280]{1,0:T(8,128)}, f32[320,1280]{1,0:T(8,128)}, f32[1280,1280]{1,0:T(8,128)}, /*index=5*/f32[1280,1280]{1,0:T(8,128)}) custom-call(bf16[1280,1280]{1,0:T(8,128)(2,1)} %get-tuple-element.137.refs_0_, bf16[1280,1280]{1,0:T(8,128)(2,1)} %get-tuple-element.138.refs_1_, ...), custom_call_target="tpu_custom_call" | custom-call | flops 1638400 | bytes 29491200 | tf_op jit(solution)/shard_map/finish/pallas_call | solution.py:131
  696.0 0.6 pad_maximum_fusion.2
  696.6 2.0 copy.52
  698.6 2.6 copy-done.2
  701.3 3.2 copy.53
  (36 shorter events, 0.1 us)
Async XLA Ops:
  0.6 3.9 copy-start
  0.7 13.4 %copy-start.5 = (bf16[1280,320]{0,1:T(8,128)(2,1)S(1)}, bf16[1280,320]{0,1:T(8,128)(2,1)}, u32[]{:S(2)}) copy-start(bf16[1280,320]{0,1:T(8,128)(2,1)} %param.17) | copy-start | bytes 2457604
  1.4 14.8 %copy-start.7 = (bf16[1,1280]{1,0:T(2,128)(2,1)}, bf16[1,1280]{1,0:T(2,128)(2,1)S(1)}, u32[]{:S(2)}) copy-start(bf16[1,1280]{1,0:T(2,128)(2,1)S(1)} %reshape.139.refs_2_) | copy-start | bytes 7684
  1.4 130.1 %collective-permute-start = (bf16[1,1280]{1,0:T(2,128)(2,1)S(1)}, bf16[1,1280]{1,0:T(2,128)(2,1)S(1)}, u32[]{:S(2)}, u32[]{:S(2)}) collective-permute-start(bf16[1,1280]{1,0:T(2,128)(2,1)S(1)} %reshape.139.refs_2_), channel_id=1, source_target_pairs={{0,1},{1,0},{2,3},{3,2},{4,5},{5,4},{6,7},{7,6},{8,9},{9,8},{10,11... | collective-permute-start | bytes 7688 | tf_op jit(solution)/shard_map/ppermute | solution.py:801
  1.9 230.1 %collective-permute-start.1 = (bf16[1,1280]{1,0:T(2,128)(2,1)S(1)}, bf16[1,1280]{1,0:T(2,128)(2,1)S(1)}, u32[]{:S(2)}, u32[]{:S(2)}) collective-permute-start(bf16[1,1280]{1,0:T(2,128)(2,1)S(1)} %reshape.139.refs_2_), channel_id=1, source_target_pairs={{0,2},{1,3},{2,0},{3,1},{4,6},{5,7},{6,4},{7,5},{8,10},{9,11},{10,... | collective-permute-start | bytes 7688 | tf_op jit(solution)/shard_map/ppermute | solution.py:801
  18.8 94.7 %copy-start.4 = (bf16[320,1280]{1,0:T(8,128)(2,1)S(1)}, bf16[320,1280]{1,0:T(8,128)(2,1)}, u32[]{:S(2)}) copy-start(bf16[320,1280]{1,0:T(8,128)(2,1)} %refs_5_.1) | copy-start | bytes 2457604
  117.4 13.6 %copy-start.10 = (bf16[1280]{0:T(1024)(128)(2,1)S(1)}, bf16[1280]{0:T(1024)(128)(2,1)}, u32[]{:S(2)}) copy-start(bf16[1280]{0:T(1024)(128)(2,1)} %param.23) | copy-start | bytes 7684
  131.5 0.6 copy-start.12
  232.0 1.2 copy-start.11
  232.0 1.2 collective-permute-start.2
  233.2 0.6 copy-start.13
  330.2 18.4 %copy-start.9 = (f32[1,1280]{1,0:T(1,128)S(1)}, f32[1,1280]{1,0:T(1,128)}, u32[]{:S(2)}) copy-start(f32[1,1280]{1,0:T(1,128)} %get-tuple-element.126) | copy-start | bytes 15364
  330.2 18.4 %copy-start.8 = (f32[1,1280]{1,0:T(1,128)S(1)}, f32[1,1280]{1,0:T(1,128)}, u32[]{:S(2)}) copy-start(f32[1,1280]{1,0:T(1,128)} %get-tuple-element.127) | copy-start | bytes 15364
  330.2 19.7 %copy-start.6 = (f32[1,1280]{1,0:T(1,128)S(1)}, f32[1,1280]{1,0:T(1,128)}, u32[]{:S(2)}) copy-start(f32[1,1280]{1,0:T(1,128)} %get-tuple-element.129) | copy-start | bytes 15364
  684.3 12.4 %copy-start.3 = (bf16[1536,1280]{1,0:T(8,128)(2,1)S(1)}, bf16[1536,1280]{1,0:T(8,128)(2,1)}, u32[]{:S(2)}) copy-start(bf16[1536,1280]{1,0:T(8,128)(2,1)} %get-tuple-element.171) | copy-start | bytes 11796484
  696.6 4.7 copy-start.2
  701.3 3.2 copy-start.1

commit v4 on v3

--- a/solution.py
+++ b/solution.py
@@ -324,9 +324,7 @@
             return [t.copy(name, self.quarter(own), t.refs[self.tag + "q"], Y)]
         if step == "a":
             q = t.refs[self.tag + "q"]
-            return [t.copy(name + str(b), q, self.quarter(o), ("dp", b)) for b in (1, 2)] + [
-                t.local(name + "l", q, self.quarter(o))
-            ]
+            return [t.copy(name + str(b), q, self.quarter(o), ("dp", b)) for b in (1, 2)]
         if step == "b":
             top = (self.n // 2 + 15) // 16 * 16
             to_x = self.quarter(o, flip_z=1, rows=top)
@@ -338,6 +336,8 @@
         def action(t):
             for c in self.copies(t, step):
                 c.start()
+            if step == "a":
+                add_rows([(t.refs[self.tag + "q"], 0)], self.quarter(t.refs[self.tag + "o"]), self.n)
 
         return action
 
@@ -833,10 +833,11 @@
         merge(*[g.buffers("s", "q", "o", "p") for g in both], *[g.buffers("s", "q") for g in (U, V)]),
     )
     t.on(0, "start", *[g.start(s) for s in "sy" for g in both], J.wait("s"))
-    t.on(1, "start", *[g.wait("y") for g in both], *[g.start("a") for g in both])
-    t.on(1, "start", *[g.start(s) for s in "ys" for g in (U, V)])
-    t.on(steps, "start", *[g.wait("a") for g in both], *[g.start("b") for g in both])
-    t.on(steps, "start", *[g.wait("b") for g in both], *[g.start("p") for g in both], J.wait("p"))
+    t.on(0, "middle", *[g.wait("y") for g in both], *[g.start("a") for g in both])
+    t.on(0, "middle", *[g.start(s) for s in "ys" for g in (U, V)])
+    t.on(2, "start", *[g.wait("a") for g in both], *[g.start("b") for g in both])
+    t.on(steps - 1, "end", *[g.wait("b") for g in both], *[g.start("p") for g in both])
+    t.on(steps, "start", J.wait("p"))
     t.on(2 * steps - 1, "end", W.wait("s"), W.wait("p"), *[g.wait(s) for s in "ys" for g in (U, V)])
     (qkv, mixed, w, n1), got = attend(x, gains[0], *ids, h, [("j", "js"), ("jo", "jp")], t)
     wo_all = jnp.stack([jnp.concatenate([wo, got["ws"]]), jnp.concatenate([got["wo"], got["wp"]])])
@@ -851,8 +852,8 @@
     )
     fs = hidden_units // pick(hidden_units, 256)
     t.on(0, "start", *[g.start("a") for g in (U, V)])
-    t.on(2, "middle", *[g.wait("a") for g in (U, V)], *[g.start("b") for g in (U, V)])
-    t.on(3, "middle", *[g.wait("b") for g in (U, V)], *[g.start("p") for g in (U, V)])
+    t.on(3, "start", *[g.wait("a") for g in (U, V)], *[g.start("b") for g in (U, V)])
+    t.on(4, "start", *[g.wait("b") for g in (U, V)], *[g.start("p") for g in (U, V)])
     t.on(fs - 1, "end", *[g.wait("p") for g in (U, V)])
     own, far_weights = feed_forward(
         n2, cotangent, (bias, swap(bias, "mp", 1)), (up, got["us"]), (down, got["vs"]), t

time: 714 us -> 696 us (0.975)
  Pallas kernels: 660 us -> 641 us
    pallas_call x9, Pallas kernels: 660 us -> 641 us  [launch(): pl.pallas_call(kernel, grid=grid, in_specs=[*in_specs, *[anywhere] * len(...]
  transfers between devices with their start and end apart: 3 -> 3, of which waited for: 1 -> 1; matrix products, arithmetic and copies ran while one was open for 3% -> 3% of each run, Pallas kernels for 29% -> 27%
where the time goes in v4:
time: 696 us; the launch traced here: 687 us
  Pallas kernels  641 us (92%)
  local copies, waits for them, and re-layouts  26.4 us (4%)
  other arithmetic  11.3 us (2%)
    pallas_call x9, Pallas kernels, launch(): pl.pallas_call(kernel, grid=grid, in_specs=[*in_specs, *[anywhere] * len(...  641 us
  transfers between devices with their start and end apart: 3, of which 1 were waited for; matrix products, arithmetic and copies ran while one was open for 3% of the time, Pallas kernels for 27%

profile of v4, /device:TPU:0, one launch (start us, length us, event | category | flops | bytes accessed | tf_op | source)
XLA Modules:
  0.0 686.7 jit_solution(15084071493388597111)
XLA Ops:
  0.7 0.8 reshape.139.refs_2_
  1.4 0.5 collective-permute-start
  1.9 2.6 collective-permute-start.1
  4.5 0.1 constant_dynamic-slice_fusion
  4.6 0.1 copy.38
  4.7 0.5 select_reduce_fusion
  5.1 0.2 convert_reduce_fusion
  5.4 0.1 broadcast_add_fusion
  5.4 1.6 add.49.refs_2_.refs_3_
  7.0 0.7 add.44.refs_3_.refs_4_
  7.7 0.6 fusion.1
  8.3 1.3 reshape.136.refs_1_.refs_2_
  9.6 1.6 reshape.143.refs_2_.refs_4_
  11.2 1.3 reshape.137.refs_1_
  12.5 1.5 copy.41
  14.1 0.6 copy.40
  14.7 1.6 copy.39
  16.3 2.5 pad_maximum_fusion.1.refs_4_
  18.8 87.6 %attend.1 = (bf16[2,1536,1920]{2,1,0:T(8,128)(2,1)}, bf16[2,1536,640]{2,1,0:T(8,128)(2,1)}, bf16[2,1280,1920]{2,1,0:T(8,128)(2,1)}, bf16[1536,1280]{1,0:T(8,128)...) custom-call(bf16[1536,1280]{1,0:T(8,128)(2,1)} %refs_0_.5, ...), custom_call_target="tpu_custom_call" | custom-call | flops 22649241600 | bytes 40632320 | tf_op jit(solution)/shard_map/attend/pallas_call | solution.py:131
  106.4 1.9 maximum_bitcast_fusion
  108.2 2.0 pad_maximum_fusion.refs_4_.refs_1_
  110.2 12.9 %project.1 = (f32[1536,1280]{1,0:T(8,128)}, bf16[1536,1280]{1,0:T(8,128)(2,1)}, f32[1,1280]{1,0:T(1,128)}) custom-call(bf16[1536,1280]{1,0:T(8,128)(2,1)} %refs_0_.5, bf16[1,1280]{1,0:T(2,128)(2,1)} %reshape.136.refs_1_.refs_2_, f32[1536,1]{1,0:T(8,128)} %reshape.143.refs_2_.refs_4_, bf16[2,1536,640]{2,1,0:T(8,128)(2,1)} %get-tuple-element.80.refs_3_, ...), custom_call_target="tpu_custom_call" | custom-call | flops 5033164800 | bytes 23592960 | tf_op jit(solution)/shard_map/project/pallas_call | solution.py:131
  123.1 0.6 compare_select_fusion
  123.8 0.6 reshape.138.refs_3_
  124.4 0.6 copy-done.12
  125.0 88.3 %feed_forward.2 = (bf16[1536,1280]{1,0:T(8,128)(2,1)}, bf16[1536,1280]{1,0:T(8,128)(2,1)}, bf16[1280,1280]{1,0:T(8,128)(2,1)}, bf16[1280,1280]{1,0:T(8,128)(2,1)...) custom-call(bf16[1536,1280]{1,0:T(8,128)(2,1)} %get-tuple-element.85, ...), custom_call_target="tpu_custom_call" | custom-call | flops 60397977600 | bytes 57671680 | tf_op jit(solution)/shard_map/feed_forward/pallas_call | solution.py:131
  213.4 0.7 constant_dynamic-update-slice_fusion.3
  214.1 0.7 constant_dynamic-update-slice_fusion.2
  214.8 0.5 collective-permute-done.2.refs_3_
  215.2 0.6 copy-done.13
  215.8 96.4 %feed_forward.3 = (bf16[1536,1280]{1,0:T(8,128)(2,1)}, bf16[1536,1280]{1,0:T(8,128)(2,1)}, bf16[1280,1280]{1,0:T(8,128)(2,1)}, bf16[1280,1280]{1,0:T(8,128)(2,1)...) custom-call(bf16[1536,1280]{1,0:T(8,128)(2,1)} %get-tuple-element.85, ...), custom_call_target="tpu_custom_call" | custom-call | flops 60397977600 | bytes 57671680 | tf_op jit(solution)/shard_map/feed_forward/pallas_call | solution.py:131
  312.3 17.6 %middle.1 = (bf16[1536,1280]{1,0:T(8,128)(2,1)}, bf16[1536,1280]{1,0:T(8,128)(2,1)}, f32[8,1280]{1,0:T(8,128)}, bf16[1280,1280]{1,0:T(8,128)(2,1)}, bf16[1280,1280]{1,0:T(8,128)(2,1)}) custom-call(f32[1536,1280]{1,0:T(8,128)} %get-tuple-element.84.refs_0_, bf16[1536,1280]{1,0:T(8,128)(2,1)} %refs_1_.5, bf16[1,1280]{1,0:T(2,128)(2,1)} %reshape.136.refs_1_.refs_2_, ...), custom_call_target="tpu_custom_call" | custom-call | flops 78643200 | bytes 35389440 | tf_op jit(solution)/shard_map/middle/pallas_call | solution.py:131
  329.9 0.8 slice.32
  330.7 0.5 broadcast.63
  331.2 0.7 reduce.10
  332.0 0.7 select_maximum_fusion.refs_11_
  332.6 73.6 %attend_back.1 = (bf16[2,1536,1920]{2,1,0:T(8,128)(2,1)}, bf16[640,1280]{1,0:T(8,128)(2,1)}, bf16[640,1280]{1,0:T(8,128)(2,1)}, bf16[320,1280]{1,0:T(8,128)(2,1)...) custom-call(bf16[1536,1280]{1,0:T(8,128)(2,1)} %get-tuple-element.10, ...), custom_call_target="tpu_custom_call" | custom-call | flops 30198988800 | bytes 34734080 | tf_op jit(solution)/shard_map/attend_back/pallas_call | solution.py:131
  406.2 46.3 %weight_grads.1 = (bf16[1280,1280]{1,0:T(8,128)(2,1)}, bf16[1280,1280]{1,0:T(8,128)(2,1)}, bf16[1280,1280]{1,0:T(8,128)(2,1)}, bf16[1280,1280]{1,0:T(8,128)(2,1)...) custom-call(bf16[1536,1280]{1,0:T(8,128)(2,1)} %get-tuple-element.11, ...), custom_call_target="tpu_custom_call" | custom-call | flops 20132659200 | bytes 44564480 | tf_op jit(solution)/shard_map/weight_grads/pallas_call | solution.py:131
  452.5 206.8 %last.1 = (f32[1536,1280]{1,0:T(8,128)}, f32[1,1280]{1,0:T(1,128)}, f32[16,1280]{1,0:T(8,128)}, bf16[160,1280]{1,0:T(8,128)(2,1)}, bf16[160,1280]{1,0:T(8,128)(2...) custom-call(bf16[1536,1280]{1,0:T(8,128)(2,1)} %refs_0_.5, ...), custom_call_target="tpu_custom_call" | custom-call | flops 15099494400 | bytes 25559040 | tf_op jit(solution)/shard_map/last/pallas_call | solution.py:131
  659.4 1.0 slice_reduce_fusion
  660.4 1.5 slice_reduce_fusion.1
  661.9 0.7 dynamic_slice.7
  662.6 0.6 fusion.2
  665.9 11.8 %finish.1 = (f32[320,1280]{1,0:T(8,128)}, f32[320,1280]{1,0:T(8,128)}, f32[320,1280]{1,0:T(8,128)}, f32[320,1280]{1,0:T(8,128)}, f32[1280,1280]{1,0:T(8,128)}, /*index=5*/f32[1280,1280]{1,0:T(8,128)}) custom-call(bf16[1280,1280]{1,0:T(8,128)(2,1)} %get-tuple-element.137.refs_0_, bf16[1280,1280]{1,0:T(8,128)(2,1)} %get-tuple-element.138.refs_1_, ...), custom_call_target="tpu_custom_call" | custom-call | flops 1638400 | bytes 29491200 | tf_op jit(solution)/shard_map/finish/pallas_call | solution.py:131
  677.7 0.6 pad_maximum_fusion.2
  678.3 2.0 copy.52
  680.3 2.6 copy-done.2
  683.0 3.2 copy.53
  (36 shorter events, 0.1 us)
Async XLA Ops:
  0.6 3.9 copy-start
  0.7 13.4 %copy-start.5 = (bf16[1280,320]{0,1:T(8,128)(2,1)S(1)}, bf16[1280,320]{0,1:T(8,128)(2,1)}, u32[]{:S(2)}) copy-start(bf16[1280,320]{0,1:T(8,128)(2,1)} %param.17) | copy-start | bytes 2457604
  1.4 14.8 %copy-start.7 = (bf16[1,1280]{1,0:T(2,128)(2,1)}, bf16[1,1280]{1,0:T(2,128)(2,1)S(1)}, u32[]{:S(2)}) copy-start(bf16[1,1280]{1,0:T(2,128)(2,1)S(1)} %reshape.139.refs_2_) | copy-start | bytes 7684
  1.4 122.9 %collective-permute-start = (bf16[1,1280]{1,0:T(2,128)(2,1)S(1)}, bf16[1,1280]{1,0:T(2,128)(2,1)S(1)}, u32[]{:S(2)}, u32[]{:S(2)}) collective-permute-start(bf16[1,1280]{1,0:T(2,128)(2,1)S(1)} %reshape.139.refs_2_), channel_id=1, source_target_pairs={{0,1},{1,0},{2,3},{3,2},{4,5},{5,4},{6,7},{7,6},{8,9},{9,8},{10,11... | collective-permute-start | bytes 7688 | tf_op jit(solution)/shard_map/ppermute | solution.py:801
  1.9 212.2 %collective-permute-start.1 = (bf16[1,1280]{1,0:T(2,128)(2,1)S(1)}, bf16[1,1280]{1,0:T(2,128)(2,1)S(1)}, u32[]{:S(2)}, u32[]{:S(2)}) collective-permute-start(bf16[1,1280]{1,0:T(2,128)(2,1)S(1)} %reshape.139.refs_2_), channel_id=1, source_target_pairs={{0,2},{1,3},{2,0},{3,1},{4,6},{5,7},{6,4},{7,5},{8,10},{9,11},{10,... | collective-permute-start | bytes 7688 | tf_op jit(solution)/shard_map/ppermute | solution.py:801
  18.8 87.6 %copy-start.4 = (bf16[320,1280]{1,0:T(8,128)(2,1)S(1)}, bf16[320,1280]{1,0:T(8,128)(2,1)}, u32[]{:S(2)}) copy-start(bf16[320,1280]{1,0:T(8,128)(2,1)} %refs_5_.1) | copy-start | bytes 2457604
  110.2 13.6 %copy-start.10 = (bf16[1280]{0:T(1024)(128)(2,1)S(1)}, bf16[1280]{0:T(1024)(128)(2,1)}, u32[]{:S(2)}) copy-start(bf16[1280]{0:T(1024)(128)(2,1)} %param.23) | copy-start | bytes 7684
  124.4 0.6 copy-start.12
  214.1 1.2 copy-start.11
  214.1 1.2 collective-permute-start.2
  215.2 0.6 copy-start.13
  312.2 18.4 %copy-start.9 = (f32[1,1280]{1,0:T(1,128)S(1)}, f32[1,1280]{1,0:T(1,128)}, u32[]{:S(2)}) copy-start(f32[1,1280]{1,0:T(1,128)} %get-tuple-element.126) | copy-start | bytes 15364
  312.2 18.4 %copy-start.8 = (f32[1,1280]{1,0:T(1,128)S(1)}, f32[1,1280]{1,0:T(1,128)}, u32[]{:S(2)}) copy-start(f32[1,1280]{1,0:T(1,128)} %get-tuple-element.127) | copy-start | bytes 15364
  312.3 19.7 %copy-start.6 = (f32[1,1280]{1,0:T(1,128)S(1)}, f32[1,1280]{1,0:T(1,128)}, u32[]{:S(2)}) copy-start(f32[1,1280]{1,0:T(1,128)} %get-tuple-element.129) | copy-start | bytes 15364
  665.9 12.4 %copy-start.3 = (bf16[1536,1280]{1,0:T(8,128)(2,1)S(1)}, bf16[1536,1280]{1,0:T(8,128)(2,1)}, u32[]{:S(2)}) copy-start(bf16[1536,1280]{1,0:T(8,128)(2,1)} %get-tuple-element.171) | copy-start | bytes 11796484
  678.3 4.7 copy-start.2
  683.0 3.2 copy-start.1

commit v5 on v4

--- a/solution.py
+++ b/solution.py
@@ -177,13 +177,19 @@
             first = first + bit_of("dp", bit) * n
         return first, n
 
+    def raw(self, t, first, arrived):
+        out = [(t.refs[self.mine], first + self.base), (t.refs[self.name("c")], first)]
+        return out + [(t.refs[self.name(f"r{j}")], first - self.place(j + 1)[0]) for j in range(arrived)]
+
     def sources(self, t, first, arrived):
-        out = [(t.refs[self.mine], first + self.base), (t.refs[self.name("c")], first)]
-        for j in range(arrived):
-            out.append((t.refs[self.name(f"r{j}")], first - self.place(j + 1)[0]))
-        if self.joins is not None and arrived >= self.cut:
-            out.append((t.refs[self.joins + "y"], first - self.place(self.cut)[0]))
-        return out
+        if self.joins is None or arrived < self.cut:
+            return self.raw(t, first, arrived)
+        start = self.place(self.cut)[0]
+        joined = (t.refs[self.joins + "y"], first - start)
+        if self.name("e") not in t.refs:
+            return [*self.raw(t, first, arrived), joined]
+        late = [(t.refs[self.name(f"r{j}")], first - self.place(j + 1)[0]) for j in range(self.cut, arrived)]
+        return [(t.refs[self.name("e")], first - start), *late, joined]
 
     def core(self, t):
         src = t.refs[self.theirs].at[pl.ds(self.base, self.rows), :]
@@ -213,7 +219,7 @@
 
     def keep(self, t):
         first, n = self.place(self.cut)
-        add_rows(self.sources(t, first, self.cut), t.refs[self.name("e")], n)
+        add_rows(self.raw(t, first, self.cut), t.refs[self.name("e")], n)
 
     def cross(self, t):
         return t.copy(self.name("y"), t.refs[self.name("e")], t.refs[self.name("y")], Y)
@@ -257,8 +263,8 @@
         size = lambda w: self.rows if w == "m" else self.buffers(w)[self.name(w)][0]
         return {self.name(w): pltpu.VMEM((size(w), self.columns), BF) for w in what}
 
-    def sources(self, t, first, arrived):
-        out = super().sources(t, first, arrived)
+    def raw(self, t, first, arrived):
+        out = super().raw(t, first, arrived)
         return [(t.refs[self.name("m")], first), *out[1:]]
 
     def load(self, t):
@@ -283,7 +289,7 @@
 
     def keep(self, t):
         first, n = self.place(self.cut)
-        sum_rows(self.sources(t, first, self.cut), t.refs[self.name("e")], n)
+        sum_rows(self.raw(t, first, self.cut), t.refs[self.name("e")], n)
 
     def total(self, t):
         first, n = self.place(len(self.order))
@@ -840,7 +846,7 @@
     t.on(steps, "start", J.wait("p"))
     t.on(2 * steps - 1, "end", W.wait("s"), W.wait("p"), *[g.wait(s) for s in "ys" for g in (U, V)])
     (qkv, mixed, w, n1), got = attend(x, gains[0], *ids, h, [("j", "js"), ("jo", "jp")], t)
-    wo_all = jnp.stack([jnp.concatenate([wo, got["ws"]]), jnp.concatenate([got["wo"], got["wp"]])])
+    wo_all = jnp.concatenate([wo, got["ws"], got["wo"], got["wp"]]).reshape(2, 2 * h, D)
     hidden, n2, att_square = project(x, gains[1], valid, mixed, wo_all)
 
     bias_o = swap(bias, "mp", 2)
@@ -852,7 +858,7 @@
     )
     fs = hidden_units // pick(hidden_units, 256)
     t.on(0, "start", *[g.start("a") for g in (U, V)])
-    t.on(3, "start", *[g.wait("a") for g in (U, V)], *[g.start("b") for g in (U, V)])
+    t.on(2, "middle", *[g.wait("a") for g in (U, V)], *[g.start("b") for g in (U, V)])
     t.on(4, "start", *[g.wait("b") for g in (U, V)], *[g.start("p") for g in (U, V)])
     t.on(fs - 1, "end", *[g.wait("p") for g in (U, V)])
     own, far_weights = feed_forward(
@@ -868,7 +874,7 @@
     half = D // 2
     att = [
         [
-            Near(f"j{n}{m}", f"j{n}a", f"j{n}b", half, 4 * h, (a, b)[m], 1, m * half, None if n else f"j1{m}")
+            Near(f"j{n}{m}", f"j{n}a", f"j{n}b", half, 4 * h, (a, b)[m], 2, m * half, None if n else f"j1{m}")
             for m in range(2)
         ]
         for n in range(2)
@@ -907,9 +913,16 @@
     )
 
     held = dict(u1a=other[2], d1a=other[4]) | cores
-    t = Traffic(4, [near, far], held, merge(*[s.buffers("s0", "r0", "s1", "r1") for s in second]))
+    early = dict(u0a=own[2], d0a=own[4]) | {k: v for k, v in left.items() if k[2] in "cr"}
+    t = Traffic(
+        4,
+        [near, far],
+        held | early,
+        merge(*[s.buffers("s0", "r0", "s1", "r1") for s in second], *[s.buffers("e") for s in first]),
+    )
     t.on(0, "start", *[s.start(0) for s in second])
     t.on(2 * steps - 2, "start", *[s.wait(0) for s in second], *[s.start(1) for s in second])
+    t.on(2 * steps - 1, "start", *[s.keep for s in first])
     t.on(2 * steps - 1, "end", *[s.wait(1) for s in second])
     (dqkv,), arrived = attend_back(low, wo_all, qkv, *ids, t)
 
@@ -931,7 +944,7 @@
     small = jnp.pad(rows, ((1, tall - n_rows), (0, 0)))
 
     held = dict(j0a=dw[0], j0b=dw[1], j1a=dw[2], j1b=dw[3], u1y=crossed["u1y"], d1y=crossed["d1y"], small=small)
-    held |= dict(u0a=own[2], d0a=own[4]) | {k: v for k, v in left.items() if k[2] in "cr"}
+    held |= dict(u0e=arrived["u0e"], d0e=arrived["d0e"])
     flat = [s for pair in att for s in pair]
     bits = [CORE, Y, near, far, deep]
     t = Traffic(
@@ -940,8 +953,8 @@
         held,
         merge(*[s.buffers("s2", "r2", "f") for s in first], dict(joined=(D, 4 * h))),
         merge(
-            *[s.scratch("m", "c", "s0", "r0") for s in flat],
-            *[s.scratch("s1", "r1", "s2", "r2", "f") for s in att[0]],
+            *[s.scratch("m", "c", "s0", "r0", "s1", "r1") for s in flat],
+            *[s.scratch("s2", "r2", "f") for s in att[0]],
             *[s.scratch("e", "y") for s in att[1]],
             {f"t{n}": pltpu.VMEM((tall, D), F32) for n in range(2 * len(bits) + 1)},
         ),
@@ -976,12 +989,12 @@
     end = [first_small, start_small(0)]
     end += [f for s in first for f in (s.wait(2), s.total, s.start_spread(2))]
     end += [end_small(0), start_small(1)]
-    end += [f for s in att[1] for f in (s.wait(0), s.keep, s.start_cross)] + [s.wait(0) for s in att[0]]
+    end += [s.wait(0) for s in flat] + [s.start(1) for s in (*att[1], *att[0])]
     end += [end_small(1), start_small(2)]
     end += [f for s in first for f in (s.wait_spread(2), s.start_spread(1))]
-    end += [s.wait_cross for s in att[1]] + [s.start(1) for s in att[0]]
+    end += [f for s in att[1] for f in (s.wait(1), s.keep, s.start_cross)] + [s.wait(1) for s in att[0]]
     end += [end_small(2), start_small(3)]
-    end += [f for s in att[0] for f in (s.wait(1), s.start(2))]
+    end += [s.wait_cross for s in att[1]] + [s.start(2) for s in att[0]]
     end += [f for s in first for f in (s.wait_spread(1), s.start_spread(0))]
     end += [f for s in att[0] for f in (s.wait(2), s.total, s.start_spread(2))]
     end += [end_small(3), start_small(4)]

time: 696 us -> 699 us (level)
  no operation moved by 1% of the time
where the time goes in v5:
time: 699 us; the launch traced here: 690 us
  Pallas kernels  646 us (92%)
  local copies, waits for them, and re-layouts  26.4 us (4%)
  other arithmetic  10.6 us (2%)
    pallas_call x9, Pallas kernels, launch(): pl.pallas_call(kernel, grid=grid, in_specs=[*in_specs, *[anywhere] * len(...  646 us
  transfers between devices with their start and end apart: 3, of which 1 were waited for; matrix products, arithmetic and copies ran while one was open for 3% of the time, Pallas kernels for 27%

profile of v5, /device:TPU:0, one launch (start us, length us, event | category | flops | bytes accessed | tf_op | source)
XLA Modules:
  0.0 690.3 jit_solution(1460393461908801100)
XLA Ops:
  0.6 0.0 copy-start
  0.7 0.8 reshape.143.refs_2_
  1.4 0.5 collective-permute-start
  1.9 2.6 collective-permute-start.1
  4.5 0.1 constant_dynamic-slice_fusion
  4.6 0.1 copy.38
  4.7 0.5 select_reduce_fusion
  5.1 0.2 convert_reduce_fusion
  5.4 0.1 broadcast_add_fusion
  5.4 1.6 add.49.refs_2_.refs_3_
  7.0 0.7 add.44.refs_3_.refs_4_
  7.7 0.6 fusion.1
  8.3 1.3 reshape.139.refs_1_.refs_2_
  9.6 1.6 reshape.147.refs_2_.refs_4_
  11.2 1.3 reshape.140.refs_1_
  12.5 1.5 copy.41
  14.1 0.6 copy.40
  14.7 1.6 copy.39
  16.3 2.5 pad_maximum_fusion.1.refs_4_
  18.8 87.6 %attend.1 = (bf16[2,1536,1920]{2,1,0:T(8,128)(2,1)}, bf16[2,1536,640]{2,1,0:T(8,128)(2,1)}, bf16[2,1280,1920]{2,1,0:T(8,128)(2,1)}, bf16[1536,1280]{1,0:T(8,128)...) custom-call(bf16[1536,1280]{1,0:T(8,128)(2,1)} %refs_0_.5, ...), custom_call_target="tpu_custom_call" | custom-call | flops 22649241600 | bytes 40632320 | tf_op jit(solution)/shard_map/attend/pallas_call | solution.py:131
  106.4 3.1 pad_maximum_fusion
  109.5 12.9 %project.1 = (f32[1536,1280]{1,0:T(8,128)}, bf16[1536,1280]{1,0:T(8,128)(2,1)}, f32[1,1280]{1,0:T(1,128)}) custom-call(bf16[1536,1280]{1,0:T(8,128)(2,1)} %refs_0_.5, bf16[1,1280]{1,0:T(2,128)(2,1)} %reshape.139.refs_1_.refs_2_, f32[1536,1]{1,0:T(8,128)} %reshape.147.refs_2_.refs_4_, bf16[2,1536,640]{2,1,0:T(8,128)(2,1)} %get-tuple-element.82.refs_3_, ...), custom_call_target="tpu_custom_call" | custom-call | flops 5033164800 | bytes 23592960 | tf_op jit(solution)/shard_map/project/pallas_call | solution.py:131
  122.4 0.6 compare_select_fusion
  123.1 0.6 reshape.142.refs_3_
  123.7 0.6 copy-done.12
  124.2 84.0 %feed_forward.2 = (bf16[1536,1280]{1,0:T(8,128)(2,1)}, bf16[1536,1280]{1,0:T(8,128)(2,1)}, bf16[1280,1280]{1,0:T(8,128)(2,1)}, bf16[1280,1280]{1,0:T(8,128)(2,1)...) custom-call(bf16[1536,1280]{1,0:T(8,128)(2,1)} %get-tuple-element.87, ...), custom_call_target="tpu_custom_call" | custom-call | flops 60397977600 | bytes 57671680 | tf_op jit(solution)/shard_map/feed_forward/pallas_call | solution.py:131
  208.3 0.7 constant_dynamic-update-slice_fusion.3
  209.0 0.7 constant_dynamic-update-slice_fusion.2
  209.7 0.5 collective-permute-done.2.refs_3_
  210.2 0.6 copy-done.13
  210.7 96.5 %feed_forward.3 = (bf16[1536,1280]{1,0:T(8,128)(2,1)}, bf16[1536,1280]{1,0:T(8,128)(2,1)}, bf16[1280,1280]{1,0:T(8,128)(2,1)}, bf16[1280,1280]{1,0:T(8,128)(2,1)...) custom-call(bf16[1536,1280]{1,0:T(8,128)(2,1)} %get-tuple-element.87, ...), custom_call_target="tpu_custom_call" | custom-call | flops 60397977600 | bytes 57671680 | tf_op jit(solution)/shard_map/feed_forward/pallas_call | solution.py:131
  307.2 17.6 %middle.1 = (bf16[1536,1280]{1,0:T(8,128)(2,1)}, bf16[1536,1280]{1,0:T(8,128)(2,1)}, f32[8,1280]{1,0:T(8,128)}, bf16[1280,1280]{1,0:T(8,128)(2,1)}, bf16[1280,1280]{1,0:T(8,128)(2,1)}) custom-call(f32[1536,1280]{1,0:T(8,128)} %get-tuple-element.86.refs_0_, bf16[1536,1280]{1,0:T(8,128)(2,1)} %refs_1_.5, bf16[1,1280]{1,0:T(2,128)(2,1)} %reshape.139.refs_1_.refs_2_, ...), custom_call_target="tpu_custom_call" | custom-call | flops 78643200 | bytes 35389440 | tf_op jit(solution)/shard_map/middle/pallas_call | solution.py:131
  324.8 0.8 slice.32
  325.6 0.5 broadcast.63
  326.2 0.7 reduce.10
  326.9 0.7 select_maximum_fusion.refs_11_
  327.6 74.5 %attend_back.1 = (bf16[2,1536,1920]{2,1,0:T(8,128)(2,1)}, bf16[640,1280]{1,0:T(8,128)(2,1)}, bf16[640,1280]{1,0:T(8,128)(2,1)}, bf16[320,1280]{1,0:T(8,128)(2,1)...) custom-call(bf16[1536,1280]{1,0:T(8,128)(2,1)} %get-tuple-element.10, ...), custom_call_target="tpu_custom_call" | custom-call | flops 30198988800 | bytes 34734080 | tf_op jit(solution)/shard_map/attend_back/pallas_call | solution.py:131
  402.1 46.8 %weight_grads.1 = (bf16[1280,1280]{1,0:T(8,128)(2,1)}, bf16[1280,1280]{1,0:T(8,128)(2,1)}, bf16[1280,1280]{1,0:T(8,128)(2,1)}, bf16[1280,1280]{1,0:T(8,128)(2,1)...) custom-call(bf16[1536,1280]{1,0:T(8,128)(2,1)} %get-tuple-element.12, ...), custom_call_target="tpu_custom_call" | custom-call | flops 20132659200 | bytes 44564480 | tf_op jit(solution)/shard_map/weight_grads/pallas_call | solution.py:131
  448.9 214.1 %last.1 = (f32[1536,1280]{1,0:T(8,128)}, f32[1,1280]{1,0:T(1,128)}, f32[16,1280]{1,0:T(8,128)}, bf16[160,1280]{1,0:T(8,128)(2,1)}, bf16[160,1280]{1,0:T(8,128)(2...) custom-call(bf16[1536,1280]{1,0:T(8,128)(2,1)} %refs_0_.5, ...), custom_call_target="tpu_custom_call" | custom-call | flops 15099494400 | bytes 25559040 | tf_op jit(solution)/shard_map/last/pallas_call | solution.py:131
  663.0 1.0 slice_reduce_fusion
  664.0 1.5 slice_reduce_fusion.1
  665.6 0.7 dynamic_slice.7
  666.2 0.6 fusion.2
  669.6 11.8 %finish.1 = (f32[320,1280]{1,0:T(8,128)}, f32[320,1280]{1,0:T(8,128)}, f32[320,1280]{1,0:T(8,128)}, f32[320,1280]{1,0:T(8,128)}, f32[1280,1280]{1,0:T(8,128)}, /*index=5*/f32[1280,1280]{1,0:T(8,128)}) custom-call(bf16[1280,1280]{1,0:T(8,128)(2,1)} %get-tuple-element.141.refs_0_, bf16[1280,1280]{1,0:T(8,128)(2,1)} %get-tuple-element.142.refs_1_, ...), custom_call_target="tpu_custom_call" | custom-call | flops 1638400 | bytes 29491200 | tf_op jit(solution)/shard_map/finish/pallas_call | solution.py:131
  681.4 0.6 pad_maximum_fusion.2
  681.9 2.0 copy.52
  683.9 2.6 copy-done.2
  686.6 3.2 copy.53
  (35 shorter events, 0.1 us)
Async XLA Ops:
  0.6 3.9 copy-start
  0.7 13.4 %copy-start.5 = (bf16[1280,320]{0,1:T(8,128)(2,1)S(1)}, bf16[1280,320]{0,1:T(8,128)(2,1)}, u32[]{:S(2)}) copy-start(bf16[1280,320]{0,1:T(8,128)(2,1)} %param.17) | copy-start | bytes 2457604
  1.4 14.8 %copy-start.7 = (bf16[1,1280]{1,0:T(2,128)(2,1)}, bf16[1,1280]{1,0:T(2,128)(2,1)S(1)}, u32[]{:S(2)}) copy-start(bf16[1,1280]{1,0:T(2,128)(2,1)S(1)} %reshape.143.refs_2_) | copy-start | bytes 7684
  1.4 122.2 %collective-permute-start = (bf16[1,1280]{1,0:T(2,128)(2,1)S(1)}, bf16[1,1280]{1,0:T(2,128)(2,1)S(1)}, u32[]{:S(2)}, u32[]{:S(2)}) collective-permute-start(bf16[1,1280]{1,0:T(2,128)(2,1)S(1)} %reshape.143.refs_2_), channel_id=1, source_target_pairs={{0,1},{1,0},{2,3},{3,2},{4,5},{5,4},{6,7},{7,6},{8,9},{9,8},{10,11... | collective-permute-start | bytes 7688 | tf_op jit(solution)/shard_map/ppermute | solution.py:807
  1.9 207.1 %collective-permute-start.1 = (bf16[1,1280]{1,0:T(2,128)(2,1)S(1)}, bf16[1,1280]{1,0:T(2,128)(2,1)S(1)}, u32[]{:S(2)}, u32[]{:S(2)}) collective-permute-start(bf16[1,1280]{1,0:T(2,128)(2,1)S(1)} %reshape.143.refs_2_), channel_id=1, source_target_pairs={{0,2},{1,3},{2,0},{3,1},{4,6},{5,7},{6,4},{7,5},{8,10},{9,11},{10,... | collective-permute-start | bytes 7688 | tf_op jit(solution)/shard_map/ppermute | solution.py:807
  18.8 87.6 %copy-start.4 = (bf16[320,1280]{1,0:T(8,128)(2,1)S(1)}, bf16[320,1280]{1,0:T(8,128)(2,1)}, u32[]{:S(2)}) copy-start(bf16[320,1280]{1,0:T(8,128)(2,1)} %refs_5_.1) | copy-start | bytes 2457604
  109.5 13.6 %copy-start.10 = (bf16[1280]{0:T(1024)(128)(2,1)S(1)}, bf16[1280]{0:T(1024)(128)(2,1)}, u32[]{:S(2)}) copy-start(bf16[1280]{0:T(1024)(128)(2,1)} %param.23) | copy-start | bytes 7684
  123.7 0.6 copy-start.12
  209.0 1.2 copy-start.11
  209.0 1.2 collective-permute-start.2
  210.2 0.6 copy-start.13
  307.2 18.4 %copy-start.9 = (f32[1,1280]{1,0:T(1,128)S(1)}, f32[1,1280]{1,0:T(1,128)}, u32[]{:S(2)}) copy-start(f32[1,1280]{1,0:T(1,128)} %get-tuple-element.134) | copy-start | bytes 15364
  307.2 18.4 %copy-start.8 = (f32[1,1280]{1,0:T(1,128)S(1)}, f32[1,1280]{1,0:T(1,128)}, u32[]{:S(2)}) copy-start(f32[1,1280]{1,0:T(1,128)} %get-tuple-element.135) | copy-start | bytes 15364
  307.2 19.7 %copy-start.6 = (f32[1,1280]{1,0:T(1,128)S(1)}, f32[1,1280]{1,0:T(1,128)}, u32[]{:S(2)}) copy-start(f32[1,1280]{1,0:T(1,128)} %get-tuple-element.137) | copy-start | bytes 15364
  669.6 12.4 %copy-start.3 = (bf16[1536,1280]{1,0:T(8,128)(2,1)S(1)}, bf16[1536,1280]{1,0:T(8,128)(2,1)}, u32[]{:S(2)}) copy-start(bf16[1536,1280]{1,0:T(8,128)(2,1)} %get-tuple-element.173) | copy-start | bytes 11796484
  681.9 4.7 copy-start.2
  686.6 3.2 copy-start.1

commit v6 on v4

--- a/solution.py
+++ b/solution.py
@@ -840,7 +840,7 @@
     t.on(steps, "start", J.wait("p"))
     t.on(2 * steps - 1, "end", W.wait("s"), W.wait("p"), *[g.wait(s) for s in "ys" for g in (U, V)])
     (qkv, mixed, w, n1), got = attend(x, gains[0], *ids, h, [("j", "js"), ("jo", "jp")], t)
-    wo_all = jnp.stack([jnp.concatenate([wo, got["ws"]]), jnp.concatenate([got["wo"], got["wp"]])])
+    wo_all = jnp.concatenate([wo, got["ws"], got["wo"], got["wp"]]).reshape(2, 2 * h, D)
     hidden, n2, att_square = project(x, gains[1], valid, mixed, wo_all)
 
     bias_o = swap(bias, "mp", 2)
@@ -852,7 +852,7 @@
     )
     fs = hidden_units // pick(hidden_units, 256)
     t.on(0, "start", *[g.start("a") for g in (U, V)])
-    t.on(3, "start", *[g.wait("a") for g in (U, V)], *[g.start("b") for g in (U, V)])
+    t.on(2, "middle", *[g.wait("a") for g in (U, V)], *[g.start("b") for g in (U, V)])
     t.on(4, "start", *[g.wait("b") for g in (U, V)], *[g.start("p") for g in (U, V)])
     t.on(fs - 1, "end", *[g.wait("p") for g in (U, V)])
     own, far_weights = feed_forward(

time: 696 us -> 690 us (level)
  no operation moved by 1% of the time
where the time goes in v6:
time: 690 us; the launch traced here: 681 us
  Pallas kernels  637 us (92%)
  local copies, waits for them, and re-layouts  26.4 us (4%)
  other arithmetic  10.6 us (2%)
    pallas_call x9, Pallas kernels, launch(): pl.pallas_call(kernel, grid=grid, in_specs=[*in_specs, *[anywhere] * len(...  637 us
  transfers between devices with their start and end apart: 3, of which 1 were waited for; matrix products, arithmetic and copies ran while one was open for 3% of the time, Pallas kernels for 27%

profile of v6, /device:TPU:0, one launch (start us, length us, event | category | flops | bytes accessed | tf_op | source)
XLA Modules:
  0.0 681.5 jit_solution(13061661682850119501)
XLA Ops:
  0.6 0.0 copy-start
  0.7 0.8 reshape.143.refs_2_
  1.4 0.5 collective-permute-start
  1.9 2.6 collective-permute-start.1
  4.5 0.1 constant_dynamic-slice_fusion
  4.6 0.1 copy.38
  4.7 0.5 select_reduce_fusion
  5.1 0.2 convert_reduce_fusion
  5.4 0.1 broadcast_add_fusion
  5.4 1.6 add.49.refs_2_.refs_3_
  7.0 0.7 add.44.refs_3_.refs_4_
  7.7 0.6 fusion.1
  8.3 1.3 reshape.139.refs_1_.refs_2_
  9.6 1.6 reshape.147.refs_2_.refs_4_
  11.2 1.3 reshape.140.refs_1_
  12.5 1.5 copy.41
  14.1 0.6 copy.40
  14.7 1.6 copy.39
  16.3 2.5 pad_maximum_fusion.1.refs_4_
  18.8 87.6 %attend.1 = (bf16[2,1536,1920]{2,1,0:T(8,128)(2,1)}, bf16[2,1536,640]{2,1,0:T(8,128)(2,1)}, bf16[2,1280,1920]{2,1,0:T(8,128)(2,1)}, bf16[1536,1280]{1,0:T(8,128)...) custom-call(bf16[1536,1280]{1,0:T(8,128)(2,1)} %refs_0_.5, ...), custom_call_target="tpu_custom_call" | custom-call | flops 22649241600 | bytes 40632320 | tf_op jit(solution)/shard_map/attend/pallas_call | solution.py:131
  106.4 3.1 pad_maximum_fusion
  109.5 12.9 %project.1 = (f32[1536,1280]{1,0:T(8,128)}, bf16[1536,1280]{1,0:T(8,128)(2,1)}, f32[1,1280]{1,0:T(1,128)}) custom-call(bf16[1536,1280]{1,0:T(8,128)(2,1)} %refs_0_.5, bf16[1,1280]{1,0:T(2,128)(2,1)} %reshape.139.refs_1_.refs_2_, f32[1536,1]{1,0:T(8,128)} %reshape.147.refs_2_.refs_4_, bf16[2,1536,640]{2,1,0:T(8,128)(2,1)} %get-tuple-element.80.refs_3_, ...), custom_call_target="tpu_custom_call" | custom-call | flops 5033164800 | bytes 23592960 | tf_op jit(solution)/shard_map/project/pallas_call | solution.py:131
  122.4 0.6 compare_select_fusion
  123.1 0.6 reshape.142.refs_3_
  123.7 0.6 copy-done.12
  124.2 83.9 %feed_forward.2 = (bf16[1536,1280]{1,0:T(8,128)(2,1)}, bf16[1536,1280]{1,0:T(8,128)(2,1)}, bf16[1280,1280]{1,0:T(8,128)(2,1)}, bf16[1280,1280]{1,0:T(8,128)(2,1)...) custom-call(bf16[1536,1280]{1,0:T(8,128)(2,1)} %get-tuple-element.85, ...), custom_call_target="tpu_custom_call" | custom-call | flops 60397977600 | bytes 57671680 | tf_op jit(solution)/shard_map/feed_forward/pallas_call | solution.py:131
  208.2 0.7 constant_dynamic-update-slice_fusion.3
  208.9 0.7 constant_dynamic-update-slice_fusion.2
  209.6 0.5 collective-permute-done.2.refs_3_
  210.1 0.6 copy-done.13
  210.7 96.4 %feed_forward.3 = (bf16[1536,1280]{1,0:T(8,128)(2,1)}, bf16[1536,1280]{1,0:T(8,128)(2,1)}, bf16[1280,1280]{1,0:T(8,128)(2,1)}, bf16[1280,1280]{1,0:T(8,128)(2,1)...) custom-call(bf16[1536,1280]{1,0:T(8,128)(2,1)} %get-tuple-element.85, ...), custom_call_target="tpu_custom_call" | custom-call | flops 60397977600 | bytes 57671680 | tf_op jit(solution)/shard_map/feed_forward/pallas_call | solution.py:131
  307.1 17.6 %middle.1 = (bf16[1536,1280]{1,0:T(8,128)(2,1)}, bf16[1536,1280]{1,0:T(8,128)(2,1)}, f32[8,1280]{1,0:T(8,128)}, bf16[1280,1280]{1,0:T(8,128)(2,1)}, bf16[1280,1280]{1,0:T(8,128)(2,1)}) custom-call(f32[1536,1280]{1,0:T(8,128)} %get-tuple-element.84.refs_0_, bf16[1536,1280]{1,0:T(8,128)(2,1)} %refs_1_.5, bf16[1,1280]{1,0:T(2,128)(2,1)} %reshape.139.refs_1_.refs_2_, ...), custom_call_target="tpu_custom_call" | custom-call | flops 78643200 | bytes 35389440 | tf_op jit(solution)/shard_map/middle/pallas_call | solution.py:131
  324.7 0.8 slice.32
  325.5 0.5 broadcast.63
  326.0 0.7 reduce.10
  326.7 0.7 select_maximum_fusion.refs_11_
  327.4 73.5 %attend_back.1 = (bf16[2,1536,1920]{2,1,0:T(8,128)(2,1)}, bf16[640,1280]{1,0:T(8,128)(2,1)}, bf16[640,1280]{1,0:T(8,128)(2,1)}, bf16[320,1280]{1,0:T(8,128)(2,1)...) custom-call(bf16[1536,1280]{1,0:T(8,128)(2,1)} %get-tuple-element.10, ...), custom_call_target="tpu_custom_call" | custom-call | flops 30198988800 | bytes 34734080 | tf_op jit(solution)/shard_map/attend_back/pallas_call | solution.py:131
  400.9 46.3 %weight_grads.1 = (bf16[1280,1280]{1,0:T(8,128)(2,1)}, bf16[1280,1280]{1,0:T(8,128)(2,1)}, bf16[1280,1280]{1,0:T(8,128)(2,1)}, bf16[1280,1280]{1,0:T(8,128)(2,1)...) custom-call(bf16[1536,1280]{1,0:T(8,128)(2,1)} %get-tuple-element.11, ...), custom_call_target="tpu_custom_call" | custom-call | flops 20132659200 | bytes 44564480 | tf_op jit(solution)/shard_map/weight_grads/pallas_call | solution.py:131
  447.3 206.9 %last.1 = (f32[1536,1280]{1,0:T(8,128)}, f32[1,1280]{1,0:T(1,128)}, f32[16,1280]{1,0:T(8,128)}, bf16[160,1280]{1,0:T(8,128)(2,1)}, bf16[160,1280]{1,0:T(8,128)(2...) custom-call(bf16[1536,1280]{1,0:T(8,128)(2,1)} %refs_0_.5, ...), custom_call_target="tpu_custom_call" | custom-call | flops 15099494400 | bytes 25559040 | tf_op jit(solution)/shard_map/last/pallas_call | solution.py:131
  654.1 1.0 slice_reduce_fusion
  655.1 1.5 slice_reduce_fusion.1
  656.7 0.7 dynamic_slice.7
  657.4 0.6 fusion.2
  660.7 11.8 %finish.1 = (f32[320,1280]{1,0:T(8,128)}, f32[320,1280]{1,0:T(8,128)}, f32[320,1280]{1,0:T(8,128)}, f32[320,1280]{1,0:T(8,128)}, f32[1280,1280]{1,0:T(8,128)}, /*index=5*/f32[1280,1280]{1,0:T(8,128)}) custom-call(bf16[1280,1280]{1,0:T(8,128)(2,1)} %get-tuple-element.137.refs_0_, bf16[1280,1280]{1,0:T(8,128)(2,1)} %get-tuple-element.138.refs_1_, ...), custom_call_target="tpu_custom_call" | custom-call | flops 1638400 | bytes 29491200 | tf_op jit(solution)/shard_map/finish/pallas_call | solution.py:131
  672.5 0.6 pad_maximum_fusion.2
  673.1 2.0 copy.52
  675.1 2.6 copy-done.2
  677.7 3.2 copy.53
  (35 shorter events, 0.1 us)
Async XLA Ops:
  0.6 3.9 copy-start
  0.7 13.4 %copy-start.5 = (bf16[1280,320]{0,1:T(8,128)(2,1)S(1)}, bf16[1280,320]{0,1:T(8,128)(2,1)}, u32[]{:S(2)}) copy-start(bf16[1280,320]{0,1:T(8,128)(2,1)} %param.17) | copy-start | bytes 2457604
  1.4 14.8 %copy-start.7 = (bf16[1,1280]{1,0:T(2,128)(2,1)}, bf16[1,1280]{1,0:T(2,128)(2,1)S(1)}, u32[]{:S(2)}) copy-start(bf16[1,1280]{1,0:T(2,128)(2,1)S(1)} %reshape.143.refs_2_) | copy-start | bytes 7684
  1.4 122.2 %collective-permute-start = (bf16[1,1280]{1,0:T(2,128)(2,1)S(1)}, bf16[1,1280]{1,0:T(2,128)(2,1)S(1)}, u32[]{:S(2)}, u32[]{:S(2)}) collective-permute-start(bf16[1,1280]{1,0:T(2,128)(2,1)S(1)} %reshape.143.refs_2_), channel_id=1, source_target_pairs={{0,1},{1,0},{2,3},{3,2},{4,5},{5,4},{6,7},{7,6},{8,9},{9,8},{10,11... | collective-permute-start | bytes 7688 | tf_op jit(solution)/shard_map/ppermute | solution.py:801
  1.9 207.0 %collective-permute-start.1 = (bf16[1,1280]{1,0:T(2,128)(2,1)S(1)}, bf16[1,1280]{1,0:T(2,128)(2,1)S(1)}, u32[]{:S(2)}, u32[]{:S(2)}) collective-permute-start(bf16[1,1280]{1,0:T(2,128)(2,1)S(1)} %reshape.143.refs_2_), channel_id=1, source_target_pairs={{0,2},{1,3},{2,0},{3,1},{4,6},{5,7},{6,4},{7,5},{8,10},{9,11},{10,... | collective-permute-start | bytes 7688 | tf_op jit(solution)/shard_map/ppermute | solution.py:801
  18.8 87.6 %copy-start.4 = (bf16[320,1280]{1,0:T(8,128)(2,1)S(1)}, bf16[320,1280]{1,0:T(8,128)(2,1)}, u32[]{:S(2)}) copy-start(bf16[320,1280]{1,0:T(8,128)(2,1)} %refs_5_.1) | copy-start | bytes 2457604
  109.5 13.6 %copy-start.10 = (bf16[1280]{0:T(1024)(128)(2,1)S(1)}, bf16[1280]{0:T(1024)(128)(2,1)}, u32[]{:S(2)}) copy-start(bf16[1280]{0:T(1024)(128)(2,1)} %param.23) | copy-start | bytes 7684
  123.7 0.6 copy-start.12
  208.9 1.2 copy-start.11
  208.9 1.2 collective-permute-start.2
  210.1 0.6 copy-start.13
  307.0 18.4 %copy-start.9 = (f32[1,1280]{1,0:T(1,128)S(1)}, f32[1,1280]{1,0:T(1,128)}, u32[]{:S(2)}) copy-start(f32[1,1280]{1,0:T(1,128)} %get-tuple-element.126) | copy-start | bytes 15364
  307.1 18.4 %copy-start.8 = (f32[1,1280]{1,0:T(1,128)S(1)}, f32[1,1280]{1,0:T(1,128)}, u32[]{:S(2)}) copy-start(f32[1,1280]{1,0:T(1,128)} %get-tuple-element.127) | copy-start | bytes 15364
  307.1 19.7 %copy-start.6 = (f32[1,1280]{1,0:T(1,128)S(1)}, f32[1,1280]{1,0:T(1,128)}, u32[]{:S(2)}) copy-start(f32[1,1280]{1,0:T(1,128)} %get-tuple-element.129) | copy-start | bytes 15364
  660.7 12.4 %copy-start.3 = (bf16[1536,1280]{1,0:T(8,128)(2,1)S(1)}, bf16[1536,1280]{1,0:T(8,128)(2,1)}, u32[]{:S(2)}) copy-start(bf16[1536,1280]{1,0:T(8,128)(2,1)} %get-tuple-element.169) | copy-start | bytes 11796484
  673.1 4.7 copy-start.2
  677.7 3.2 copy-start.1
